TPU v7x, 32 devices: a whole 2x2x4 slice. The times are simulated.
32 devices in a mesh: grp: 2 (over x), seq: 16 (over z, y, core).
Axes of the slice: x: 2, y: 2, z: 4, core: 2. Of those that a mesh axis runs over, the one named last changes fastest.
Arguments:
- query_in: bfloat16 [4096, 4096], P(('grp', 'seq')), parts along dimension 0, may hold values from -6 to 6
- key_in: bfloat16 [4096, 4096], P(('grp', 'seq')), parts along dimension 0, may hold values from -6 to 6
- value_in: bfloat16 [4096, 4096], P(('grp', 'seq')), parts along dimension 0, may hold values from -6 to 6
- short_filter: float32 [3, 3, 4096], replicated, may hold values from -4 to 4
- residue: float32 [4096, 16], replicated, may hold values from -0.125 to 0.125
- rate: float32 [4096, 16], replicated, may hold values from 0.000390625 to 0.03
- skip: float32 [4096], replicated, may hold values from -5 to 5
Outputs:
- gated: bfloat16 [4096, 4096], P(('grp', 'seq')), parts along dimension 0
There are 2 independent parts, one for each index of `grp`. A program takes and returns all parts, laid end to end along the dimension named above; an argument that names none is the same for every part. Nothing has to cross between parts.
All inputs are finite; a program needn't handle non-finite values.
Results may differ from a plain program's by a relative error of at most 0.0049.
Values may be sent and summed in bfloat16 or wider, within the bound.
No kernel may reach another device: no remote copies, remote signals or barrier semaphores. Data moves between devices by JAX's collectives and lax.ppermute only.
A program may use at most 192 MiB of HBM per device.

v0:
```python
import math

import jax
import jax.numpy as jnp
from jax import lax
from jax.sharding import PartitionSpec as P


def passed_along(array, axis, by):
    length = lax.axis_size(axis)
    pairs = [(i, i + by) for i in range(length) if 0 <= i + by < length]
    return lax.ppermute(array, axis, pairs)


def matmul_prec(form, left, right):
    return jnp.einsum(form, left, right, precision=lax.Precision.HIGHEST)


def split_length(total):
    small = 1
    for factor in range(1, math.isqrt(total) + 1):
        if total % factor == 0:
            small = factor
    return (total // small, small)


def angle_table(left, right, modulus):
    product = left[:, None] * right[None, :] % modulus
    return 2.0 * math.pi / modulus * product.astype(jnp.float32)


def make_tables(total):
    first, second = split_length(total)
    index_one = jnp.arange(first, dtype=jnp.int32)
    index_two = jnp.arange(second, dtype=jnp.int32)
    angle_one = angle_table(index_one, index_one, first)
    angle_two = angle_table(index_two, index_two, second)
    angle_turn = angle_table(index_one, index_two, total)
    return (
        jnp.cos(angle_one),
        jnp.sin(angle_one),
        jnp.cos(angle_two),
        jnp.sin(angle_two),
        jnp.cos(angle_turn)[:, :, None],
        jnp.sin(angle_turn)[:, :, None],
    )


def first_section(table, grid):
    if grid.dtype == jnp.bfloat16:
        upper = table.astype(jnp.bfloat16)
        lower = (table - upper.astype(jnp.float32)).astype(jnp.bfloat16)
        high_part = jnp.einsum("kn,nmc->kmc", upper, grid, preferred_element_type=jnp.float32)
        low_part = jnp.einsum("kn,nmc->kmc", lower, grid, preferred_element_type=jnp.float32)
        return high_part + low_part
    return matmul_prec("kn,nmc->kmc", table, grid)


def forward_real(signal, tables):
    cos_one, sin_one, cos_two, sin_two, cos_turn, sin_turn = tables
    grid = signal.reshape(cos_one.shape[0], cos_two.shape[0], signal.shape[1])
    first_re = first_section(cos_one, grid)
    first_im = -first_section(sin_one, grid)
    turned_re = first_re * cos_turn + first_im * sin_turn
    turned_im = first_im * cos_turn - first_re * sin_turn
    out_re = matmul_prec("jm,kmc->kjc", cos_two, turned_re) + matmul_prec(
        "jm,kmc->kjc", sin_two, turned_im
    )
    out_im = matmul_prec("jm,kmc->kjc", cos_two, turned_im) - matmul_prec(
        "jm,kmc->kjc", sin_two, turned_re
    )
    return (out_re, out_im)


def inverse_real(spec_re, spec_im, tables):
    cos_one, sin_one, cos_two, sin_two, cos_turn, sin_turn = tables
    total = cos_one.shape[0] * cos_two.shape[0]
    back_re = matmul_prec("jm,kjc->kmc", cos_two, spec_re) - matmul_prec(
        "jm,kjc->kmc", sin_two, spec_im
    )
    back_im = matmul_prec("jm,kjc->kmc", cos_two, spec_im) + matmul_prec(
        "jm,kjc->kmc", sin_two, spec_re
    )
    twist_re = back_re * cos_turn - back_im * sin_turn
    twist_im = back_re * sin_turn + back_im * cos_turn
    signal = matmul_prec("kn,kmc->nmc", cos_one, twist_re) - matmul_prec(
        "kn,kmc->nmc", sin_one, twist_im
    )
    return signal.reshape(total, signal.shape[2]) / total


def featurize(signal, rim, taps):
    whole = jnp.concatenate([rim, signal], axis=0).astype(jnp.float32)
    rows = signal.shape[0]
    edge = taps.shape[0] - 1
    result = taps[0] * whole[edge : edge + rows]
    for offset in range(1, taps.shape[0]):
        result = result + taps[offset] * whole[edge - offset : edge - offset + rows]
    return result


def shards(query_in, key_in, value_in, short_filter, residue, rate, skip):
    rows, width = query_in.shape
    edge = short_filter.shape[1] - 1
    rims = passed_along(
        (query_in[rows - edge :], key_in[rows - edge :], value_in[rows - edge :]), "seq", 1
    )
    query_feat = featurize(query_in, rims[0], short_filter[0])
    key_feat = featurize(key_in, rims[1], short_filter[1])
    value_feat = featurize(value_in, rims[2], short_filter[2])
    mixed = (key_feat * value_feat).astype(jnp.bfloat16)
    prev_one = passed_along(mixed, "seq", 1)
    prev_two = passed_along(prev_one, "seq", 1)
    span = 2 * rows
    total = 4 * rows
    tables = make_tables(total)
    steps = jnp.arange(span).astype(jnp.float32)
    block = min(1024, width)
    pieces = []
    for start in range(0, width, block):
        own = mixed[:, start : start + block]
        before_one = prev_one[:, start : start + block]
        before_two = prev_two[:, start : start + block]
        blank = jnp.zeros((rows, block), jnp.bfloat16)
        blank_wide = jnp.zeros((rows, block), jnp.float32)
        weights = residue[start : start + block]
        decays = rate[start : start + block]
        filt = jnp.sum(weights[None] * jnp.exp(-decays[None] * steps[:, None, None]), axis=2)
        filt_re, filt_im = forward_real(
            jnp.concatenate([filt, blank_wide, blank_wide], axis=0), tables
        )
        sig_re, sig_im = forward_real(
            jnp.concatenate([before_two, before_one, own, blank], axis=0), tables
        )
        prod_re = filt_re * sig_re - filt_im * sig_im
        prod_im = filt_re * sig_im + filt_im * sig_re
        conv = inverse_real(prod_re, prod_im, tables)[span : span + rows]
        conv = conv + skip[start : start + block] * own.astype(jnp.float32)
        pieces.append((query_feat[:, start : start + block] * conv).astype(jnp.bfloat16))
    return jnp.concatenate(pieces, axis=1)


def solution(mesh):
    return jax.shard_map(
        shards,
        mesh=mesh,
        in_specs=(
            P(("grp", "seq"), None),
            P(("grp", "seq"), None),
            P(("grp", "seq"), None),
            P(),
            P(),
            P(),
            P(),
        ),
        out_specs=P(("grp", "seq"), None),
        check_vma=False,
    )
```

profile of v0, /device:TPU:24, one launch (start us, length us, event | category | flops | bytes accessed | tf_op | source)
XLA Modules:
  0.0 349.3 jit_solution(1322488973380221542)
XLA Ops:
  3.7 3.5 %collective-permute-start.2 = (bf16[2,4096]{1,0:T(2,128)(2,1)S(1)}, bf16[2,4096]{1,0:T(2,128)(2,1)S(1)}, u32[]{:S(2)}, u32[]{:S(2)}) collective-permute-start(bf16[2,4096]{1,0:T(2,128)(2,1)S(1)} %slice.210), channel_id=1, source_target_pairs={{0,1},{1,2},{2,3},{3,4},{4,5},{5,6},{6,7},{7,8},{8,9},{9,10},{10,1... | collective-permute-start | bytes 49160 | tf_op jit(solution)/shard_map/ppermute | solution.py:12
  11.1 19.4 %multiply_reduce_fusion.3 = (f32[256,1024]{1,0:T(8,128)S(1)}, f32[256,1024]{1,0:T(8,128)S(1)}, f32[256,1024]{1,0:T(8,128)S(1)}, f32[256,1024]{1,0:T(8,128)S(1)}) fusion(f32[256]{0:T(256)S(1)} %iota_convert_fusion, f32[1024,16]{0,1:T(8,128)S(1)} %get-tuple-element.63, f32[1024,16]{0,1:T(8,128)S(1)} %get-tuple-element.103, ...), kind=kLoop, calls=%fused_computation.3 | loop fusion | flops 49283072 | bytes 4719616 | tf_op jit(solution)/shard_map/reduce_sum | solution.py:128
  30.8 4.4 %fusion.112 = f32[32,16,1024]{2,0,1:T(8,128)} fusion(f32[32,16,1024]{2,1,0:T(8,128)S(1)} %bitcast.351), kind=kOutput, calls=%fused_computation.161 | convolution fusion | flops 201340928 | bytes 4194304 | tf_op jit(solution)/shard_map/kn,nmc->kmc/dot_general | solution.py:16
  35.2 4.4 %fusion.114 = f32[32,16,1024]{2,0,1:T(8,128)} fusion(f32[32,16,1024]{2,1,0:T(8,128)S(1)} %bitcast.352), kind=kOutput, calls=%fused_computation.163 | convolution fusion | flops 201340928 | bytes 4194304 | tf_op jit(solution)/shard_map/kn,nmc->kmc/dot_general | solution.py:16
  39.9 4.4 %fusion.132 = f32[32,16,1024]{2,0,1:T(8,128)} fusion(f32[32,16,1024]{2,1,0:T(8,128)S(1)} %bitcast.353), kind=kOutput, calls=%fused_computation.181 | convolution fusion | flops 201340928 | bytes 4194304 | tf_op jit(solution)/shard_map/kn,nmc->kmc/dot_general | solution.py:16
  44.3 4.9 %fusion.134 = f32[32,16,1024]{2,0,1:T(8,128)} fusion(f32[32,16,1024]{2,1,0:T(8,128)S(1)} %bitcast.354), kind=kOutput, calls=%fused_computation.183 | convolution fusion | flops 201340928 | bytes 4194304 | tf_op jit(solution)/shard_map/kn,nmc->kmc/dot_general | solution.py:16
  49.5 4.5 %fusion.72 = f32[32,16,1024]{2,0,1:T(8,128)} fusion(f32[32,16,1024]{2,1,0:T(8,128)S(1)} %bitcast.355), kind=kOutput, calls=%fused_computation.121 | convolution fusion | flops 201340928 | bytes 4194304 | tf_op jit(solution)/shard_map/kn,nmc->kmc/dot_general | solution.py:16
  54.0 4.4 %fusion.74 = f32[32,16,1024]{2,0,1:T(8,128)} fusion(f32[32,16,1024]{2,1,0:T(8,128)S(1)} %bitcast.356), kind=kOutput, calls=%fused_computation.123 | convolution fusion | flops 201340928 | bytes 4194304 | tf_op jit(solution)/shard_map/kn,nmc->kmc/dot_general | solution.py:16
  58.8 4.4 %fusion.92 = f32[32,16,1024]{2,0,1:T(8,128)} fusion(f32[32,16,1024]{2,1,0:T(8,128)S(1)} %bitcast.349), kind=kOutput, calls=%fused_computation.141 | convolution fusion | flops 201340928 | bytes 4194304 | tf_op jit(solution)/shard_map/kn,nmc->kmc/dot_general | solution.py:16
  69.0 4.4 %fusion.94 = f32[32,16,1024]{2,0,1:T(8,128)} fusion(f32[32,16,1024]{2,1,0:T(8,128)S(1)} %bitcast.350), kind=kOutput, calls=%fused_computation.143 | convolution fusion | flops 201340928 | bytes 4194304 | tf_op jit(solution)/shard_map/kn,nmc->kmc/dot_general | solution.py:16
  75.0 9.1 %collective-permute-done.3 = bf16[128,4096]{1,0:T(8,128)(2,1)S(1)} collective-permute-done((bf16[128,4096]{1,0:T(8,128)(2,1)S(1)}, bf16[128,4096]{1,0:T(8,128)(2,1)S(1)}, u32[]{:S(2)}, u32[]{:S(2)}) %collective-permute-start.3) | collective-permute-done | bytes 1048608 | tf_op jit(solution)/shard_map/ppermute | solution.py:12
  88.1 13.1 %collective-permute-done.4 = bf16[128,4096]{1,0:T(8,128)(2,1)S(1)} collective-permute-done((bf16[128,4096]{1,0:T(8,128)(2,1)S(1)}, bf16[128,4096]{1,0:T(8,128)(2,1)S(1)}, u32[]{:S(2)}, u32[]{:S(2)}) %collective-permute-start.4) | collective-permute-done | bytes 1048608 | tf_op jit(solution)/shard_map/ppermute | solution.py:12
  139.2 17.5 %multiply_add_fusion.10 = (f32[32,16,1024]{2,0,1:T(8,128)S(1)}, f32[32,16,1024]{2,0,1:T(8,128)S(1)}, f32[32,16,1024]{2,0,1:T(8,128)}, f32[32,16,1024]{2,0,1:T(8,...) fusion(f32[32,16,1024]{2,0,1:T(8,128)} %convolution_add_fusion., ...), kind=kOutput, calls=%fused_computation.101 | convolution fusion | flops 61884416 | bytes 68161536 | tf_op jit(solution)/shard_map/kn,nmc->kmc/dot_general | solution.py:54
  156.8 4.8 %fusion.58 = f32[32,1024,16]{1,2,0:T(8,128)S(1)} fusion(f32[32,16,1024]{2,0,1:T(8,128)} %get-tuple-element.94), kind=kOutput, calls=%fused_computation.107 | convolution fusion | flops 100666880 | bytes 4194304 | tf_op jit(solution)/shard_map/jm,kmc->kjc/dot_general | solution.py:16
  171.7 3.5 %fusion.178 = f32[32,1024,16]{1,2,0:T(8,128)S(1)} fusion(f32[32,1024,16]{1,2,0:T(8,128)S(1)} %fusion.58, f32[32,16,1024]{2,0,1:T(8,128)S(1)} %get-tuple-element.95), kind=kOutput, calls=%fused_computation.199 | convolution fusion | flops 101191168 | bytes 6291456 | tf_op jit(solution)/shard_map/jm,kmc->kjc/dot_general | solution.py:16
  175.3 3.5 %fusion.181 = f32[32,1024,16]{1,2,0:T(8,128)S(1)} fusion(f32[32,1024,16]{1,2,0:T(8,128)S(1)} %fusion.56, f32[32,16,1024]{2,0,1:T(8,128)S(1)} %get-tuple-element.95), kind=kOutput, calls=%fused_computation.200 | convolution fusion | flops 101191168 | bytes 6291456 | tf_op jit(solution)/shard_map/jm,kmc->kjc/dot_general | solution.py:16
  178.8 3.5 %fusion.172 = f32[32,1024,16]{1,2,0:T(8,128)S(1)} fusion(f32[32,1024,16]{1,2,0:T(8,128)S(1)} %fusion.66, f32[32,16,1024]{2,0,1:T(8,128)S(1)} %get-tuple-element.93), kind=kOutput, calls=%fused_computation.197 | convolution fusion | flops 101191168 | bytes 6291456 | tf_op jit(solution)/shard_map/jm,kmc->kjc/dot_general | solution.py:16
  182.3 4.8 %multiply_subtract_fusion = (f32[32,1024,16]{1,2,0:T(8,128)S(1)}, f32[32,1024,16]{1,2,0:T(8,128)S(1)}) fusion(f32[32,1024,16]{1,2,0:T(8,128)S(1)} %fusion.181, f32[32,1024,16]{1,2,0:T(8,128)S(1)} %fusion.172, f32[32,1024,16]{1,2,0:T(8,128)S(1)} %fusion.178, f32[32,1024,16]{1,2,0:T(8,128)S(1)} %fusion.64, f32[32,16,1024]{2,0,1:T(8,128)S(1)} %get-tuple-element.93), kind=kOutput, calls=%fused_computation.72 | convolution fusion | flops 104336896 | bytes 14680064 | tf_op jit(solution)/shard_map/jm,kmc->kjc/dot_general | solution.py:16
  204.7 3.5 %fusion.166 = f32[32,1024,16]{1,2,0:T(8,128)S(1)} fusion(f32[32,1024,16]{1,2,0:T(8,128)S(1)} %fusion.78, f32[32,16,1024]{2,0,1:T(8,128)S(1)} %get-tuple-element.91), kind=kOutput, calls=%fused_computation.195 | convolution fusion | flops 101191168 | bytes 6291456 | tf_op jit(solution)/shard_map/jm,kmc->kjc/dot_general | solution.py:16
  208.2 3.8 %fusion.169 = f32[32,1024,16]{1,2,0:T(8,128)S(1)} fusion(f32[32,1024,16]{1,2,0:T(8,128)S(1)} %fusion.76, f32[32,16,1024]{2,0,1:T(8,128)S(1)} %get-tuple-element.91), kind=kOutput, calls=%fused_computation.196 | convolution fusion | flops 101191168 | bytes 6291456 | tf_op jit(solution)/shard_map/jm,kmc->kjc/dot_general | solution.py:16
  212.0 3.5 %fusion.160 = f32[32,1024,16]{1,2,0:T(8,128)S(1)} fusion(f32[32,1024,16]{1,2,0:T(8,128)S(1)} %fusion.86, f32[32,16,1024]{2,0,1:T(8,128)S(1)} %get-tuple-element.89), kind=kOutput, calls=%fused_computation.193 | convolution fusion | flops 101191168 | bytes 6291456 | tf_op jit(solution)/shard_map/jm,kmc->kjc/dot_general | solution.py:16
  215.5 4.7 %multiply_subtract_fusion.3 = (f32[32,1024,16]{1,2,0:T(8,128)S(1)}, f32[32,1024,16]{1,2,0:T(8,128)S(1)}) fusion(f32[32,1024,16]{1,2,0:T(8,128)S(1)} %fusion.169, f32[32,1024,16]{1,2,0:T(8,128)S(1)} %fusion.160, f32[32,1024,16]{1,2,0:T(8,128)S(1)} %fusion.166, f32[32,1024,16]{1,2,0:T(8,128)S(1)} %fusion.84, f32[32,16,1024]{2,0,1:T(8,128)S(1)} %get-tuple-element.89), kind=kOutput, calls=%fused_computation.81 | convolution fusion | flops 104336896 | bytes 14680064 | tf_op jit(solution)/shard_map/jm,kmc->kjc/dot_general | solution.py:16
  238.2 3.5 %fusion.154 = f32[32,1024,16]{1,2,0:T(8,128)S(1)} fusion(f32[32,1024,16]{1,2,0:T(8,128)S(1)} %fusion.98, f32[32,16,1024]{2,0,1:T(8,128)S(1)} %get-tuple-element.87), kind=kOutput, calls=%fused_computation.191 | convolution fusion | flops 101191168 | bytes 6291456 | tf_op jit(solution)/shard_map/jm,kmc->kjc/dot_general | solution.py:16
  241.8 3.5 %fusion.157 = f32[32,1024,16]{1,2,0:T(8,128)S(1)} fusion(f32[32,1024,16]{1,2,0:T(8,128)S(1)} %fusion.96, f32[32,16,1024]{2,0,1:T(8,128)S(1)} %get-tuple-element.87), kind=kOutput, calls=%fused_computation.192 | convolution fusion | flops 101191168 | bytes 6291456 | tf_op jit(solution)/shard_map/jm,kmc->kjc/dot_general | solution.py:16
  245.3 3.5 %fusion.148 = f32[32,1024,16]{1,2,0:T(8,128)S(1)} fusion(f32[32,1024,16]{1,2,0:T(8,128)S(1)} %fusion.106, f32[32,16,1024]{2,0,1:T(8,128)S(1)} %get-tuple-element.85), kind=kOutput, calls=%fused_computation.189 | convolution fusion | flops 101191168 | bytes 6291456 | tf_op jit(solution)/shard_map/jm,kmc->kjc/dot_general | solution.py:16
  248.8 4.9 %multiply_subtract_fusion.6 = (f32[32,1024,16]{1,2,0:T(8,128)S(1)}, f32[32,1024,16]{1,2,0:T(8,128)S(1)}) fusion(f32[32,1024,16]{1,2,0:T(8,128)S(1)} %fusion.157, f32[32,1024,16]{1,2,0:T(8,128)S(1)} %fusion.148, f32[32,1024,16]{1,2,0:T(8,128)S(1)} %fusion.154, f32[32,1024,16]{1,2,0:T(8,128)S(1)} %fusion.104, f32[32,16,1024]{2,0,1:T(8,128)S(1)} %get-tuple-element.85), kind=kOutput, calls=%fused_computation.90 | convolution fusion | flops 104336896 | bytes 14680064 | tf_op jit(solution)/shard_map/jm,kmc->kjc/dot_general | solution.py:16
  261.3 3.7 %fusion.116 = f32[32,1024,16]{1,2,0:T(8,128)S(1)} fusion(f32[32,16,1024]{2,0,1:T(8,128)S(1)} %get-tuple-element.26), kind=kOutput, calls=%fused_computation.165 | convolution fusion | flops 100666880 | bytes 4194304 | tf_op jit(solution)/shard_map/jm,kmc->kjc/dot_general | solution.py:16
  275.0 3.7 %fusion.145 = f32[32,1024,16]{1,2,0:T(8,128)S(1)} fusion(f32[32,1024,16]{1,2,0:T(8,128)S(1)} %fusion.116, f32[32,16,1024]{2,0,1:T(8,128)S(1)} %get-tuple-element.25), kind=kOutput, calls=%fused_computation.188 | convolution fusion | flops 101191168 | bytes 6291456 | tf_op jit(solution)/shard_map/jm,kmc->kjc/dot_general | solution.py:16
  278.7 3.5 %fusion.136 = f32[32,1024,16]{1,2,0:T(8,128)S(1)} fusion(f32[32,1024,16]{1,2,0:T(8,128)S(1)} %fusion.126, f32[32,16,1024]{2,0,1:T(8,128)S(1)} %get-tuple-element.97), kind=kOutput, calls=%fused_computation.185 | convolution fusion | flops 101191168 | bytes 6291456 | tf_op jit(solution)/shard_map/jm,kmc->kjc/dot_general | solution.py:16
  282.2 4.5 %multiply_subtract_fusion.9 = (f32[32,1024,16]{1,2,0:T(8,128)S(1)}, f32[32,1024,16]{1,2,0:T(8,128)S(1)}) fusion(f32[32,1024,16]{1,2,0:T(8,128)S(1)} %fusion.145, f32[32,1024,16]{1,2,0:T(8,128)S(1)} %fusion.136, f32[32,1024,16]{1,2,0:T(8,128)S(1)} %fusion.142, f32[32,1024,16]{1,2,0:T(8,128)S(1)} %fusion.124, f32[32,16,1024]{2,0,1:T(8,128)S(1)} %get-tuple-element.97), kind=kOutput, calls=%fused_computation.99 | convolution fusion | flops 104336896 | bytes 14680064 | tf_op jit(solution)/shard_map/jm,kmc->kjc/dot_general | solution.py:16
  307.7 7.5 %subtract_bitcast_fusion.3 = (f32[32,16,1024]{2,1,0:T(8,128)}, f32[32,16,1024]{2,1,0:T(8,128)}, f32[32,16,1024]{2,1,0:T(8,128)}, f32[32,16,1024]{2,1,0:T(8,128)}...) fusion(f32[32,1024,16]{1,2,0:T(8,128)S(1)} %fusion.187, ...), kind=kOutput, calls=%fused_computation.97 | convolution fusion | flops 113774080 | bytes 35655680 | tf_op jit(solution)/shard_map/jm,kjc->kmc/dot_general | solution.py:16
  315.2 4.7 %fusion.48 = f32[32,16,1024]{2,0,1:T(8,128)S(1)} fusion(f32[32,16,1024]{2,1,0:T(8,128)} %get-tuple-element.74), kind=kOutput, calls=%fused_computation.61 | convolution fusion | flops 201340928 | bytes 4194304 | tf_op jit(solution)/shard_map/kn,kmc->nmc/dot_general | solution.py:16
  (144 shorter events, 171.0 us)
Async XLA Ops:
  0.9 63.2 %collective-permute-start.1 = (bf16[2,4096]{1,0:T(2,128)(2,1)S(1)}, bf16[2,4096]{1,0:T(2,128)(2,1)S(1)}, u32[]{:S(2)}, u32[]{:S(2)}) collective-permute-start(bf16[2,4096]{1,0:T(2,128)(2,1)S(1)} %slice.203), channel_id=1, source_target_pairs={{0,1},{1,2},{2,3},{3,4},{4,5},{5,6},{6,7},{7,8},{8,9},{9,10},{10,1... | collective-permute-start | bytes 49160 | tf_op jit(solution)/shard_map/ppermute | solution.py:12
  3.7 60.7 %collective-permute-start.2 = (bf16[2,4096]{1,0:T(2,128)(2,1)S(1)}, bf16[2,4096]{1,0:T(2,128)(2,1)S(1)}, u32[]{:S(2)}, u32[]{:S(2)}) collective-permute-start(bf16[2,4096]{1,0:T(2,128)(2,1)S(1)} %slice.210), channel_id=1, source_target_pairs={{0,1},{1,2},{2,3},{3,4},{4,5},{5,6},{6,7},{7,8},{8,9},{9,10},{10,1... | collective-permute-start | bytes 49160 | tf_op jit(solution)/shard_map/ppermute | solution.py:12
  8.1 65.5 %collective-permute-start = (bf16[2,4096]{1,0:T(2,128)(2,1)S(1)}, bf16[2,4096]{1,0:T(2,128)(2,1)S(1)}, u32[]{:S(2)}, u32[]{:S(2)}) collective-permute-start(bf16[2,4096]{1,0:T(2,128)(2,1)S(1)} %slice.193), channel_id=1, source_target_pairs={{0,1},{1,2},{2,3},{3,4},{4,5},{5,6},{6,7},{7,8},{8,9},{9,10},{10,1... | collective-permute-start | bytes 49160 | tf_op jit(solution)/shard_map/ppermute | solution.py:12
  54.0 4.5 %copy-start.19 = (f32[3,3,4096]{2,1,0:T(4,128)S(1)}, f32[3,3,4096]{2,1,0:T(4,128)}, u32[]{:S(2)}) copy-start(f32[3,3,4096]{2,1,0:T(4,128)} %param.10) | copy-start | bytes 442372
  58.8 4.4 %copy-start.24 = (f32[4096]{0:T(1024)S(1)}, f32[4096]{0:T(1024)}, u32[]{:S(2)}) copy-start(f32[4096]{0:T(1024)} %param.13) | copy-start | bytes 49156
  58.8 5.3 %copy-start.16 = (bf16[128,4096]{1,0:T(8,128)(2,1)S(1)}, bf16[128,4096]{1,0:T(8,128)(2,1)}, u32[]{:S(2)}) copy-start(bf16[128,4096]{1,0:T(8,128)(2,1)} %param.8) | copy-start | bytes 3145732
  64.0 1.2 copy-start.17
  67.1 6.4 %copy-start.6 = (bf16[128,4096]{1,0:T(8,128)(2,1)}, bf16[128,4096]{1,0:T(8,128)(2,1)S(1)}, u32[]{:S(2)}) copy-start(bf16[128,4096]{1,0:T(8,128)(2,1)S(1)} %fusion.2) | copy-start | bytes 3145732
  67.1 17.0 %collective-permute-start.3 = (bf16[128,4096]{1,0:T(8,128)(2,1)S(1)}, bf16[128,4096]{1,0:T(8,128)(2,1)S(1)}, u32[]{:S(2)}, u32[]{:S(2)}) collective-permute-start(bf16[128,4096]{1,0:T(8,128)(2,1)S(1)} %fusion.2), channel_id=1, source_target_pairs={{0,1},{1,2},{2,3},{3,4},{4,5},{5,6},{6,7},{7,8},{8,9},{9,10},{10,1... | collective-permute-start | bytes 3145736 | tf_op jit(solution)/shard_map/ppermute | solution.py:12
  73.4 1.2 copy-start.18
  84.1 17.0 %collective-permute-start.4 = (bf16[128,4096]{1,0:T(8,128)(2,1)S(1)}, bf16[128,4096]{1,0:T(8,128)(2,1)S(1)}, u32[]{:S(2)}, u32[]{:S(2)}) collective-permute-start(bf16[128,4096]{1,0:T(8,128)(2,1)S(1)} %collective-permute-done.3), channel_id=1, source_target_pairs={{0,1},{1,2},{2,3},{3,4},{4,5},{5,6},{6,7},{7,8},{8,9},{9,10},{10,1... | collective-permute-start | bytes 3145736 | tf_op jit(solution)/shard_map/ppermute | solution.py:12
  156.8 4.9 %copy-start.5 = (f32[32,16,1024]{2,0,1:T(8,128)S(1)}, f32[32,16,1024]{2,0,1:T(8,128)}, u32[]{:S(2)}) copy-start(f32[32,16,1024]{2,0,1:T(8,128)} %get-tuple-element.94) | copy-start | bytes 6291460
  161.7 3.3 copy-start.4
  189.2 2.2 copy-start.3
  194.6 3.5 copy-start.2
  222.3 2.6 copy-start.1
  228.2 3.3 copy-start
  315.2 4.7 %copy-start.14 = (f32[32,16,1024]{2,1,0:T(8,128)S(1)}, f32[32,16,1024]{2,1,0:T(8,128)}, u32[]{:S(2)}) copy-start(f32[32,16,1024]{2,1,0:T(8,128)} %get-tuple-element.75) | copy-start | bytes 6291460
  323.0 1.6 copy-start.13
  324.6 3.0 copy-start.12
  330.8 1.6 copy-start.11
  332.4 3.0 copy-start.10
  338.5 1.6 copy-start.9
  340.1 3.0 copy-start.8
  343.1 3.5 copy-start.15
  346.1 1.2 copy-start.7
  346.1 1.2 copy-start.20
  346.1 1.2 copy-start.21
  346.2 1.2 copy-start.22
  346.2 1.2 copy-start.23
where the time goes:
time: 353 us; the launch traced here: 349 us
  matrix products  272 us (77%)
  other arithmetic  30.2 us (9%)
  waiting for transfers between devices  22.2 us (6%)
  local copies, waits for them, and re-layouts  12.4 us (4%)
  starting transfers between devices  11.2 us (3%)
    dot_general x64, matrix products, matmul_prec(): return jnp.einsum(form, left, right, precision=lax.Precision.HIGHEST)  220 us
    dot_general x8, matrix products, first_section(): jnp.einsum('kn,nmc->kmc', lower, grid, preferred_element_type=jnp.float32)  38.5 us
    ppermute x5, waiting for transfers between devices, passed_along(): return lax.ppermute(array, axis, pairs)  22.2 us
    reduce_sum x1, other arithmetic, shards(): jnp.sum(weights[None] * jnp.exp(-decays[None] * steps[:, None, None]), ax...  19.4 us
    dot_general x8, matrix products, first_section(): jnp.einsum('kn,nmc->kmc', upper, grid, preferred_element_type=jnp.float32)  13.8 us
    ppermute x5, starting transfers between devices, passed_along(): return lax.ppermute(array, axis, pairs)  11.2 us
  transfers between devices with their start and end apart: 5, of which 2 were waited for; matrix products, arithmetic and copies ran while one was open for 18% of the time, Pallas kernels for 0%

commit v1 on v0

v1 whole, which is shorter than its diff:
```python
import functools
import math
from decimal import Decimal, localcontext

import jax
import jax.numpy as jnp
import numpy as np
from jax import lax
from jax.experimental import pallas as pl
from jax.experimental.pallas import tpu as pltpu
from jax.sharding import PartitionSpec as P

RATE_LOW, RATE_HIGH = 0.000390625, 0.03
NODES = 8
TILE = 512


def separable_basis(rows):
    cosines = [math.cos(math.pi * (j + 0.5) / NODES) for j in range(NODES)]
    with localcontext() as context:
        context.prec = 50
        times = [Decimal(str(round((rows - 1) / 2 * (1 - v), 2))) for v in cosines]
        span = RATE_HIGH - RATE_LOW
        rates = [Decimal(str(round(RATE_LOW + span * ((1 - v) / 2) ** 1.3, 6))) for v in cosines]
        table = [
            [(-r * t).exp() for t in times] + [(-r * t).exp() for t in range(rows)] for r in rates
        ]
        for i in range(NODES):
            best = max(range(i, NODES), key=lambda k: abs(table[k][i]))
            table[i], table[best] = table[best], table[i]
            inverse = 1 / table[i][i]
            table[i] = [v * inverse for v in table[i]]
            for k in range(NODES):
                if k != i:
                    factor = table[k][i]
                    table[k] = [a - factor * b for a, b in zip(table[k], table[i])]
        basis = np.array([[float(v) for v in table[i][NODES:]] for i in range(NODES)], np.float64)
    return [float(t) for t in times], basis


def make_tables(rows):
    times, basis = separable_basis(rows)
    place = np.arange(rows)
    delta = place[:, None] - place[None, :]
    wrapped = basis[:, delta % rows]
    lower = np.where(delta[None] >= 0, wrapped, 0.0)
    upper = np.where(delta[None] < 0, wrapped, 0.0)
    pieces = [lower[j] for j in range(NODES)] + [upper[j] for j in range(NODES)]
    pieces += [basis.T, np.zeros((rows, NODES))]
    outputs = np.concatenate(pieces, axis=1).astype(np.float32)
    moments = basis[:, ::-1].astype(np.float32)
    high = moments.astype(jnp.bfloat16)
    low = (moments - high.astype(np.float32)).astype(jnp.bfloat16)
    return times, outputs.astype(jnp.bfloat16), np.concatenate([high, low], axis=0)


def featurize(signal, taps, rim=None):
    whole = signal.astype(jnp.float32)
    row = lax.broadcasted_iota(jnp.int32, whole.shape, 0)
    result = taps[0:1] * whole
    for offset in range(1, taps.shape[0]):
        shifted = pltpu.roll(whole, offset, axis=0)
        for r in range(offset):
            edge = 0.0 if rim is None else rim[rim.shape[0] - offset + r : rim.shape[0] - offset + r + 1]
            shifted = jnp.where(row == r, edge, shifted)
        result = result + taps[offset : offset + 1] * shifted
    return result


def mix_kernel(key_ref, value_ref, taps_ref, mixed_ref):
    kf = featurize(key_ref[...], taps_ref[1])
    vf = featurize(value_ref[...], taps_ref[2])
    mixed_ref[...] = (kf * vf).astype(mixed_ref.dtype)


def coefficient_kernel(times, rows, residue_ref, rate_ref, near_ref, far_ref):
    weights, rates = residue_ref[...], rate_ref[...]
    far_weights = weights * jnp.exp(-rates * float(rows))
    near, far = [], []
    for t in times:
        decay = jnp.exp(-rates * t)
        near.append(jnp.sum(weights * decay, axis=0, keepdims=True))
        far.append(jnp.sum(far_weights * decay, axis=0, keepdims=True))
    keep = (lax.axis_index("seq") >= 2).astype(jnp.float32)
    near_ref[...] = jnp.concatenate(near, axis=0)
    far_ref[...] = jnp.concatenate(far, axis=0) * keep


def edge_kernel(
    times, edge, bounds, key_ref, value_ref, rims_ref, taps_ref, residue_ref, rate_ref, moment_ref,
    mixed_ref, fix_ref, middle_ref, third_ref, fourth_ref,
):
    tile = pl.program_id(0)
    keep = (lax.axis_index("seq") >= 1).astype(jnp.float32)
    rims = rims_ref[...].astype(jnp.float32) * keep
    kf = featurize(key_ref[...], taps_ref[1], rims[edge : 2 * edge])
    vf = featurize(value_ref[...], taps_ref[2], rims[2 * edge : 3 * edge])
    mixed = (kf * vf).astype(jnp.bfloat16)
    mixed_ref[...] = mixed
    fix_ref[...] = mixed[0:8]
    halves = jnp.dot(moment_ref[...], mixed, preferred_element_type=jnp.float32)
    moments = halves[:NODES] + halves[NODES:]
    weights, rates = residue_ref[...], rate_ref[...]
    decays = [jnp.exp(-rates * t) for t in times]
    state = decays[0] * moments[0:1]
    for j in range(1, NODES):
        state = state + decays[j] * moments[j : j + 1]
    state = state * (weights * jnp.exp(-rates))
    middle = [jnp.sum(decays[i] * state, axis=0, keepdims=True) for i in range(NODES)]
    middle_ref[...] = jnp.concatenate(middle, axis=0).astype(middle_ref.dtype)

    @pl.when((tile >= bounds[2]) & (tile < bounds[3]))
    def _():
        third_ref[...] = mixed

    @pl.when(tile >= bounds[3])
    def _():
        fourth_ref[...] = mixed


def finish_kernel(
    edge, fixed, query_ref, mixed_ref, back_ref, fix_ref, middle_ref, near_ref, far_ref, taps_ref, rims_ref,
    skip_ref, table_ref, _, out_ref, stack_ref,
):
    rows = query_ref.shape[0]
    keep = (lax.axis_index("seq") >= 1).astype(jnp.float32)
    mixed = mixed_ref[...].astype(jnp.float32)
    back = back_ref[...].astype(jnp.float32)
    if fixed:
        row = lax.broadcasted_iota(jnp.int32, back.shape, 0)
        back = jnp.where(row == 1, fix_ref[1:2].astype(jnp.float32), back)
    for j in range(NODES):
        stack_ref[j * rows : (j + 1) * rows] = (mixed * near_ref[j : j + 1]).astype(stack_ref.dtype)
        stack_ref[(NODES + j) * rows : (NODES + j + 1) * rows] = (back * far_ref[j : j + 1]).astype(stack_ref.dtype)
    middle = middle_ref[...].astype(jnp.float32) * keep
    middle = jnp.concatenate([middle, jnp.zeros_like(middle)], axis=0)
    stack_ref[2 * NODES * rows : 2 * NODES * rows + 2 * NODES] = middle.astype(stack_ref.dtype)
    conv = jnp.dot(table_ref[...], stack_ref[...], preferred_element_type=jnp.float32)
    conv = conv + skip_ref[...] * mixed
    qf = featurize(query_ref[...], taps_ref[0], rims_ref[0:edge].astype(jnp.float32) * keep)
    out_ref[...] = (qf * conv).astype(out_ref.dtype)


def ring(array, by):
    length = lax.axis_size("seq")
    return lax.ppermute(array, "seq", [(i, (i + by) % length) for i in range(length)])


def params(limit=24):
    return pltpu.CompilerParams(vmem_limit_bytes=limit * 1024 * 1024)


def shards(query_in, key_in, value_in, short_filter, residue, rate, skip):
    rows, width = query_in.shape
    kinds, count, _ = short_filter.shape
    edge = count - 1
    modes = residue.shape[1]
    times, table, moment_table = make_tables(rows)
    table, moment_table = jnp.asarray(table), jnp.asarray(moment_table)
    residue_t, rate_t, skip_row = residue.T, rate.T, skip.reshape(1, width)
    tile = math.gcd(TILE, width // 4)
    tiles = width // tile
    cuts = [0, tiles // 4, tiles // 2, 3 * tiles // 4, tiles]
    spans = [(cuts[i], cuts[i + 1]) for i in range(4)]

    def mixed_part(first, last):
        n = last - first
        return pl.pallas_call(
            mix_kernel,
            grid=(n,),
            in_specs=[pl.BlockSpec((rows, tile), lambda i: (0, first + i))] * 2
            + [pl.BlockSpec((kinds, count, tile), lambda i: (0, 0, first + i))],
            out_specs=pl.BlockSpec((rows, tile), lambda i: (0, i)),
            out_shape=jax.ShapeDtypeStruct((rows, n * tile), jnp.bfloat16),
            compiler_params=params(),
        )(key_in, value_in, short_filter)

    back = [None] * 4
    back[0] = ring(mixed_part(*spans[0]), 2)
    rims = ring(jnp.concatenate([query_in[rows - edge :], key_in[rows - edge :], value_in[rows - edge :]], axis=0), 1)
    back[1] = ring(mixed_part(*spans[1]), 2)

    near, far = pl.pallas_call(
        functools.partial(coefficient_kernel, times, rows),
        grid=(tiles,),
        in_specs=[pl.BlockSpec((modes, tile), lambda i: (0, i))] * 2,
        out_specs=[pl.BlockSpec((NODES, tile), lambda i: (0, i))] * 2,
        out_shape=[jax.ShapeDtypeStruct((NODES, width), jnp.float32)] * 2,
        compiler_params=params(),
    )(residue_t, rate_t)

    column = lambda i: (0, i)
    mixed, fix, middle, third, fourth = pl.pallas_call(
        functools.partial(edge_kernel, times, edge, cuts),
        grid=(tiles,),
        in_specs=[
            pl.BlockSpec((rows, tile), column),
            pl.BlockSpec((rows, tile), column),
            pl.BlockSpec((kinds * edge, tile), column),
            pl.BlockSpec((kinds, count, tile), lambda i: (0, 0, i)),
            pl.BlockSpec((modes, tile), column),
            pl.BlockSpec((modes, tile), column),
            pl.BlockSpec((2 * NODES, rows), lambda i: (0, 0)),
        ],
        out_specs=[
            pl.BlockSpec((rows, tile), column),
            pl.BlockSpec((8, tile), column),
            pl.BlockSpec((NODES, tile), column),
            pl.BlockSpec((rows, tile), lambda i: (0, jnp.clip(i - cuts[2], 0, cuts[3] - cuts[2] - 1))),
            pl.BlockSpec((rows, tile), lambda i: (0, jnp.clip(i - cuts[3], 0, cuts[4] - cuts[3] - 1))),
        ],
        out_shape=[
            jax.ShapeDtypeStruct((rows, width), jnp.bfloat16),
            jax.ShapeDtypeStruct((8, width), jnp.bfloat16),
            jax.ShapeDtypeStruct((NODES, width), jnp.bfloat16),
            jax.ShapeDtypeStruct((rows, (cuts[3] - cuts[2]) * tile), jnp.bfloat16),
            jax.ShapeDtypeStruct((rows, (cuts[4] - cuts[3]) * tile), jnp.bfloat16),
        ],
        compiler_params=params(),
    )(key_in, value_in, rims, short_filter, residue_t, rate_t, moment_table)
    middle = ring(middle, 1)
    fix = ring(fix[:, : cuts[2] * tile], 2)
    back[2] = ring(third, 2)
    back[3] = ring(fourth, 2)

    def finish(part, out):
        first, last = spans[part]
        own = lambda i: (0, first + i)
        fixed = part < 2
        return pl.pallas_call(
            functools.partial(finish_kernel, edge, fixed),
            grid=(last - first,),
            in_specs=[
                pl.BlockSpec((rows, tile), own),
                pl.BlockSpec((rows, tile), own),
                pl.BlockSpec((rows, tile), lambda i: (0, i)),
                pl.BlockSpec((8, tile), own if fixed else (lambda i: (0, 0))),
                pl.BlockSpec((NODES, tile), own),
                pl.BlockSpec((NODES, tile), own),
                pl.BlockSpec((NODES, tile), own),
                pl.BlockSpec((kinds, count, tile), lambda i: (0, 0, first + i)),
                pl.BlockSpec((kinds * edge, tile), own),
                pl.BlockSpec((1, tile), own),
                pl.BlockSpec(table.shape, lambda i: (0, 0)),
                pl.BlockSpec(memory_space=pl.ANY),
            ],
            out_specs=pl.BlockSpec((rows, tile), own),
            out_shape=jax.ShapeDtypeStruct((rows, width), jnp.bfloat16),
            scratch_shapes=[pltpu.VMEM((table.shape[1], tile), jnp.bfloat16)],
            input_output_aliases={11: 0} if out is not None else {},
            compiler_params=params(),
        )(query_in, mixed, back[part], fix, middle, near, far, short_filter, rims, skip_row, table,
          query_in if out is None else out)

    out = None
    for part in range(4):
        out = finish(part, out)
    return out


def solution(mesh):
    return jax.shard_map(
        shards,
        mesh=mesh,
        in_specs=(P(("grp", "seq"), None),) * 3 + (P(),) * 4,
        out_specs=P(("grp", "seq"), None),
        check_vma=False,
    )
```

time: 353 us -> 49.7 us (0.14)
  the two profiles are of different devices: /device:TPU:24 before, /device:TPU:0 now
where the time goes in v1:
time: 49.7 us; the launch traced here: 49.4 us
  waiting for transfers between devices  21 us (42%)
  Pallas kernels  13.3 us (27%)
  starting transfers between devices  9.87 us (20%)
  local copies, waits for them, and re-layouts  5.11 us (10%)
    ppermute x7, waiting for transfers between devices, ring(): lax.ppermute(array, 'seq', [(i, (i + by) % length) for i in range(length)])  21 us
    ppermute x7, starting transfers between devices, ring(): lax.ppermute(array, 'seq', [(i, (i + by) % length) for i in range(length)])  9.87 us
    pallas_call x4, Pallas kernels, finish(): pl.pallas_call(functools.partial(finish_kernel, edge, fixed), grid=(last...  7.21 us
    pallas_call x1, Pallas kernels, shards(): pl.pallas_call(functools.partial(edge_kernel, times, edge, cuts), grid=(t...  3.89 us
    unnamed x18, local copies, waits for them, and re-layouts  2.49 us
    pallas_call x1, Pallas kernels, shards(): pl.pallas_call(functools.partial(coefficient_kernel, times, rows), grid=(...  1.14 us
    pallas_call x2, Pallas kernels, mixed_part(): pl.pallas_call(mix_kernel, grid=(n,), in_specs=[pl.BlockSpec((rows, tile)...  1.08 us
  transfers between devices with their start and end apart: 7, of which 2 were waited for; matrix products, arithmetic and copies ran while one was open for 0% of the time, Pallas kernels for 23%

profile of v1, /device:TPU:0, one launch (start us, length us, event | category | flops | bytes accessed | tf_op | source)
XLA Modules:
  0.0 49.4 jit_solution(10846905382177628260)
XLA Ops:
  0.0 0.9 %slice.13 = bf16[2,4096]{1,0:T(2,128)(2,1)S(1)} slice(bf16[128,4096]{1,0:T(8,128)(2,1)} %key_ref.5), slice={[126:128], [0:4096]} | slice | bytes 32768 | tf_op jit(solution)/shard_map/slice | solution.py:180
  0.9 0.9 %slice.14 = bf16[2,4096]{1,0:T(2,128)(2,1)S(1)} slice(bf16[128,4096]{1,0:T(8,128)(2,1)} %value_ref.5), slice={[126:128], [0:4096]} | slice | bytes 32768 | tf_op jit(solution)/shard_map/slice | solution.py:180
  1.8 0.9 %slice.12 = bf16[2,4096]{1,0:T(2,128)(2,1)S(1)} slice(bf16[128,4096]{1,0:T(8,128)(2,1)} %query_ref.7), slice={[126:128], [0:4096]} | slice | bytes 32768 | tf_op jit(solution)/shard_map/slice | solution.py:180
  2.6 0.1 pad_maximum_fusion
  2.7 0.5 %collective-permute-start = (bf16[6,4096]{1,0:T(8,128)(2,1)S(1)}, bf16[6,4096]{1,0:T(8,128)(2,1)S(1)}, u32[]{:S(2)}, u32[]{:S(2)}) collective-permute-start(bf16[6,4096]{1,0:T(8,128)(2,1)S(1)} %pad_maximum_fusion), channel_id=1, source_target_pairs={{0,1},{1,2},{2,3},{3,4},{4,5},{5,6},{6,7},{7,8},{8,9},{9,10},{10,1... | collective-permute-start | bytes 147464 | tf_op jit(solution)/shard_map/ppermute | solution.py:146
  3.2 1.2 %copy-done.2 = bf16[128,4096]{1,0:T(8,128)(2,1)S(1)} copy-done((bf16[128,4096]{1,0:T(8,128)(2,1)S(1)}, bf16[128,4096]{1,0:T(8,128)(2,1)}, u32[]{:S(2)}) %copy-start.2) | copy-done | bytes 1048600
  4.4 1.2 %copy-done.3 = bf16[128,4096]{1,0:T(8,128)(2,1)S(1)} copy-done((bf16[128,4096]{1,0:T(8,128)(2,1)S(1)}, bf16[128,4096]{1,0:T(8,128)(2,1)}, u32[]{:S(2)}) %copy-start.3) | copy-done | bytes 1048600
  5.7 0.5 %shard_map.94 = bf16[128,1024]{1,0:T(8,128)(2,1)S(1)} custom-call(bf16[128,4096]{1,0:T(8,128)(2,1)S(1)} %copy-done.2, bf16[128,4096]{1,0:T(8,128)(2,1)S(1)} %copy-done.3, f32[3,3,4096]{2,1,0:T(4,128)S(1)} %copy-done.1), custom_call_target="tpu_custom_call" | custom-call | tf_op jit(solution)/shard_map/pallas_call | solution.py:168
  6.2 0.0 copy-start.5
  6.2 0.0 copy-start.6
  6.2 2.6 %collective-permute-start.6 = (bf16[128,1024]{1,0:T(8,128)(2,1)S(1)}, bf16[128,1024]{1,0:T(8,128)(2,1)S(1)}, u32[]{:S(2)}, u32[]{:S(2)}) collective-permute-start(bf16[128,1024]{1,0:T(8,128)(2,1)S(1)} %shard_map.94), channel_id=1, source_target_pairs={{0,2},{1,3},{2,4},{3,5},{4,6},{5,7},{6,8},{7,9},{8,10},{9,11},{10,... | collective-permute-start | bytes 786440 | tf_op jit(solution)/shard_map/ppermute | solution.py:146
  8.8 0.5 %shard_map.93 = bf16[128,1024]{1,0:T(8,128)(2,1)S(1)} custom-call(bf16[128,4096]{1,0:T(8,128)(2,1)S(1)} %copy-done.2, bf16[128,4096]{1,0:T(8,128)(2,1)S(1)} %copy-done.3, f32[3,3,4096]{2,1,0:T(4,128)S(1)} %copy-done.1), custom_call_target="tpu_custom_call" | custom-call | tf_op jit(solution)/shard_map/pallas_call | solution.py:168
  9.4 1.6 %collective-permute-start.5 = (bf16[128,1024]{1,0:T(8,128)(2,1)S(1)}, bf16[128,1024]{1,0:T(8,128)(2,1)S(1)}, u32[]{:S(2)}, u32[]{:S(2)}) collective-permute-start(bf16[128,1024]{1,0:T(8,128)(2,1)S(1)} %shard_map.93), channel_id=1, source_target_pairs={{0,2},{1,3},{2,4},{3,5},{4,6},{5,7},{6,8},{7,9},{8,10},{9,11},{10,... | collective-permute-start | bytes 786440 | tf_op jit(solution)/shard_map/ppermute | solution.py:146
  10.9 0.0 collective-permute-done.rims_ref
  11.0 0.0 copy-start
  11.0 3.9 %shard_map.91 = (bf16[128,4096]{1,0:T(8,128)(2,1)S(1)}, bf16[8,4096]{1,0:T(8,128)(2,1)S(1)}, bf16[8,4096]{1,0:T(8,128)(2,1)S(1)}, bf16[128,1024]{1,0:T(8,128)(2,1)S(1)}, bf16[128,1024]{1,0:T(8,128)(2,1)S(1)}) custom-call(bf16[128,4096]{1,0:T(8,128)(2,1)S(1)} %copy-done.2, bf16[128,4096]{1,0:T(8,128)(2,1)S(1)} %copy-done.3, ...), custom_call_target="tpu_custom_call" | custom-call | tf_op jit(solution)/shard_map/pallas_call | solution.py:193
  14.9 0.0 copy-start.4
  14.9 1.6 %collective-permute-start.4 = (bf16[128,1024]{1,0:T(8,128)(2,1)S(1)}, bf16[128,1024]{1,0:T(8,128)(2,1)S(1)}, u32[]{:S(2)}, u32[]{:S(2)}) collective-permute-start(bf16[128,1024]{1,0:T(8,128)(2,1)S(1)} %get-tuple-element.18), channel_id=1, source_target_pairs={{0,2},{1,3},{2,4},{3,5},{4,6},{5,7},{6,8},{7,9},{8,10},{9,11},{10,... | collective-permute-start | bytes 786440 | tf_op jit(solution)/shard_map/ppermute | solution.py:146
  16.5 1.5 %collective-permute-start.1 = (bf16[128,1024]{1,0:T(8,128)(2,1)S(1)}, bf16[128,1024]{1,0:T(8,128)(2,1)S(1)}, u32[]{:S(2)}, u32[]{:S(2)}) collective-permute-start(bf16[128,1024]{1,0:T(8,128)(2,1)S(1)} %get-tuple-element.13), channel_id=1, source_target_pairs={{0,2},{1,3},{2,4},{3,5},{4,6},{5,7},{6,8},{7,9},{8,10},{9,11},{10,... | collective-permute-start | bytes 786440 | tf_op jit(solution)/shard_map/ppermute | solution.py:146
  18.0 1.5 %collective-permute-start.2 = (bf16[8,2048]{1,0:T(8,128)(2,1)S(1)}, bf16[8,2048]{1,0:T(8,128)(2,1)S(1)}, u32[]{:S(2)}, u32[]{:S(2)}) collective-permute-start(bf16[8,2048]{1,0:T(8,128)(2,1)S(1)} %slice.15), channel_id=1, source_target_pairs={{0,2},{1,3},{2,4},{3,5},{4,6},{5,7},{6,8},{7,9},{8,10},{9,11},{10,... | collective-permute-start | bytes 98312 | tf_op jit(solution)/shard_map/ppermute | solution.py:146
  19.5 16.3 %collective-permute-done.2.fix_ref = bf16[8,2048]{1,0:T(8,128)(2,1)S(1)} collective-permute-done((bf16[8,2048]{1,0:T(8,128)(2,1)S(1)}, bf16[8,2048]{1,0:T(8,128)(2,1)S(1)}, u32[]{:S(2)}, u32[]{:S(2)}) %collective-permute-start.2) | collective-permute-done | bytes 32800 | tf_op jit(solution)/shard_map/ppermute | solution.py:146
  35.8 0.6 %collective-permute-start.3 = (bf16[8,4096]{1,0:T(8,128)(2,1)S(1)}, bf16[8,4096]{1,0:T(8,128)(2,1)S(1)}, u32[]{:S(2)}, u32[]{:S(2)}) collective-permute-start(bf16[8,4096]{1,0:T(8,128)(2,1)S(1)} %get-tuple-element.15), channel_id=1, source_target_pairs={{0,1},{1,2},{2,3},{3,4},{4,5},{5,6},{6,7},{7,8},{8,9},{9,10},{10,1... | collective-permute-start | bytes 196616 | tf_op jit(solution)/shard_map/ppermute | solution.py:146
  36.4 1.1 %shard_map.92 = (f32[8,4096]{1,0:T(8,128)S(1)}, f32[8,4096]{1,0:T(8,128)S(1)}) custom-call(f32[16,4096]{1,0:T(8,128)S(1)} %bitcast.4, f32[16,4096]{1,0:T(8,128)S(1)} %bitcast.6), custom_call_target="tpu_custom_call" | custom-call | tf_op jit(solution)/shard_map/pallas_call | solution.py:183
  37.5 4.6 %collective-permute-done.3.middle_ref = bf16[8,4096]{1,0:T(8,128)(2,1)S(1)} collective-permute-done((bf16[8,4096]{1,0:T(8,128)(2,1)S(1)}, bf16[8,4096]{1,0:T(8,128)(2,1)S(1)}, u32[]{:S(2)}, u32[]{:S(2)}) %collective-permute-start.3) | collective-permute-done | bytes 65568 | tf_op jit(solution)/shard_map/ppermute | solution.py:146
  42.2 0.0 collective-permute-done.6.back_ref
  42.2 1.8 %shard_map.95._ = bf16[128,4096]{1,0:T(8,128)(2,1)} custom-call(bf16[128,4096]{1,0:T(8,128)(2,1)S(1)} %copy-done, bf16[128,4096]{1,0:T(8,128)(2,1)S(1)} %get-tuple-element.12.mixed_ref, bf16[128,1024]{1,0:T(8,128)(2,1)S(1)} %collective-permute-done.6.back_ref, bf16[8,2048]{1,0:T(8,128)(2,1)S(1)} %collective-permute-done.2.fix_ref, ...), custom_call_target="tpu_custom_call" | custom-call | tf_op jit(solution)/shard_map/pallas_call | solution.py:230
  44.0 0.0 collective-permute-done.5.back_ref
  44.0 1.8 %shard_map.96._ = bf16[128,4096]{1,0:T(8,128)(2,1)} custom-call(bf16[128,4096]{1,0:T(8,128)(2,1)S(1)} %copy-done, bf16[128,4096]{1,0:T(8,128)(2,1)S(1)} %get-tuple-element.12.mixed_ref, bf16[128,1024]{1,0:T(8,128)(2,1)S(1)} %collective-permute-done.5.back_ref, bf16[8,2048]{1,0:T(8,128)(2,1)S(1)} %collective-permute-done.2.fix_ref, ...), custom_call_target="tpu_custom_call", output_to_operand_aliasing={{}: (11, {})} | custom-call | tf_op jit(solution)/shard_map/pallas_call | solution.py:230
  45.8 0.0 collective-permute-done.4.back_ref
  45.8 1.8 %shard_map.97._ = bf16[128,4096]{1,0:T(8,128)(2,1)} custom-call(bf16[128,4096]{1,0:T(8,128)(2,1)S(1)} %copy-done, bf16[128,4096]{1,0:T(8,128)(2,1)S(1)} %get-tuple-element.12.mixed_ref, bf16[128,1024]{1,0:T(8,128)(2,1)S(1)} %collective-permute-done.4.back_ref, bf16[8,2048]{1,0:T(8,128)(2,1)S(1)} %collective-permute-done.2.fix_ref, ...), custom_call_target="tpu_custom_call", output_to_operand_aliasing={{}: (11, {})} | custom-call | tf_op jit(solution)/shard_map/pallas_call | solution.py:230
  47.6 0.0 collective-permute-done.1.back_ref
  47.6 1.8 %shard_map.98 = bf16[128,4096]{1,0:T(8,128)(2,1)} custom-call(bf16[128,4096]{1,0:T(8,128)(2,1)S(1)} %copy-done, bf16[128,4096]{1,0:T(8,128)(2,1)S(1)} %get-tuple-element.12.mixed_ref, bf16[128,1024]{1,0:T(8,128)(2,1)S(1)} %collective-permute-done.1.back_ref, bf16[8,2048]{1,0:T(8,128)(2,1)S(1)} %collective-permute-done.2.fix_ref, ...), custom_call_target="tpu_custom_call", output_to_operand_aliasing={{}: (11, {})} | custom-call | tf_op jit(solution)/shard_map/pallas_call | solution.py:230
  (13 shorter events, 0.0 us)
Async XLA Ops:
  0.0 3.2 %copy-start.1 = (f32[3,3,4096]{2,1,0:T(4,128)S(1)}, f32[3,3,4096]{2,1,0:T(4,128)}, u32[]{:S(2)}) copy-start(f32[3,3,4096]{2,1,0:T(4,128)} %taps_ref.13) | copy-start | bytes 442372
  2.7 8.3 %collective-permute-start = (bf16[6,4096]{1,0:T(8,128)(2,1)S(1)}, bf16[6,4096]{1,0:T(8,128)(2,1)S(1)}, u32[]{:S(2)}, u32[]{:S(2)}) collective-permute-start(bf16[6,4096]{1,0:T(8,128)(2,1)S(1)} %pad_maximum_fusion), channel_id=1, source_target_pairs={{0,1},{1,2},{2,3},{3,4},{4,5},{5,6},{6,7},{7,8},{8,9},{9,10},{10,1... | collective-permute-start | bytes 147464 | tf_op jit(solution)/shard_map/ppermute | solution.py:146
  3.2 1.2 %copy-start.2 = (bf16[128,4096]{1,0:T(8,128)(2,1)S(1)}, bf16[128,4096]{1,0:T(8,128)(2,1)}, u32[]{:S(2)}) copy-start(bf16[128,4096]{1,0:T(8,128)(2,1)} %key_ref.5) | copy-start | bytes 3145732
  4.4 1.2 %copy-start.3 = (bf16[128,4096]{1,0:T(8,128)(2,1)S(1)}, bf16[128,4096]{1,0:T(8,128)(2,1)}, u32[]{:S(2)}) copy-start(bf16[128,4096]{1,0:T(8,128)(2,1)} %value_ref.5) | copy-start | bytes 3145732
  6.2 4.7 %copy-start.5 = (f32[4096,16]{0,1:T(8,128)S(1)}, f32[4096,16]{0,1:T(8,128)}, u32[]{:S(2)}) copy-start(f32[4096,16]{0,1:T(8,128)} %param.13) | copy-start | bytes 786436
  6.2 4.7 %copy-start.6 = (f32[4096,16]{0,1:T(8,128)S(1)}, f32[4096,16]{0,1:T(8,128)}, u32[]{:S(2)}) copy-start(f32[4096,16]{0,1:T(8,128)} %param.14) | copy-start | bytes 786436
  6.2 36.0 %collective-permute-start.6 = (bf16[128,1024]{1,0:T(8,128)(2,1)S(1)}, bf16[128,1024]{1,0:T(8,128)(2,1)S(1)}, u32[]{:S(2)}, u32[]{:S(2)}) collective-permute-start(bf16[128,1024]{1,0:T(8,128)(2,1)S(1)} %shard_map.94), channel_id=1, source_target_pairs={{0,2},{1,3},{2,4},{3,5},{4,6},{5,7},{6,8},{7,9},{8,10},{9,11},{10,... | collective-permute-start | bytes 786440 | tf_op jit(solution)/shard_map/ppermute | solution.py:146
  8.8 2.1 %copy-start.8 = (bf16[16,128]{1,0:T(8,128)(2,1)S(1)}, bf16[16,128]{1,0:T(8,128)(2,1)}, u32[]{:S(2)}) copy-start(bf16[16,128]{1,0:T(8,128)(2,1)} %constant.5.clone.moment_ref) | copy-start | bytes 12292
  9.4 34.7 %collective-permute-start.5 = (bf16[128,1024]{1,0:T(8,128)(2,1)S(1)}, bf16[128,1024]{1,0:T(8,128)(2,1)S(1)}, u32[]{:S(2)}, u32[]{:S(2)}) collective-permute-start(bf16[128,1024]{1,0:T(8,128)(2,1)S(1)} %shard_map.93), channel_id=1, source_target_pairs={{0,2},{1,3},{2,4},{3,5},{4,6},{5,7},{6,8},{7,9},{8,10},{9,11},{10,... | collective-permute-start | bytes 786440 | tf_op jit(solution)/shard_map/ppermute | solution.py:146
  11.0 31.2 %copy-start = (bf16[128,4096]{1,0:T(8,128)(2,1)S(1)}, bf16[128,4096]{1,0:T(8,128)(2,1)}, u32[]{:S(2)}) copy-start(bf16[128,4096]{1,0:T(8,128)(2,1)} %query_ref.7) | copy-start | bytes 3145732
  14.9 27.3 %copy-start.4 = (bf16[128,2064]{1,0:T(8,128)(2,1)S(1)}, bf16[128,2064]{1,0:T(8,128)(2,1)}, u32[]{:S(2)}) copy-start(bf16[128,2064]{1,0:T(8,128)(2,1)} %constant.4.clone.table_ref) | copy-start | bytes 1585156
  14.9 30.9 %collective-permute-start.4 = (bf16[128,1024]{1,0:T(8,128)(2,1)S(1)}, bf16[128,1024]{1,0:T(8,128)(2,1)S(1)}, u32[]{:S(2)}, u32[]{:S(2)}) collective-permute-start(bf16[128,1024]{1,0:T(8,128)(2,1)S(1)} %get-tuple-element.18), channel_id=1, source_target_pairs={{0,2},{1,3},{2,4},{3,5},{4,6},{5,7},{6,8},{7,9},{8,10},{9,11},{10,... | collective-permute-start | bytes 786440 | tf_op jit(solution)/shard_map/ppermute | solution.py:146
  16.5 31.2 %collective-permute-start.1 = (bf16[128,1024]{1,0:T(8,128)(2,1)S(1)}, bf16[128,1024]{1,0:T(8,128)(2,1)S(1)}, u32[]{:S(2)}, u32[]{:S(2)}) collective-permute-start(bf16[128,1024]{1,0:T(8,128)(2,1)S(1)} %get-tuple-element.13), channel_id=1, source_target_pairs={{0,2},{1,3},{2,4},{3,5},{4,6},{5,7},{6,8},{7,9},{8,10},{9,11},{10,... | collective-permute-start | bytes 786440 | tf_op jit(solution)/shard_map/ppermute | solution.py:146
  18.0 17.8 %collective-permute-start.2 = (bf16[8,2048]{1,0:T(8,128)(2,1)S(1)}, bf16[8,2048]{1,0:T(8,128)(2,1)S(1)}, u32[]{:S(2)}, u32[]{:S(2)}) collective-permute-start(bf16[8,2048]{1,0:T(8,128)(2,1)S(1)} %slice.15), channel_id=1, source_target_pairs={{0,2},{1,3},{2,4},{3,5},{4,6},{5,7},{6,8},{7,9},{8,10},{9,11},{10,... | collective-permute-start | bytes 98312 | tf_op jit(solution)/shard_map/ppermute | solution.py:146
  35.8 6.4 %collective-permute-start.3 = (bf16[8,4096]{1,0:T(8,128)(2,1)S(1)}, bf16[8,4096]{1,0:T(8,128)(2,1)S(1)}, u32[]{:S(2)}, u32[]{:S(2)}) collective-permute-start(bf16[8,4096]{1,0:T(8,128)(2,1)S(1)} %get-tuple-element.15), channel_id=1, source_target_pairs={{0,1},{1,2},{2,3},{3,4},{4,5},{5,6},{6,7},{7,8},{8,9},{9,10},{10,1... | collective-permute-start | bytes 196616 | tf_op jit(solution)/shard_map/ppermute | solution.py:146
  36.4 5.8 %copy-start.7 = (f32[4096]{0:T(1024)S(1)}, f32[4096]{0:T(1024)}, u32[]{:S(2)}) copy-start(f32[4096]{0:T(1024)} %param.15) | copy-start | bytes 49156

commit v2 on v1

v2 whole, which is shorter than its diff:
```python
import functools
import math
from decimal import Decimal, localcontext

import jax
import jax.numpy as jnp
import numpy as np
from jax import lax
from jax.experimental import pallas as pl
from jax.experimental.pallas import tpu as pltpu
from jax.sharding import PartitionSpec as P

RATE_LOW, RATE_HIGH = 0.000390625, 0.03
NODES = 8
OWN_COST = 80000000


def separable_basis(rows):
    cosines = [math.cos(math.pi * (j + 0.5) / NODES) for j in range(NODES)]
    with localcontext() as context:
        context.prec = 50
        times = [Decimal(str(round((rows - 1) / 2 * (1 - v), 2))) for v in cosines]
        span = RATE_HIGH - RATE_LOW
        rates = [Decimal(str(round(RATE_LOW + span * ((1 - v) / 2) ** 1.3, 6))) for v in cosines]
        table = [
            [(-r * t).exp() for t in times] + [(-r * t).exp() for t in range(rows)] for r in rates
        ]
        for i in range(NODES):
            best = max(range(i, NODES), key=lambda k: abs(table[k][i]))
            table[i], table[best] = table[best], table[i]
            inverse = 1 / table[i][i]
            table[i] = [v * inverse for v in table[i]]
            for k in range(NODES):
                if k != i:
                    factor = table[k][i]
                    table[k] = [a - factor * b for a, b in zip(table[k], table[i])]
        basis = np.array([[float(v) for v in table[i][NODES:]] for i in range(NODES)], np.float64)
    return [float(t) for t in times], basis


def make_tables(rows):
    times, basis = separable_basis(rows)
    place = np.arange(rows)
    delta = place[:, None] - place[None, :]
    wrapped = basis[:, delta % rows]
    lower = np.where(delta[None] >= 0, wrapped, 0.0)
    upper = np.where(delta[None] < 0, wrapped, 0.0)
    near = np.concatenate(list(lower) + [basis.T, np.zeros((rows, NODES))], axis=1).astype(np.float32)
    far = np.concatenate(list(upper), axis=1).astype(np.float32)
    moments = basis[:, ::-1].astype(np.float32)
    high = moments.astype(jnp.bfloat16)
    low = (moments - high.astype(np.float32)).astype(jnp.bfloat16)
    return times, near.astype(jnp.bfloat16), far.astype(jnp.bfloat16), np.concatenate([high, low], axis=0)


def shifted(whole, offset, rim):
    rolled = pltpu.roll(whole, offset, axis=0)
    top = rolled[:8]
    row = lax.broadcasted_iota(jnp.int32, top.shape, 0)
    for r in range(offset):
        at = None if rim is None else rim.shape[0] - offset + r
        top = jnp.where(row == r, 0.0 if rim is None else rim[at : at + 1], top)
    return top if whole.shape[0] == 8 else jnp.concatenate([top, rolled[8:]], axis=0)


def featurize(signal, taps, rim=None):
    whole = signal.astype(jnp.float32)
    result = taps[0:1] * whole
    for offset in range(1, taps.shape[0]):
        result = result + taps[offset : offset + 1] * shifted(whole, offset, rim)
    return result


def columns(start, stop, step):
    return [(at, min(at + step, stop)) for at in range(start, stop, step)]


def early_kernel(key_ref, value_ref, taps_ref, mixed_ref, key_vmem, value_vmem, taps_vmem, sems):
    rows, width = mixed_ref.shape
    spans = columns(0, width, 256)
    taps_copy = pltpu.make_async_copy(taps_ref.at[:, :, pl.ds(0, width)], taps_vmem, sems.at[0])
    taps_copy.start()
    copies = []
    for n, (a, b) in enumerate(spans):
        at = pl.ds(a, b - a)
        pair = (
            pltpu.make_async_copy(key_ref.at[:, at], key_vmem.at[:, at], sems.at[1 + 2 * n]),
            pltpu.make_async_copy(value_ref.at[:, at], value_vmem.at[:, at], sems.at[2 + 2 * n]),
        )
        for copy in pair:
            copy.start()
        copies.append(pair)
    taps_copy.wait()
    for (a, b), pair in zip(spans, copies):
        for copy in pair:
            copy.wait()
        kf = featurize(key_vmem[:, a:b], taps_vmem[1, :, a:b])
        vf = featurize(value_vmem[:, a:b], taps_vmem[2, :, a:b])
        mixed_ref[:, a:b] = (kf * vf).astype(mixed_ref.dtype)


def second_kernel(
    start, edge, _, query_ref, key_ref, value_ref, taps_ref, residue_ref, rate_ref, mixed_ref, rims_ref, key_vmem,
    value_vmem, taps_vmem, residue_vmem, rate_vmem, held, sems,
):
    rows, width = mixed_ref.shape
    whole = key_ref.shape[1]
    count = 0

    def copy(source, target):
        nonlocal count
        made = pltpu.make_async_copy(source, target, sems.at[count])
        made.start()
        count += 1
        return made

    taps_copy = copy(taps_ref, taps_vmem)
    spans = columns(start, start + width, 256)
    cut = lambda a, b: [
        copy(ref.at[:, pl.ds(a, b - a)], vmem.at[:, pl.ds(a, b - a)])
        for ref, vmem in ((key_ref, key_vmem), (value_ref, value_vmem))
    ]
    copies = [cut(a, b) for a, b in spans]
    rim_copy = copy(query_ref.at[pl.ds(rows - 8, 8)], held)
    rest = cut(start + width, whole) + cut(0, start)
    rest += [copy(residue_ref, residue_vmem), copy(rate_ref, rate_vmem)]
    taps_copy.wait()
    for (a, b), pair in zip(spans, copies):
        for made in pair:
            made.wait()
        kf = featurize(key_vmem[:, a:b], taps_vmem[1, :, a:b])
        vf = featurize(value_vmem[:, a:b], taps_vmem[2, :, a:b])
        mixed_ref[:, a - start : b - start] = (kf * vf).astype(mixed_ref.dtype)
    rim_copy.wait()
    for made in rest:
        made.wait()
    for n, last in enumerate((held[...], key_vmem[rows - 16 :][8:], value_vmem[rows - 16 :][8:])):
        rims_ref[:, n * whole : (n + 1) * whole] = last[8 - edge :]


def pass_kernel(*refs):
    del refs


def prepare_kernel(
    times, rows, residue_ref, rate_ref, moment_ref, c1, c2, near_ref, far_ref, state_ref, first_ref, second_ref,
    decay_ref, spread_ref,
):
    modes, width = rate_ref.shape
    keep = (lax.axis_index("seq") >= 2).astype(jnp.float32)
    early = c1.shape[1]
    for c, d in columns(0, width, 256):
        weights, rates = residue_ref[:, c:d], rate_ref[:, c:d]
        far_weights = weights * jnp.exp(-rates * float(rows))
        later = weights * jnp.exp(-rates)
        near, far = [], []
        for j, t in enumerate(times):
            decay = jnp.exp(-rates * t)
            near.append(jnp.sum(weights * decay, axis=0, keepdims=True))
            far.append(jnp.sum(far_weights * decay, axis=0, keepdims=True))
            decay_ref[j * modes : (j + 1) * modes, c:d] = decay
            spread_ref[j * modes : (j + 1) * modes, c:d] = later * decay
        near_ref[:, c:d] = jnp.concatenate(near, axis=0)
        far_ref[:, c:d] = jnp.concatenate(far, axis=0) * keep
        if c < state_ref.shape[1]:
            part = c1[:, c:d] if c < early else c2[:, c - early : d - early]
            state_ref[:, c:d] = modal_state(moment_ref, part, decay_ref, c, d)
            first_ref[:, c:d] = jnp.exp(-rates * float(rows - 1))
            second_ref[:, c:d] = jnp.exp(-rates * float(rows - 2))


def modal_state(moment_ref, mixed, decay_ref, c, d):
    halves = jnp.dot(moment_ref[...], mixed, preferred_element_type=jnp.float32)
    moments = halves[:NODES] + halves[NODES:]
    modes = decay_ref.shape[0] // NODES
    state = decay_ref[0:modes, c:d] * moments[0:1]
    for j in range(1, NODES):
        state = state + decay_ref[j * modes : (j + 1) * modes, c:d] * moments[j : j + 1]
    return state


def edge_kernel(
    edge, _, key_ref, value_ref, rims_ref, taps_ref, moment_ref, c1, c2, state_ref, first_ref, second_ref, decay_ref,
    spread_ref, c3, c4, head_ref, fix_ref, middle_ref,
):
    width = key_ref.shape[1]
    early = c1.shape[1] + c2.shape[1]
    modes = state_ref.shape[0]
    keep = (lax.axis_index("seq") >= 1).astype(jnp.float32)
    offset = 0
    for chunk in (c1, c2, c3, c4):
        for a, b in columns(0, chunk.shape[1], 256):
            c, d = offset + a, offset + b
            key_rim = rims_ref[:, width + c : width + d].astype(jnp.float32) * keep
            value_rim = rims_ref[:, 2 * width + c : 2 * width + d].astype(jnp.float32) * keep
            if c < early:
                kf = featurize(key_ref[0:16, c:d].astype(jnp.float32)[:8], taps_ref[1, :, c:d], key_rim)
                vf = featurize(value_ref[0:16, c:d].astype(jnp.float32)[:8], taps_ref[2, :, c:d], value_rim)
                head = (kf * vf).astype(jnp.bfloat16)
                head_ref[:, c:d] = head
                fix_ref[:, c:d] = head[:edge]
                delta = head.astype(jnp.float32) - chunk[0:16, a:b].astype(jnp.float32)[:8]
                state = state_ref[:, c:d] + first_ref[:, c:d] * delta[0:1] + second_ref[:, c:d] * delta[1:2]
            else:
                kf = featurize(key_ref[:, c:d], taps_ref[1, :, c:d], key_rim)
                vf = featurize(value_ref[:, c:d], taps_ref[2, :, c:d], value_rim)
                mixed = (kf * vf).astype(jnp.bfloat16)
                chunk[:, a:b] = mixed
                state = modal_state(moment_ref, mixed, decay_ref, c, d)
            middle = [
                jnp.sum(spread_ref[i * modes : (i + 1) * modes, c:d] * state, axis=0, keepdims=True)
                for i in range(NODES)
            ]
            middle_ref[:, c:d] = jnp.concatenate(middle, axis=0).astype(middle_ref.dtype)
        offset = offset + chunk.shape[1]


def own_kernel(
    edge, query_ref, c1, c2, c3, c4, head_ref, near_ref, taps_ref, rims_ref, skip_ref, middle_ref, table_ref, part_ref,
    gate_ref, stack_ref,
):
    rows, _ = query_ref.shape
    keep = (lax.axis_index("seq") >= 1).astype(jnp.float32)
    offset = 0
    for chunk in (c1, c2, c3, c4):
        for a, b in columns(0, chunk.shape[1], stack_ref.shape[1]):
            c, d = offset + a, offset + b
            mixed = chunk[:, a:b].astype(jnp.float32)
            if c < head_ref.shape[1]:
                mixed = jnp.concatenate([head_ref[:, c:d].astype(jnp.float32), mixed[8:]], axis=0)
            for j in range(NODES):
                stack_ref[j * rows : (j + 1) * rows, : b - a] = (mixed * near_ref[j : j + 1, c:d]).astype(stack_ref.dtype)
            middle = middle_ref[:, c:d].astype(jnp.float32) * keep
            middle = jnp.concatenate([middle, jnp.zeros_like(middle)], axis=0)
            stack_ref[NODES * rows : NODES * rows + 2 * NODES, : b - a] = middle.astype(stack_ref.dtype)
            conv = jnp.dot(table_ref[...], stack_ref[:, : b - a], preferred_element_type=jnp.float32)
            part_ref[:, c:d] = conv + skip_ref[:, c:d] * mixed
            rim = rims_ref[:, c:d].astype(jnp.float32) * keep
            gate_ref[:, c:d] = featurize(query_ref[:, c:d], taps_ref[0, :, c:d], rim)
        offset = offset + chunk.shape[1]


def finish_kernel(
    offset, fixed, back_ref, fix_ref, far_ref, part_ref, gate_ref, table_ref, _, out_ref, stack_ref,
    stage_ref, sems,
):
    rows, width = back_ref.shape
    copies = []
    for n, (a, b) in enumerate(columns(0, width, stack_ref.shape[1])):
        c, d = offset + a, offset + b
        back = back_ref[:, a:b].astype(jnp.float32)
        if fixed:
            top = back[:8]
            row = lax.broadcasted_iota(jnp.int32, top.shape, 0)
            top = jnp.where(row == 1, fix_ref[1:2, c:d].astype(jnp.float32), top)
            back = jnp.concatenate([top, back[8:]], axis=0)
        for j in range(NODES):
            stack_ref[j * rows : (j + 1) * rows, : b - a] = (back * far_ref[j : j + 1, c:d]).astype(stack_ref.dtype)
        conv = jnp.dot(table_ref[...], stack_ref[:, : b - a], preferred_element_type=jnp.float32)
        stage_ref[:, a:b] = (gate_ref[:, c:d] * (part_ref[:, c:d] + conv)).astype(stage_ref.dtype)
        copies.append(pltpu.make_async_copy(stage_ref.at[:, pl.ds(a, b - a)], out_ref.at[:, pl.ds(c, b - a)], sems.at[n]))
        copies[-1].start()
    for copy in copies:
        copy.wait()


def ring(array, by, closed=True):
    length = lax.axis_size("seq")
    return lax.ppermute(
        array, "seq", [(i, (i + by) % length) for i in range(length) if closed or i + by < length]
    )


def shards(query_in, key_in, value_in, short_filter, residue, rate, skip):
    rows, width = query_in.shape
    kinds, count, _ = short_filter.shape
    edge = count - 1
    modes = residue.shape[1]
    times, near_table, far_table, moment_table = make_tables(rows)
    near_table, far_table, moment_table = (jnp.asarray(t) for t in (near_table, far_table, moment_table))
    residue_t, rate_t, skip_row = residue.T, rate.T, skip.reshape(1, width)
    unit = width // 32
    cuts = [0, 8 * unit, 18 * unit, 25 * unit, 32 * unit]
    sizes = [cuts[i + 1] - cuts[i] for i in range(4)]
    bf16, f32 = jnp.bfloat16, jnp.float32
    vmem, hbm, anywhere = (pl.BlockSpec(memory_space=m) for m in (pltpu.VMEM, pltpu.HBM, pl.ANY))

    def call(body, ins, outs, operands, scratch=(), limit=40, cost=1, **kw):
        return pl.pallas_call(
            body,
            in_specs=ins,
            out_specs=[o[2] if len(o) > 2 else vmem for o in outs],
            out_shape=[jax.ShapeDtypeStruct(o[0], o[1]) for o in outs],
            scratch_shapes=list(scratch),
            compiler_params=pltpu.CompilerParams(vmem_limit_bytes=limit * 1024 * 1024),
            cost_estimate=pl.CostEstimate(flops=cost, bytes_accessed=cost, transcendentals=0),
            **kw,
        )(*(pltpu.with_memory_space_constraint(x, pltpu.HBM) if i is hbm else x for i, x in zip(ins, operands)))

    back = [None] * 4
    (c1,) = call(
        early_kernel,
        [hbm] * 3,
        [((rows, sizes[0]), bf16)],
        (key_in, value_in, short_filter),
        [
            pltpu.VMEM((rows, sizes[0]), bf16),
            pltpu.VMEM((rows, sizes[0]), bf16),
            pltpu.VMEM((kinds, count, sizes[0]), f32),
            pltpu.SemaphoreType.DMA((1 + 2 * len(columns(0, sizes[0], 256)),)),
        ],
    )
    back[0] = ring(c1, 2)
    c2, rims, key_v, value_v, taps_v, residue_v, rate_v = call(
        functools.partial(second_kernel, cuts[1], edge),
        [anywhere] + [hbm] * 6,
        [
            ((rows, sizes[1]), bf16),
            ((edge, kinds * width), bf16),
            ((rows, width), bf16),
            ((rows, width), bf16),
            (short_filter.shape, f32),
            ((modes, width), f32),
            ((modes, width), f32),
        ],
        (c1, query_in, key_in, value_in, short_filter, residue_t, rate_t),
        [pltpu.VMEM((8, width), bf16), pltpu.SemaphoreType.DMA((8 + 2 * len(columns(0, sizes[1], 256)),))],
    )
    rims_in = ring(rims, 1)
    back[1] = ring(c2, 2)
    near, far, *states = call(
        functools.partial(prepare_kernel, times, rows),
        [vmem] * 5,
        [((NODES, width), f32)] * 2 + [((modes, cuts[2]), f32)] * 3 + [((NODES * modes, width), f32)] * 2,
        (residue_v, rate_v, moment_table, c1, c2),
    )
    c3, c4, head, fix, middle = call(
        functools.partial(edge_kernel, edge),
        [anywhere] + [vmem] * 12,
        [
            ((rows, sizes[2]), bf16),
            ((rows, sizes[3]), bf16),
            ((8, cuts[2]), bf16),
            ((edge, cuts[2]), bf16),
            ((NODES, width), bf16),
        ],
        (back[0], key_v, value_v, rims_in, taps_v, moment_table, c1, c2, *states),
    )
    fix = ring(fix, 2)
    middle_in = ring(middle, 1)
    back[2] = ring(c3, 2)
    (c4,) = call(
        pass_kernel, [anywhere] * 3, [((rows, sizes[3]), bf16, anywhere)], (fix, middle_in, c4), input_output_aliases={2: 0}
    )
    back[3] = ring(c4, 2, closed=False)

    tile = 512
    part, gate = call(
        functools.partial(own_kernel, edge),
        [vmem] * 12,
        [((rows, width), f32)] * 2,
        (query_in, c1, c2, c3, c4, head, near, taps_v, rims_in, skip_row, middle_in, near_table),
        [pltpu.VMEM((near_table.shape[1], tile), bf16)],
        cost=OWN_COST,
    )
    out = None
    for i in range(4):
        (out,) = call(
            functools.partial(finish_kernel, cuts[i], i < 2),
            [vmem] * 6 + [anywhere],
            [((rows, width), bf16, hbm)],
            (back[i], fix, far, part, gate, far_table, query_in if out is None else out),
            [
                pltpu.VMEM((far_table.shape[1], tile), bf16),
                pltpu.VMEM((rows, sizes[i]), bf16),
                pltpu.SemaphoreType.DMA((len(columns(0, sizes[i], tile)),)),
            ],
            input_output_aliases={} if out is None else {6: 0},
        )
    return out


def solution(mesh):
    return jax.shard_map(
        shards,
        mesh=mesh,
        in_specs=(P(("grp", "seq"), None),) * 3 + (P(),) * 4,
        out_specs=P(("grp", "seq"), None),
        check_vma=False,
    )
```

time: 49.7 us -> 32.5 us (0.65)
  waiting for transfers between devices: 21 us -> 10.2 us
  local copies, waits for them, and re-layouts: 5.11 us -> 0.02 us
  starting transfers between devices: 9.87 us -> 7.51 us
  Pallas kernels: 13.3 us -> 14.4 us
    ppermute x7, waiting for transfers between devices: 21 us -> 10.2 us  [ring(): lax.ppermute(array, 'seq', [(i, (i + by) % length) for i in range(length)...]
    slice x4 -> x0, local copies, waits for them, and re-layouts: 2.63 us -> none  [the longest x1 0.9 us: shards(): key_in[rows - edge:]]
    unnamed x18 -> x10, local copies, waits for them, and re-layouts: 2.49 us -> 0.02 us
    ppermute x7, starting transfers between devices: 9.87 us -> 7.51 us  [ring(): lax.ppermute(array, 'seq', [(i, (i + by) % length) for i in range(length)...]
    pallas_call x8 -> x10, Pallas kernels: 13.3 us -> 14.4 us  [call(): pl.pallas_call(body, in_specs=ins, out_specs=[o[2] if len(o) > 2 else vme...]
  transfers between devices with their start and end apart: 7 -> 7, of which waited for: 2 -> 3; matrix products, arithmetic and copies ran while one was open for 0% -> 0% of each run, Pallas kernels for 23% -> 36%
where the time goes in v2:
time: 32.5 us; the launch traced here: 32.3 us
  Pallas kernels  14.4 us (44%)
  waiting for transfers between devices  10.2 us (31%)
  starting transfers between devices  7.51 us (23%)
    pallas_call x10, Pallas kernels, call(): pl.pallas_call(body, in_specs=ins, out_specs=[o[2] if len(o) > 2 else vme...  14.4 us
    ppermute x7, waiting for transfers between devices, ring(): lax.ppermute(array, 'seq', [(i, (i + by) % length) for i in range(length)...  10.2 us
    ppermute x7, starting transfers between devices, ring(): lax.ppermute(array, 'seq', [(i, (i + by) % length) for i in range(length)...  7.51 us
  transfers between devices with their start and end apart: 7, of which 3 were waited for; matrix products, arithmetic and copies ran while one was open for 0% of the time, Pallas kernels for 36%

profile of v2, /device:TPU:0, one launch (start us, length us, event | category | flops | bytes accessed | tf_op | source)
XLA Modules:
  0.0 32.3 jit_solution(10571192221060866104)
XLA Ops:
  0.0 1.4 %shard_map.100._.c1 = bf16[128,1024]{1,0:T(8,128)(2,1)S(1)} custom-call(bf16[128,4096]{1,0:T(8,128)(2,1)} %key_ref.3, bf16[128,4096]{1,0:T(8,128)(2,1)} %value_ref.3, f32[3,3,4096]{2,1,0:T(4,128)} %taps_ref.3), custom_call_target="tpu_custom_call" | custom-call | flops 1 | bytes 1 | tf_op jit(solution)/shard_map/pallas_call | solution.py:289
  1.4 0.0 copy-start.3
  1.4 3.0 %collective-permute-start = (bf16[128,1024]{1,0:T(8,128)(2,1)S(1)}, bf16[128,1024]{1,0:T(8,128)(2,1)S(1)}, u32[]{:S(2)}, u32[]{:S(2)}) collective-permute-start(bf16[128,1024]{1,0:T(8,128)(2,1)S(1)} %shard_map.100._.c1), channel_id=1, source_target_pairs={{0,2},{1,3},{2,4},{3,5},{4,6},{5,7},{6,8},{7,9},{8,10},{9,11},{10,... | collective-permute-start | bytes 786440 | tf_op jit(solution)/shard_map/ppermute | solution.py:269
  4.4 2.0 %shard_map.101 = (bf16[128,1280]{1,0:T(8,128)(2,1)S(1)}, bf16[2,12288]{1,0:T(2,128)(2,1)S(1)}, bf16[128,4096]{1,0:T(8,128)(2,1)S(1)}, bf16[128,4096]{1,0:T(8,128...) custom-call(bf16[128,1024]{1,0:T(8,128)(2,1)S(1)} %shard_map.100._.c1, ...), custom_call_target="tpu_custom_call" | custom-call | flops 1 | bytes 1 | tf_op jit(solution)/shard_map/pallas_call | solution.py:289
  6.5 0.1 collective-permute-start.1
  6.5 1.6 %collective-permute-start.6 = (bf16[128,1280]{1,0:T(8,128)(2,1)S(1)}, bf16[128,1280]{1,0:T(8,128)(2,1)S(1)}, u32[]{:S(2)}, u32[]{:S(2)}) collective-permute-start(bf16[128,1280]{1,0:T(8,128)(2,1)S(1)} %get-tuple-element.30.c2), channel_id=1, source_target_pairs={{0,2},{1,3},{2,4},{3,5},{4,6},{5,7},{6,8},{7,9},{8,10},{9,11},{10,... | collective-permute-start | bytes 983048 | tf_op jit(solution)/shard_map/ppermute | solution.py:269
  8.1 0.0 copy-done.3
  8.1 1.3 %shard_map.102 = (f32[8,4096]{1,0:T(8,128)S(1)}, f32[8,4096]{1,0:T(8,128)S(1)}, f32[16,2304]{1,0:T(8,128)S(1)}, f32[16,2304]{1,0:T(8,128)S(1)}, f32[16,2304]{1,0...) custom-call(f32[16,4096]{1,0:T(8,128)S(1)} %get-tuple-element.31.residue_ref, ...), custom_call_target="tpu_custom_call" | custom-call | flops 1 | bytes 1 | tf_op jit(solution)/shard_map/pallas_call | solution.py:289
  9.4 4.6 %collective-permute-done.1.rims_ref = bf16[2,12288]{1,0:T(2,128)(2,1)S(1)} collective-permute-done((bf16[2,12288]{1,0:T(2,128)(2,1)S(1)}, bf16[2,12288]{1,0:T(2,128)(2,1)S(1)}, u32[]{:S(2)}, u32[]{:S(2)}) %collective-permute-start.1) | collective-permute-done | bytes 49184 | tf_op jit(solution)/shard_map/ppermute | solution.py:269
  14.0 0.6 %collective-permute-done._.back_ref = bf16[128,1024]{1,0:T(8,128)(2,1)S(1)} collective-permute-done((bf16[128,1024]{1,0:T(8,128)(2,1)S(1)}, bf16[128,1024]{1,0:T(8,128)(2,1)S(1)}, u32[]{:S(2)}, u32[]{:S(2)}) %collective-permute-start) | collective-permute-done | bytes 262176 | tf_op jit(solution)/shard_map/ppermute | solution.py:269
  14.6 0.0 copy-start
  14.6 0.0 copy-start.2
  14.6 1.3 %shard_map.103 = (bf16[128,896]{1,0:T(8,128)(2,1)S(1)}, bf16[128,896]{1,0:T(8,128)(2,1)S(1)}, bf16[8,2304]{1,0:T(8,128)(2,1)S(1)}, bf16[2,2304]{1,0:T(2,128)(2,1)S(1)}, bf16[8,4096]{1,0:T(8,128)(2,1)S(1)}) custom-call(bf16[128,1024]{1,0:T(8,128)(2,1)S(1)} %collective-permute-done._.back_ref, bf16[128,4096]{1,0:T(8,128)(2,1)S(1)} %get-tuple-element.26.key_ref, ...), custom_call_target="tpu_custom_call" | custom-call | flops 1 | bytes 1 | tf_op jit(solution)/shard_map/pallas_call | solution.py:289
  15.9 0.0 copy-start.1
  15.9 0.1 collective-permute-start.3
  15.9 0.1 collective-permute-start.2
  16.0 1.5 %collective-permute-start.5 = (bf16[128,896]{1,0:T(8,128)(2,1)S(1)}, bf16[128,896]{1,0:T(8,128)(2,1)S(1)}, u32[]{:S(2)}, u32[]{:S(2)}) collective-permute-start(bf16[128,896]{1,0:T(8,128)(2,1)S(1)} %get-tuple-element.42.c3), channel_id=1, source_target_pairs={{0,2},{1,3},{2,4},{3,5},{4,6},{5,7},{6,8},{7,9},{8,10},{9,11},{10,... | collective-permute-start | bytes 688136 | tf_op jit(solution)/shard_map/ppermute | solution.py:269
  17.5 4.9 %collective-permute-done.2.refs_0_.fix_ref = bf16[2,2304]{1,0:T(2,128)(2,1)S(1)} collective-permute-done((bf16[2,2304]{1,0:T(2,128)(2,1)S(1)}, bf16[2,2304]{1,0:T(2,128)(2,1)S(1)}, u32[]{:S(2)}, u32[]{:S(2)}) %collective-permute-start.2) | collective-permute-done | bytes 9248 | tf_op jit(solution)/shard_map/ppermute | solution.py:269
  22.4 0.0 collective-permute-done.3.refs_1_.middle_ref
  22.4 1.3 %collective-permute-start.4 = (bf16[128,896]{1,0:T(8,128)(2,1)S(1)}, bf16[128,896]{1,0:T(8,128)(2,1)S(1)}, u32[]{:S(2)}, u32[]{:S(2)}) collective-permute-start(bf16[128,896]{1,0:T(8,128)(2,1)S(1)} %shard_map.104.c4), channel_id=1, source_target_pairs={{0,2},{1,3},{2,4},{3,5},{4,6},{5,7},{6,8},{7,9},{8,10},{9,11},{10,... | collective-permute-start | bytes 688136 | tf_op jit(solution)/shard_map/ppermute | solution.py:269
  23.7 0.0 copy-done
  23.7 0.0 copy-done.2
  23.7 0.0 copy-done.4
  23.8 3.4 %shard_map.105 = (f32[128,4096]{1,0:T(8,128)S(1)}, f32[128,4096]{1,0:T(8,128)S(1)}) custom-call(bf16[128,4096]{1,0:T(8,128)(2,1)S(1)} %copy-done, bf16[128,1024]{1,0:T(8,128)(2,1)S(1)} %shard_map.100._.c1, bf16[128,1280]{1,0:T(8,128)(2,1)S(1)} %get-tuple-element.30.c2, bf16[128,896]{1,0:T(8,128)(2,1)S(1)} %get-tuple-element.42.c3, ...), custom_call_target="tpu_custom_call" | custom-call | flops 80000000 | bytes 80000000 | tf_op jit(solution)/shard_map/pallas_call | solution.py:289
  27.2 0.0 copy-done.1
  27.2 1.2 %shard_map.106._ = bf16[128,4096]{1,0:T(8,128)(2,1)} custom-call(bf16[128,1024]{1,0:T(8,128)(2,1)S(1)} %collective-permute-done._.back_ref, bf16[2,2304]{1,0:T(2,128)(2,1)S(1)} %collective-permute-done.2.refs_0_.fix_ref, f32[8,4096]{1,0:T(8,128)S(1)} %get-tuple-element.41.far_ref, f32[128,4096]{1,0:T(8,128)S(1)} %get-tuple-element.45.part_ref, ...), custom_call_target="tpu_custom_call" | custom-call | flops 1 | bytes 1 | tf_op jit(solution)/shard_map/pallas_call | solution.py:289
  28.4 0.0 collective-permute-done.6.back_ref
  28.4 1.3 %shard_map.107._ = bf16[128,4096]{1,0:T(8,128)(2,1)} custom-call(bf16[128,1280]{1,0:T(8,128)(2,1)S(1)} %collective-permute-done.6.back_ref, bf16[2,2304]{1,0:T(2,128)(2,1)S(1)} %collective-permute-done.2.refs_0_.fix_ref, f32[8,4096]{1,0:T(8,128)S(1)} %get-tuple-element.41.far_ref, ...), custom_call_target="tpu_custom_call", output_to_operand_aliasing={{}: (6, {})} | custom-call | flops 1 | bytes 1 | tf_op jit(solution)/shard_map/pallas_call | solution.py:289
  29.8 0.0 collective-permute-done.5.back_ref
  29.8 1.2 %shard_map.108._ = bf16[128,4096]{1,0:T(8,128)(2,1)} custom-call(bf16[128,896]{1,0:T(8,128)(2,1)S(1)} %collective-permute-done.5.back_ref, bf16[2,2304]{1,0:T(2,128)(2,1)S(1)} %collective-permute-done.2.refs_0_.fix_ref, f32[8,4096]{1,0:T(8,128)S(1)} %get-tuple-element.41.far_ref, ...), custom_call_target="tpu_custom_call", output_to_operand_aliasing={{}: (6, {})} | custom-call | flops 1 | bytes 1 | tf_op jit(solution)/shard_map/pallas_call | solution.py:289
  31.0 0.0 collective-permute-done.4.back_ref
  31.1 1.2 %shard_map.109 = bf16[128,4096]{1,0:T(8,128)(2,1)} custom-call(bf16[128,896]{1,0:T(8,128)(2,1)S(1)} %collective-permute-done.4.back_ref, bf16[2,2304]{1,0:T(2,128)(2,1)S(1)} %collective-permute-done.2.refs_0_.fix_ref, f32[8,4096]{1,0:T(8,128)S(1)} %get-tuple-element.41.far_ref, ...), custom_call_target="tpu_custom_call", output_to_operand_aliasing={{}: (6, {})} | custom-call | flops 1 | bytes 1 | tf_op jit(solution)/shard_map/pallas_call | solution.py:289
  (2 shorter events, 0.0 us)
Async XLA Ops:
  1.4 6.7 %copy-start.3 = (bf16[16,128]{1,0:T(8,128)(2,1)S(1)}, bf16[16,128]{1,0:T(8,128)(2,1)}, u32[]{:S(2)}) copy-start(bf16[16,128]{1,0:T(8,128)(2,1)} %constant.8.clone.moment_ref) | copy-start | bytes 12292
  1.4 13.2 %collective-permute-start = (bf16[128,1024]{1,0:T(8,128)(2,1)S(1)}, bf16[128,1024]{1,0:T(8,128)(2,1)S(1)}, u32[]{:S(2)}, u32[]{:S(2)}) collective-permute-start(bf16[128,1024]{1,0:T(8,128)(2,1)S(1)} %shard_map.100._.c1), channel_id=1, source_target_pairs={{0,2},{1,3},{2,4},{3,5},{4,6},{5,7},{6,8},{7,9},{8,10},{9,11},{10,... | collective-permute-start | bytes 786440 | tf_op jit(solution)/shard_map/ppermute | solution.py:269
  6.5 7.5 %collective-permute-start.1 = (bf16[2,12288]{1,0:T(2,128)(2,1)S(1)}, bf16[2,12288]{1,0:T(2,128)(2,1)S(1)}, u32[]{:S(2)}, u32[]{:S(2)}) collective-permute-start(bf16[2,12288]{1,0:T(2,128)(2,1)S(1)} %get-tuple-element.28), channel_id=1, source_target_pairs={{0,1},{1,2},{2,3},{3,4},{4,5},{5,6},{6,7},{7,8},{8,9},{9,10},{10,1... | collective-permute-start | bytes 147464 | tf_op jit(solution)/shard_map/ppermute | solution.py:269
  6.5 21.9 %collective-permute-start.6 = (bf16[128,1280]{1,0:T(8,128)(2,1)S(1)}, bf16[128,1280]{1,0:T(8,128)(2,1)S(1)}, u32[]{:S(2)}, u32[]{:S(2)}) collective-permute-start(bf16[128,1280]{1,0:T(8,128)(2,1)S(1)} %get-tuple-element.30.c2), channel_id=1, source_target_pairs={{0,2},{1,3},{2,4},{3,5},{4,6},{5,7},{6,8},{7,9},{8,10},{9,11},{10,... | collective-permute-start | bytes 983048 | tf_op jit(solution)/shard_map/ppermute | solution.py:269
  14.6 9.1 %copy-start = (bf16[128,4096]{1,0:T(8,128)(2,1)S(1)}, bf16[128,4096]{1,0:T(8,128)(2,1)}, u32[]{:S(2)}) copy-start(bf16[128,4096]{1,0:T(8,128)(2,1)} %_.1) | copy-start | bytes 3145732
  14.6 9.1 %copy-start.2 = (bf16[128,1040]{1,0:T(8,128)(2,1)S(1)}, bf16[128,1040]{1,0:T(8,128)(2,1)}, u32[]{:S(2)}) copy-start(bf16[128,1040]{1,0:T(8,128)(2,1)} %constant.6.clone.table_ref) | copy-start | bytes 798724
  14.6 9.2 %copy-start.4 = (f32[4096]{0:T(1024)S(1)}, f32[4096]{0:T(1024)}, u32[]{:S(2)}) copy-start(f32[4096]{0:T(1024)} %param.16) | copy-start | bytes 49156
  15.9 11.3 %copy-start.1 = (bf16[128,1024]{1,0:T(8,128)(2,1)S(1)}, bf16[128,1024]{1,0:T(8,128)(2,1)}, u32[]{:S(2)}) copy-start(bf16[128,1024]{1,0:T(8,128)(2,1)} %constant.7.clone.table_ref) | copy-start | bytes 786436
  15.9 6.6 %collective-permute-start.3 = (bf16[8,4096]{1,0:T(8,128)(2,1)S(1)}, bf16[8,4096]{1,0:T(8,128)(2,1)S(1)}, u32[]{:S(2)}, u32[]{:S(2)}) collective-permute-start(bf16[8,4096]{1,0:T(8,128)(2,1)S(1)} %get-tuple-element.39), channel_id=1, source_target_pairs={{0,1},{1,2},{2,3},{3,4},{4,5},{5,6},{6,7},{7,8},{8,9},{9,10},{10,1... | collective-permute-start | bytes 196616 | tf_op jit(solution)/shard_map/ppermute | solution.py:269
  15.9 6.5 %collective-permute-start.2 = (bf16[2,2304]{1,0:T(2,128)(2,1)S(1)}, bf16[2,2304]{1,0:T(2,128)(2,1)S(1)}, u32[]{:S(2)}, u32[]{:S(2)}) collective-permute-start(bf16[2,2304]{1,0:T(2,128)(2,1)S(1)} %get-tuple-element.38), channel_id=1, source_target_pairs={{0,2},{1,3},{2,4},{3,5},{4,6},{5,7},{6,8},{7,9},{8,10},{9,11},{10,... | collective-permute-start | bytes 27656 | tf_op jit(solution)/shard_map/ppermute | solution.py:269
  16.0 13.8 %collective-permute-start.5 = (bf16[128,896]{1,0:T(8,128)(2,1)S(1)}, bf16[128,896]{1,0:T(8,128)(2,1)S(1)}, u32[]{:S(2)}, u32[]{:S(2)}) collective-permute-start(bf16[128,896]{1,0:T(8,128)(2,1)S(1)} %get-tuple-element.42.c3), channel_id=1, source_target_pairs={{0,2},{1,3},{2,4},{3,5},{4,6},{5,7},{6,8},{7,9},{8,10},{9,11},{10,... | collective-permute-start | bytes 688136 | tf_op jit(solution)/shard_map/ppermute | solution.py:269
  22.4 8.6 %collective-permute-start.4 = (bf16[128,896]{1,0:T(8,128)(2,1)S(1)}, bf16[128,896]{1,0:T(8,128)(2,1)S(1)}, u32[]{:S(2)}, u32[]{:S(2)}) collective-permute-start(bf16[128,896]{1,0:T(8,128)(2,1)S(1)} %shard_map.104.c4), channel_id=1, source_target_pairs={{0,2},{1,3},{2,4},{3,5},{4,6},{5,7},{6,8},{7,9},{8,10},{9,11},{10,... | collective-permute-start | bytes 688136 | tf_op jit(solution)/shard_map/ppermute | solution.py:269

commit v3 on v2

v3 whole, which is shorter than its diff:
```python
import functools
import math
from decimal import Decimal, localcontext

import jax
import jax.numpy as jnp
import numpy as np
from jax import lax
from jax.experimental import pallas as pl
from jax.experimental.pallas import tpu as pltpu
from jax.sharding import PartitionSpec as P

RATE_LOW, RATE_HIGH = 0.000390625, 0.03
NODES = 8
LAST_TILE = 256


def separable_basis(rows):
    cosines = [math.cos(math.pi * (j + 0.5) / NODES) for j in range(NODES)]
    with localcontext() as context:
        context.prec = 50
        times = [Decimal(str(round((rows - 1) / 2 * (1 - v), 2))) for v in cosines]
        span = RATE_HIGH - RATE_LOW
        rates = [Decimal(str(round(RATE_LOW + span * ((1 - v) / 2) ** 1.3, 6))) for v in cosines]
        table = [
            [(-r * t).exp() for t in times] + [(-r * t).exp() for t in range(rows)] for r in rates
        ]
        for i in range(NODES):
            best = max(range(i, NODES), key=lambda k: abs(table[k][i]))
            table[i], table[best] = table[best], table[i]
            inverse = 1 / table[i][i]
            table[i] = [v * inverse for v in table[i]]
            for k in range(NODES):
                if k != i:
                    factor = table[k][i]
                    table[k] = [a - factor * b for a, b in zip(table[k], table[i])]
        basis = np.array([[float(v) for v in table[i][NODES:]] for i in range(NODES)], np.float64)
    return [float(t) for t in times], basis


def make_tables(rows):
    times, basis = separable_basis(rows)
    place = np.arange(rows)
    delta = place[:, None] - place[None, :]
    wrapped = basis[:, delta % rows]
    lower = np.where(delta[None] >= 0, wrapped, 0.0)
    upper = np.where(delta[None] < 0, wrapped, 0.0)
    near = np.concatenate(list(lower), axis=1).astype(np.float32)
    far = np.concatenate(list(upper) + [basis.T, np.zeros((rows, NODES))], axis=1).astype(np.float32)
    moments = basis[:, ::-1].astype(np.float32)
    high = moments.astype(jnp.bfloat16)
    low = (moments - high.astype(np.float32)).astype(jnp.bfloat16)
    last = [float(v) for v in basis[:, rows - 1]]
    return times, last, near.astype(jnp.bfloat16), far.astype(jnp.bfloat16), np.concatenate([high, low], axis=0)


def shifted(whole, offset, rim):
    rolled = pltpu.roll(whole, offset, axis=0)
    top = rolled[:8]
    row = lax.broadcasted_iota(jnp.int32, top.shape, 0)
    for r in range(offset):
        at = None if rim is None else rim.shape[0] - offset + r
        top = jnp.where(row == r, 0.0 if rim is None else rim[at : at + 1], top)
    return top if whole.shape[0] == 8 else jnp.concatenate([top, rolled[8:]], axis=0)


def featurize(signal, taps, rim=None):
    whole = signal.astype(jnp.float32)
    result = taps[0:1] * whole
    for offset in range(1, taps.shape[0]):
        result = result + taps[offset : offset + 1] * shifted(whole, offset, rim)
    return result


def columns(start, stop, step):
    return [(at, min(at + step, stop)) for at in range(start, stop, step)]


def early_kernel(key_ref, value_ref, taps_ref, mixed_ref, key_vmem, value_vmem, taps_vmem, sems):
    rows, width = mixed_ref.shape
    spans = columns(0, width, 256)
    taps_copy = pltpu.make_async_copy(taps_ref.at[:, :, pl.ds(0, width)], taps_vmem, sems.at[0])
    taps_copy.start()
    copies = []
    for n, (a, b) in enumerate(spans):
        at = pl.ds(a, b - a)
        pair = (
            pltpu.make_async_copy(key_ref.at[:, at], key_vmem.at[:, at], sems.at[1 + 2 * n]),
            pltpu.make_async_copy(value_ref.at[:, at], value_vmem.at[:, at], sems.at[2 + 2 * n]),
        )
        for copy in pair:
            copy.start()
        copies.append(pair)
    taps_copy.wait()
    for (a, b), pair in zip(spans, copies):
        for copy in pair:
            copy.wait()
        kf = featurize(key_vmem[:, a:b], taps_vmem[1, :, a:b])
        vf = featurize(value_vmem[:, a:b], taps_vmem[2, :, a:b])
        mixed_ref[:, a:b] = (kf * vf).astype(mixed_ref.dtype)


def second_kernel(
    start, edge, _, query_ref, key_ref, value_ref, taps_ref, residue_ref, rate_ref, mixed_ref, rims_ref, taps_vmem,
    residue_vmem, rate_vmem, key_vmem, value_vmem, held, sems,
):
    rows, width = mixed_ref.shape
    whole = key_ref.shape[1]
    count = 0

    def copy(source, target):
        nonlocal count
        made = pltpu.make_async_copy(source, target, sems.at[count])
        made.start()
        count += 1
        return made

    taps_copy = copy(taps_ref, taps_vmem)
    spans = columns(0, width, 256)
    copies = [
        [
            copy(ref.at[:, pl.ds(start + a, b - a)], vmem.at[:, pl.ds(a, b - a)])
            for ref, vmem in ((key_ref, key_vmem), (value_ref, value_vmem))
        ]
        for a, b in spans
    ]
    rest = [copy(ref.at[pl.ds(rows - 8, 8)], held.at[n]) for n, ref in enumerate((query_ref, key_ref, value_ref))]
    rest += [copy(residue_ref, residue_vmem), copy(rate_ref, rate_vmem)]
    taps_copy.wait()
    for (a, b), pair in zip(spans, copies):
        for made in pair:
            made.wait()
        kf = featurize(key_vmem[:, a:b], taps_vmem[1, :, start + a : start + b])
        vf = featurize(value_vmem[:, a:b], taps_vmem[2, :, start + a : start + b])
        mixed_ref[:, a:b] = (kf * vf).astype(mixed_ref.dtype)
    for made in rest:
        made.wait()
    for n in range(held.shape[0]):
        rims_ref[:, n * whole : (n + 1) * whole] = held[n][8 - edge :]


def pass_kernel(*refs):
    del refs


def prepare_kernel(
    times, rows, key_ref, value_ref, residue_ref, rate_ref, moment_ref, c1, c2, near_ref, far_ref, state_ref, first_ref,
    second_ref, decay_ref, spread_ref, key_vmem, value_vmem, sems,
):
    modes, width = rate_ref.shape
    keep = (lax.axis_index("seq") >= 2).astype(jnp.float32)
    early, late = c1.shape[1], state_ref.shape[1]
    copies = []
    for ref, vmem in ((key_ref, key_vmem), (value_ref, value_vmem)):
        for tall, a, b in ((rows, late, width), (16, 0, late)):
            at = (pl.ds(0, tall), pl.ds(a, b - a))
            copies.append(pltpu.make_async_copy(ref.at[at], vmem.at[at], sems.at[len(copies)]))
            copies[-1].start()
    for c, d in columns(0, early, 256) + columns(early, late, 256) + columns(late, width, 256):
        weights, rates = residue_ref[:, c:d], rate_ref[:, c:d]
        far_weights = weights * jnp.exp(-rates * float(rows))
        later = weights * jnp.exp(-rates)
        near, far = [], []
        for j, t in enumerate(times):
            decay = jnp.exp(-rates * t)
            near.append(jnp.sum(weights * decay, axis=0, keepdims=True))
            far.append(jnp.sum(far_weights * decay, axis=0, keepdims=True))
            decay_ref[j * modes : (j + 1) * modes, c:d] = decay
            spread_ref[j * modes : (j + 1) * modes, c:d] = later * decay
        near_ref[:, c:d] = jnp.concatenate(near, axis=0)
        far_ref[:, c:d] = jnp.concatenate(far, axis=0) * keep
        if c < late:
            part = c1[:, c:d] if c < early else c2[:, c - early : d - early]
            state_ref[:, c:d] = modal_state(moment_ref, part, decay_ref, c, d)
            first_ref[:, c:d] = jnp.exp(-rates * float(rows - 1))
            second_ref[:, c:d] = jnp.exp(-rates * float(rows - 2))
    for copy in copies:
        copy.wait()


def modal_state(moment_ref, mixed, decay_ref, c, d):
    halves = jnp.dot(moment_ref[...], mixed, preferred_element_type=jnp.float32)
    moments = halves[:NODES] + halves[NODES:]
    modes = decay_ref.shape[0] // NODES
    state = decay_ref[0:modes, c:d] * moments[0:1]
    for j in range(1, NODES):
        state = state + decay_ref[j * modes : (j + 1) * modes, c:d] * moments[j : j + 1]
    return state


def edge_kernel(
    key_ref, value_ref, rims_ref, taps_ref, moment_ref, c1, c2, state_ref, first_ref, second_ref, decay_ref,
    spread_ref, head_ref, middle_ref, *late,
):
    width = key_ref.shape[1]
    early = c1.shape[1] + c2.shape[1]
    modes = state_ref.shape[0]
    keep = (lax.axis_index("seq") >= 1).astype(jnp.float32)
    offset = 0
    for chunk in (c1, c2, *late):
        for a, b in columns(0, chunk.shape[1], 256):
            c, d = offset + a, offset + b
            key_rim = rims_ref[:, width + c : width + d].astype(jnp.float32) * keep
            value_rim = rims_ref[:, 2 * width + c : 2 * width + d].astype(jnp.float32) * keep
            if c < early:
                kf = featurize(key_ref[0:16, c:d].astype(jnp.float32)[:8], taps_ref[1, :, c:d], key_rim)
                vf = featurize(value_ref[0:16, c:d].astype(jnp.float32)[:8], taps_ref[2, :, c:d], value_rim)
                head = (kf * vf).astype(jnp.bfloat16)
                delta = head.astype(jnp.float32) - chunk[0:16, a:b].astype(jnp.float32)[:8]
                state = state_ref[:, c:d] + first_ref[:, c:d] * delta[0:1] + second_ref[:, c:d] * delta[1:2]
            else:
                kf = featurize(key_ref[:, c:d], taps_ref[1, :, c:d], key_rim)
                vf = featurize(value_ref[:, c:d], taps_ref[2, :, c:d], value_rim)
                mixed = (kf * vf).astype(jnp.bfloat16)
                head = mixed[:8]
                state = modal_state(moment_ref, mixed, decay_ref, c, d)
                slot = c - early
                if slot < early:
                    second = head_ref[:, slot : slot + b - a].astype(jnp.float32)[1:2]
                    whole = (kf * vf)[:16]
                    row = lax.broadcasted_iota(jnp.int32, whole.shape, 0)
                    chunk[0:16, a:b] = jnp.where(row == 0, second, whole).astype(jnp.bfloat16)
                    chunk[16:, a:b] = mixed[16:]
                else:
                    chunk[:, a:b] = mixed
            head_ref[:, c:d] = head
            middle = [
                jnp.sum(spread_ref[i * modes : (i + 1) * modes, c:d] * state, axis=0, keepdims=True)
                for i in range(NODES)
            ]
            middle_ref[:, c:d] = jnp.concatenate(middle, axis=0).astype(middle_ref.dtype)
        offset = offset + chunk.shape[1]


def own_kernel(edge, start, query_ref, head_ref, near_ref, taps_ref, rims_ref, skip_ref, table_ref, *refs):
    *chunks, part_ref, gate_ref, stack_ref = refs
    rows, _ = query_ref.shape
    keep = (lax.axis_index("seq") >= 1).astype(jnp.float32)
    offset = start
    for chunk in chunks:
        for a, b in columns(0, chunk.shape[1], stack_ref.shape[1]):
            c, d = offset + a, offset + b
            mixed = chunk[:, a:b].astype(jnp.float32)
            mixed = jnp.concatenate([head_ref[:, c:d].astype(jnp.float32), mixed[8:]], axis=0)
            for j in range(NODES):
                stack_ref[j * rows : (j + 1) * rows, : b - a] = (mixed * near_ref[j : j + 1, c:d]).astype(stack_ref.dtype)
            conv = jnp.dot(table_ref[...], stack_ref[:, : b - a], preferred_element_type=jnp.float32)
            part_ref[:, c - start : d - start] = conv + skip_ref[:, c:d] * mixed
            rim = rims_ref[:, c:d].astype(jnp.float32) * keep
            gate_ref[:, c - start : d - start] = featurize(query_ref[:, c:d], taps_ref[0, :, c:d], rim)
        offset = offset + chunk.shape[1]


def finish_kernel(offset, base, slots, last, middle_ref, far_ref, part_ref, gate_ref, table_ref, *refs):
    keep = (lax.axis_index("seq") >= 1).astype(jnp.float32)
    if slots is None:
        _, *backs, out_ref, pre_ref, stack_ref, stage_ref, sems = refs
    else:
        pre_ref, _, *backs, out_ref, stack_ref, stage_ref, repair_ref, sems = refs
    copies = []

    def write(source, rows, c, d):
        copies.append(pltpu.make_async_copy(source, out_ref.at[pl.ds(0, rows), pl.ds(c, d - c)], sems.at[len(copies)]))
        copies[-1].start()

    at = 0
    for back_ref in backs:
        rows, width = back_ref.shape
        for a, b in columns(0, width, stack_ref.shape[1]):
            c, d = offset + at + a, offset + at + b
            back = back_ref[:, a:b].astype(jnp.float32)
            for j in range(NODES):
                stack_ref[j * rows : (j + 1) * rows, : b - a] = (back * far_ref[j : j + 1, c:d]).astype(stack_ref.dtype)
            middle = middle_ref[:, c:d].astype(jnp.float32) * keep
            middle = jnp.concatenate([middle, jnp.zeros_like(middle)], axis=0)
            stack_ref[NODES * rows : NODES * rows + 2 * NODES, : b - a] = middle.astype(stack_ref.dtype)
            conv = jnp.dot(table_ref[...], stack_ref[:, : b - a], preferred_element_type=jnp.float32)
            total = part_ref[:, c - base : d - base] + conv
            gate = gate_ref[:, c - base : d - base]
            stage_ref[:, at + a : at + b] = (gate * total).astype(stage_ref.dtype)
            write(stage_ref.at[:, pl.ds(at + a, b - a)], rows, c, d)
            if slots is None:
                pre_ref[0:16, c:d] = total[:16]
                pre_ref[16:32, c:d] = gate[:16]
                pre_ref[32:40, c:d] = back[:8]
        at = at + width
    start = 0
    for (first, stop), back_ref in zip(slots or (), backs):
        for c, d in columns(first, stop, 512):
            end = far_ref[0:1, c:d] * last[0]
            for j in range(1, NODES):
                end = end + far_ref[j : j + 1, c:d] * last[j]
            right = back_ref[0:16, c - first : d - first].astype(jnp.float32)[0:1]
            total = pre_ref[0:16, c:d]
            row = lax.broadcasted_iota(jnp.int32, total.shape, 0)
            total = jnp.where(row == 0, total + end * (right - pre_ref[33:34, c:d]), total)
            repair_ref[:, start + c - first : start + d - first] = (pre_ref[16:32, c:d] * total).astype(repair_ref.dtype)
        if stop > first:
            write(repair_ref.at[:, pl.ds(start, stop - first)], 16, first, stop)
        start = start + stop - first
    for copy in copies:
        copy.wait()


def ring(array, by, closed=True):
    length = lax.axis_size("seq")
    return lax.ppermute(
        array, "seq", [(i, (i + by) % length) for i in range(length) if closed or i + by < length]
    )


def shards(query_in, key_in, value_in, short_filter, residue, rate, skip):
    rows, width = query_in.shape
    kinds, count, _ = short_filter.shape
    edge = count - 1
    modes = residue.shape[1]
    times, last, near_table, far_table, moment_table = make_tables(rows)
    near_table, far_table, moment_table = (jnp.asarray(t) for t in (near_table, far_table, moment_table))
    residue_t, rate_t, skip_row = residue.T, rate.T, skip.reshape(1, width)
    unit = width // 32
    cuts = [0, 7 * unit, 15 * unit, 21 * unit, 27 * unit, 32 * unit]
    count_chunks = len(cuts) - 1
    sizes = [cuts[i + 1] - cuts[i] for i in range(count_chunks)]
    bf16, f32 = jnp.bfloat16, jnp.float32
    vmem, hbm, anywhere = (pl.BlockSpec(memory_space=m) for m in (pltpu.VMEM, pltpu.HBM, pl.ANY))

    def call(body, ins, outs, operands, scratch=(), limit=40, cost=1, **kw):
        return pl.pallas_call(
            body,
            in_specs=ins,
            out_specs=[o[2] if len(o) > 2 else vmem for o in outs],
            out_shape=[jax.ShapeDtypeStruct(o[0], o[1]) for o in outs],
            scratch_shapes=list(scratch),
            compiler_params=pltpu.CompilerParams(vmem_limit_bytes=limit * 1024 * 1024),
            cost_estimate=pl.CostEstimate(flops=cost, bytes_accessed=cost, transcendentals=0),
            **kw,
        )(*(pltpu.with_memory_space_constraint(x, pltpu.HBM) if i is hbm else x for i, x in zip(ins, operands)))

    back = [None] * count_chunks
    (c1,) = call(
        early_kernel,
        [hbm] * 3,
        [((rows, sizes[0]), bf16)],
        (key_in, value_in, short_filter),
        [
            pltpu.VMEM((rows, sizes[0]), bf16),
            pltpu.VMEM((rows, sizes[0]), bf16),
            pltpu.VMEM((kinds, count, sizes[0]), f32),
            pltpu.SemaphoreType.DMA((1 + 2 * len(columns(0, sizes[0], 256)),)),
        ],
    )
    back[0] = ring(c1, 2)
    c2, rims, taps_v, residue_v, rate_v = call(
        functools.partial(second_kernel, cuts[1], edge),
        [anywhere] + [hbm] * 6,
        [
            ((rows, sizes[1]), bf16),
            ((edge, kinds * width), bf16),
            (short_filter.shape, f32),
            ((modes, width), f32),
            ((modes, width), f32),
        ],
        (c1, query_in, key_in, value_in, short_filter, residue_t, rate_t),
        [
            pltpu.VMEM((rows, sizes[1]), bf16),
            pltpu.VMEM((rows, sizes[1]), bf16),
            pltpu.VMEM((kinds, 8, width), bf16),
            pltpu.SemaphoreType.DMA((3 + kinds + 2 * len(columns(0, sizes[1], 256)),)),
        ],
    )
    rims_in = ring(rims, 1)
    back[1] = ring(c2, 2)
    near, far, *states, key_v, value_v = call(
        functools.partial(prepare_kernel, times, rows),
        [hbm] * 2 + [vmem] * 5,
        [((NODES, width), f32)] * 2
        + [((modes, cuts[2]), f32)] * 3
        + [((NODES * modes, width), f32)] * 2
        + [((rows, width), bf16)] * 2,
        (key_in, value_in, residue_v, rate_v, moment_table, c1, c2),
        [pltpu.SemaphoreType.DMA((4,))],
    )
    late = range(2, count_chunks)
    head, middle, *chunks = call(
        edge_kernel,
        [vmem] * 12,
        [((8, width), bf16), ((NODES, width), bf16)] + [((rows, sizes[i]), bf16) for i in late],
        (key_v, value_v, rims_in, taps_v, moment_table, c1, c2, *states),
    )
    middle_in = ring(middle, 1)
    for i in late[:-1]:
        back[i] = ring(chunks[i - 2], 2, closed=i < late[-2])

    tile = 512

    def own(first, stop, some):
        return call(
            functools.partial(own_kernel, edge, cuts[first]),
            [vmem] * (7 + len(some)),
            [((rows, cuts[stop] - cuts[first]), f32)] * 2,
            (query_in, head, near, taps_v, rims_in, skip_row, near_table, *some),
            [pltpu.VMEM((near_table.shape[1], tile), bf16)],
        )

    early_own = own(0, 2, (c1, c2))
    (final,) = call(
        pass_kernel,
        [anywhere] * 4,
        [((rows, sizes[-1]), bf16, anywhere)],
        (middle_in, early_own[0], back[0], chunks[-1]),
        input_output_aliases={3: 0},
    )
    back[-1] = ring(final, 2, closed=False)
    late_own = own(2, count_chunks, chunks)

    def finish(first, stop, out, pre):
        some = range(first, stop)
        size = cuts[stop] - cuts[first]
        step = tile if stop < count_chunks else LAST_TILE
        pieces = sum(len(columns(0, sizes[i], step)) for i in some)
        scratch = [pltpu.VMEM((far_table.shape[1], step), bf16), pltpu.VMEM((rows, size), bf16)]
        slots = None
        if out is not None:
            slots = [(min(cuts[i] - cuts[2], cuts[2]), min(cuts[i + 1] - cuts[2], cuts[2])) for i in some]
            scratch.append(pltpu.VMEM((16, max(sum(b - a for a, b in slots), unit)), bf16))
        scratch.append(pltpu.SemaphoreType.DMA((pieces + len(some),)))
        return call(
            functools.partial(finish_kernel, cuts[first], cuts[0 if out is None else 2], slots, last),
            [vmem] * 5 + ([anywhere] if out is None else [vmem, anywhere]) + [vmem] * len(some),
            [((rows, width), bf16, anywhere)] + ([((40, cuts[2]), f32)] if out is None else []),
            (middle_in, far, *(early_own if out is None else late_own), far_table)
            + ((late_own[0],) if out is None else (pre, out))
            + tuple(back[i] for i in some),
            scratch,
            input_output_aliases={} if out is None else {6: 0},
        )

    out, pre = finish(0, 2, None, None)
    (out,) = finish(2, count_chunks - 1, out, pre)
    (out,) = finish(count_chunks - 1, count_chunks, out, pre)
    return out


def solution(mesh):
    return jax.shard_map(
        shards,
        mesh=mesh,
        in_specs=(P(("grp", "seq"), None),) * 3 + (P(),) * 4,
        out_specs=P(("grp", "seq"), None),
        check_vma=False,
    )
```

time: 32.5 us -> 30.2 us (0.929)
  the two profiles are of different devices: /device:TPU:0 before, /device:TPU:24 now
where the time goes in v3:
time: 30.2 us; the launch traced here: 30 us
  Pallas kernels  13.3 us (44%)
  starting transfers between devices  9.56 us (32%)
  waiting for transfers between devices  6.93 us (23%)
    pallas_call x10, Pallas kernels, call(): pl.pallas_call(body, in_specs=ins, out_specs=[o[2] if len(o) > 2 else vme...  13.3 us
    ppermute x7, starting transfers between devices, ring(): lax.ppermute(array, 'seq', [(i, (i + by) % length) for i in range(length)...  9.56 us
    ppermute x7, waiting for transfers between devices, ring(): lax.ppermute(array, 'seq', [(i, (i + by) % length) for i in range(length)...  6.93 us
  transfers between devices with their start and end apart: 7, of which 3 were waited for; matrix products, arithmetic and copies ran while one was open for 0% of the time, Pallas kernels for 36%

profile of v3, /device:TPU:24, one launch (start us, length us, event | category | flops | bytes accessed | tf_op | source)
XLA Modules:
  0.0 30.0 jit_solution(13934761739184924731)
XLA Ops:
  0.0 1.3 %shard_map.100._.c1.refs_0_ = bf16[128,896]{1,0:T(8,128)(2,1)S(1)} custom-call(bf16[128,4096]{1,0:T(8,128)(2,1)} %key_ref.5, bf16[128,4096]{1,0:T(8,128)(2,1)} %value_ref.5, f32[3,3,4096]{2,1,0:T(4,128)} %taps_ref.3), custom_call_target="tpu_custom_call" | custom-call | flops 1 | bytes 1 | tf_op jit(solution)/shard_map/pallas_call | solution.py:328
  1.3 0.0 copy-start.4
  1.3 1.6 %collective-permute-start.2 = (bf16[128,896]{1,0:T(8,128)(2,1)S(1)}, bf16[128,896]{1,0:T(8,128)(2,1)S(1)}, u32[]{:S(2)}, u32[]{:S(2)}) collective-permute-start(bf16[128,896]{1,0:T(8,128)(2,1)S(1)} %shard_map.100._.c1.refs_0_), channel_id=1, source_target_pairs={{0,2},{1,3},{2,4},{3,5},{4,6},{5,7},{6,8},{7,9},{8,10},{9,11},{10,... | collective-permute-start | bytes 688136 | tf_op jit(solution)/shard_map/ppermute | solution.py:307
  2.9 1.6 %shard_map.101 = (bf16[128,1024]{1,0:T(8,128)(2,1)S(1)}, bf16[2,12288]{1,0:T(2,128)(2,1)S(1)}, f32[3,3,4096]{2,1,0:T(4,128)S(1)}, f32[16,4096]{1,0:T(8,128)S(1)}, f32[16,4096]{1,0:T(8,128)S(1)}) custom-call(bf16[128,896]{1,0:T(8,128)(2,1)S(1)} %shard_map.100._.c1.refs_0_, bf16[128,4096]{1,0:T(8,128)(2,1)} %query_ref.5, bf16[128,4096]{1,0:T(8,128)(2,1)} %key_ref.5, ...), custom_call_target="tpu_custom_call" | custom-call | flops 1 | bytes 1 | tf_op jit(solution)/shard_map/pallas_call | solution.py:328
  4.5 0.1 collective-permute-start
  4.6 0.1 collective-permute-start.3
  4.6 0.0 copy-done.4
  4.6 1.4 %shard_map.102 = (f32[8,4096]{1,0:T(8,128)S(1)}, f32[8,4096]{1,0:T(8,128)S(1)}, f32[16,1920]{1,0:T(8,128)S(1)}, f32[16,1920]{1,0:T(8,128)S(1)}, f32[16,1920]{1,0...) custom-call(bf16[128,4096]{1,0:T(8,128)(2,1)} %key_ref.5, ...), custom_call_target="tpu_custom_call" | custom-call | flops 1 | bytes 1 | tf_op jit(solution)/shard_map/pallas_call | solution.py:328
  6.0 3.5 %collective-permute-done.rims_ref = bf16[2,12288]{1,0:T(2,128)(2,1)S(1)} collective-permute-done((bf16[2,12288]{1,0:T(2,128)(2,1)S(1)}, bf16[2,12288]{1,0:T(2,128)(2,1)S(1)}, u32[]{:S(2)}, u32[]{:S(2)}) %collective-permute-start) | collective-permute-done | bytes 49184 | tf_op jit(solution)/shard_map/ppermute | solution.py:307
  9.5 0.0 copy-start
  9.5 0.0 copy-start.2
  9.6 1.4 %shard_map.103 = (bf16[8,4096]{1,0:T(8,128)(2,1)S(1)}, bf16[8,4096]{1,0:T(8,128)(2,1)S(1)}, bf16[128,768]{1,0:T(8,128)(2,1)S(1)}, bf16[128,768]{1,0:T(8,128)(2,1)S(1)}, bf16[128,640]{1,0:T(8,128)(2,1)S(1)}) custom-call(bf16[128,4096]{1,0:T(8,128)(2,1)S(1)} %get-tuple-element.33.key_ref, bf16[128,4096]{1,0:T(8,128)(2,1)S(1)} %get-tuple-element.34.value_ref, ...), custom_call_target="tpu_custom_call" | custom-call | flops 1 | bytes 1 | tf_op jit(solution)/shard_map/pallas_call | solution.py:328
  11.0 0.1 collective-permute-start.1
  11.1 0.7 %collective-permute-start.4 = (bf16[128,768]{1,0:T(8,128)(2,1)S(1)}, bf16[128,768]{1,0:T(8,128)(2,1)S(1)}, u32[]{:S(2)}, u32[]{:S(2)}) collective-permute-start(bf16[128,768]{1,0:T(8,128)(2,1)S(1)} %get-tuple-element.46.refs_0_), channel_id=1, source_target_pairs={{0,2},{1,3},{2,4},{3,5},{4,6},{5,7},{6,8},{7,9},{8,10},{9,11},{10,... | collective-permute-start | bytes 589832 | tf_op jit(solution)/shard_map/ppermute | solution.py:307
  11.7 5.2 %collective-permute-start.5 = (bf16[128,768]{1,0:T(8,128)(2,1)S(1)}, bf16[128,768]{1,0:T(8,128)(2,1)S(1)}, u32[]{:S(2)}, u32[]{:S(2)}) collective-permute-start(bf16[128,768]{1,0:T(8,128)(2,1)S(1)} %get-tuple-element.47.refs_1_), channel_id=1, source_target_pairs={{0,2},{1,3},{2,4},{3,5},{4,6},{5,7},{6,8},{7,9},{8,10},{9,11},{10,... | collective-permute-start | bytes 589832 | tf_op jit(solution)/shard_map/ppermute | solution.py:307
  16.9 0.0 copy-done
  16.9 0.0 copy-done.2
  16.9 0.0 copy-done.3
  17.0 1.5 %shard_map.105 = (f32[128,1920]{1,0:T(8,128)S(1)}, f32[128,1920]{1,0:T(8,128)S(1)}) custom-call(bf16[128,4096]{1,0:T(8,128)(2,1)S(1)} %copy-done, bf16[8,4096]{1,0:T(8,128)(2,1)S(1)} %get-tuple-element.44.head_ref, f32[8,4096]{1,0:T(8,128)S(1)} %get-tuple-element.45.near_ref, f32[3,3,4096]{2,1,0:T(4,128)S(1)} %get-tuple-element.36.taps_ref, ...), custom_call_target="tpu_custom_call" | custom-call | flops 1 | bytes 1 | tf_op jit(solution)/shard_map/pallas_call | solution.py:328
  18.5 0.0 copy-start.1
  18.5 1.7 %shard_map.104 = (f32[128,2176]{1,0:T(8,128)S(1)}, f32[128,2176]{1,0:T(8,128)S(1)}) custom-call(bf16[128,4096]{1,0:T(8,128)(2,1)S(1)} %copy-done, bf16[8,4096]{1,0:T(8,128)(2,1)S(1)} %get-tuple-element.44.head_ref, f32[8,4096]{1,0:T(8,128)S(1)} %get-tuple-element.45.near_ref, f32[3,3,4096]{2,1,0:T(4,128)S(1)} %get-tuple-element.36.taps_ref, ...), custom_call_target="tpu_custom_call" | custom-call | flops 1 | bytes 1 | tf_op jit(solution)/shard_map/pallas_call | solution.py:328
  20.2 0.0 collective-permute-done.1.middle_ref.refs_0_
  20.2 0.0 collective-permute-done.2.refs_1_.refs_2_
  20.2 1.9 %collective-permute-start.6 = (bf16[128,640]{1,0:T(8,128)(2,1)S(1)}, bf16[128,640]{1,0:T(8,128)(2,1)S(1)}, u32[]{:S(2)}, u32[]{:S(2)}) collective-permute-start(bf16[128,640]{1,0:T(8,128)(2,1)S(1)} %shard_map.108), channel_id=1, source_target_pairs={{0,2},{1,3},{2,4},{3,5},{4,6},{5,7},{6,8},{7,9},{8,10},{9,11},{10,... | collective-permute-start | bytes 491528 | tf_op jit(solution)/shard_map/ppermute | solution.py:307
  22.1 0.0 collective-permute-done.3.refs_2_
  22.1 0.0 copy-done.1
  22.1 1.9 %shard_map.106 = (bf16[128,4096]{1,0:T(8,128)(2,1)}, f32[40,1920]{1,0:T(8,128)S(1)}) custom-call(bf16[8,4096]{1,0:T(8,128)(2,1)S(1)} %collective-permute-done.1.middle_ref.refs_0_, f32[8,4096]{1,0:T(8,128)S(1)} %get-tuple-element.43.far_ref, f32[128,1920]{1,0:T(8,128)S(1)} %get-tuple-element.51.part_ref.refs_1_, f32[128,1920]{1,0:T(8,128)S(1)} %get-tuple-element.52.gate_ref, ...), custom_call_target="tpu_custom_call" | custom-call | flops 1 | bytes 1 | tf_op jit(solution)/shard_map/pallas_call | solution.py:328
  24.0 0.0 collective-permute-done.4.refs_2_
  24.0 0.8 %collective-permute-done.5.refs_3_ = bf16[128,768]{1,0:T(8,128)(2,1)S(1)} collective-permute-done((bf16[128,768]{1,0:T(8,128)(2,1)S(1)}, bf16[128,768]{1,0:T(8,128)(2,1)S(1)}, u32[]{:S(2)}, u32[]{:S(2)}) %collective-permute-start.5) | collective-permute-done | bytes 196640 | tf_op jit(solution)/shard_map/ppermute | solution.py:307
  24.8 1.5 %shard_map.107.refs_1_ = bf16[128,4096]{1,0:T(8,128)(2,1)} custom-call(bf16[8,4096]{1,0:T(8,128)(2,1)S(1)} %collective-permute-done.1.middle_ref.refs_0_, f32[8,4096]{1,0:T(8,128)S(1)} %get-tuple-element.43.far_ref, f32[128,2176]{1,0:T(8,128)S(1)} %get-tuple-element.49.refs_0_.part_ref, ...), custom_call_target="tpu_custom_call", output_to_operand_aliasing={{}: (6, {})} | custom-call | flops 1 | bytes 1 | tf_op jit(solution)/shard_map/pallas_call | solution.py:328
  26.3 2.6 %collective-permute-done.6.refs_2_ = bf16[128,640]{1,0:T(8,128)(2,1)S(1)} collective-permute-done((bf16[128,640]{1,0:T(8,128)(2,1)S(1)}, bf16[128,640]{1,0:T(8,128)(2,1)S(1)}, u32[]{:S(2)}, u32[]{:S(2)}) %collective-permute-start.6) | collective-permute-done | bytes 163872 | tf_op jit(solution)/shard_map/ppermute | solution.py:307
  28.9 1.1 %shard_map.109 = bf16[128,4096]{1,0:T(8,128)(2,1)} custom-call(bf16[8,4096]{1,0:T(8,128)(2,1)S(1)} %collective-permute-done.1.middle_ref.refs_0_, f32[8,4096]{1,0:T(8,128)S(1)} %get-tuple-element.43.far_ref, f32[128,2176]{1,0:T(8,128)S(1)} %get-tuple-element.49.refs_0_.part_ref, ...), custom_call_target="tpu_custom_call", output_to_operand_aliasing={{}: (6, {})} | custom-call | flops 1 | bytes 1 | tf_op jit(solution)/shard_map/pallas_call | solution.py:328
  (2 shorter events, 0.0 us)
Async XLA Ops:
  1.3 3.3 %copy-start.4 = (bf16[16,128]{1,0:T(8,128)(2,1)S(1)}, bf16[16,128]{1,0:T(8,128)(2,1)}, u32[]{:S(2)}) copy-start(bf16[16,128]{1,0:T(8,128)(2,1)} %constant.8.clone.moment_ref) | copy-start | bytes 12292
  1.3 18.8 %collective-permute-start.2 = (bf16[128,896]{1,0:T(8,128)(2,1)S(1)}, bf16[128,896]{1,0:T(8,128)(2,1)S(1)}, u32[]{:S(2)}, u32[]{:S(2)}) collective-permute-start(bf16[128,896]{1,0:T(8,128)(2,1)S(1)} %shard_map.100._.c1.refs_0_), channel_id=1, source_target_pairs={{0,2},{1,3},{2,4},{3,5},{4,6},{5,7},{6,8},{7,9},{8,10},{9,11},{10,... | collective-permute-start | bytes 688136 | tf_op jit(solution)/shard_map/ppermute | solution.py:307
  4.5 5.1 %collective-permute-start = (bf16[2,12288]{1,0:T(2,128)(2,1)S(1)}, bf16[2,12288]{1,0:T(2,128)(2,1)S(1)}, u32[]{:S(2)}, u32[]{:S(2)}) collective-permute-start(bf16[2,12288]{1,0:T(2,128)(2,1)S(1)} %get-tuple-element.35), channel_id=1, source_target_pairs={{0,1},{1,2},{2,3},{3,4},{4,5},{5,6},{6,7},{7,8},{8,9},{9,10},{10,1... | collective-permute-start | bytes 147464 | tf_op jit(solution)/shard_map/ppermute | solution.py:307
  4.6 17.6 %collective-permute-start.3 = (bf16[128,1024]{1,0:T(8,128)(2,1)S(1)}, bf16[128,1024]{1,0:T(8,128)(2,1)S(1)}, u32[]{:S(2)}, u32[]{:S(2)}) collective-permute-start(bf16[128,1024]{1,0:T(8,128)(2,1)S(1)} %get-tuple-element.32.c2.refs_1_), channel_id=1, source_target_pairs={{0,2},{1,3},{2,4},{3,5},{4,6},{5,7},{6,8},{7,9},{8,10},{9,11},{10,... | collective-permute-start | bytes 786440 | tf_op jit(solution)/shard_map/ppermute | solution.py:307
  9.5 7.4 %copy-start = (bf16[128,4096]{1,0:T(8,128)(2,1)S(1)}, bf16[128,4096]{1,0:T(8,128)(2,1)}, u32[]{:S(2)}) copy-start(bf16[128,4096]{1,0:T(8,128)(2,1)} %query_ref.5) | copy-start | bytes 3145732
  9.5 7.4 %copy-start.2 = (bf16[128,1024]{1,0:T(8,128)(2,1)S(1)}, bf16[128,1024]{1,0:T(8,128)(2,1)}, u32[]{:S(2)}) copy-start(bf16[128,1024]{1,0:T(8,128)(2,1)} %constant.6.clone.table_ref) | copy-start | bytes 786436
  9.5 7.4 %copy-start.3 = (f32[4096]{0:T(1024)S(1)}, f32[4096]{0:T(1024)}, u32[]{:S(2)}) copy-start(f32[4096]{0:T(1024)} %param.16) | copy-start | bytes 49156
  11.0 9.2 %collective-permute-start.1 = (bf16[8,4096]{1,0:T(8,128)(2,1)S(1)}, bf16[8,4096]{1,0:T(8,128)(2,1)S(1)}, u32[]{:S(2)}, u32[]{:S(2)}) collective-permute-start(bf16[8,4096]{1,0:T(8,128)(2,1)S(1)} %get-tuple-element.42), channel_id=1, source_target_pairs={{0,1},{1,2},{2,3},{3,4},{4,5},{5,6},{6,7},{7,8},{8,9},{9,10},{10,1... | collective-permute-start | bytes 196616 | tf_op jit(solution)/shard_map/ppermute | solution.py:307
  11.1 13.0 %collective-permute-start.4 = (bf16[128,768]{1,0:T(8,128)(2,1)S(1)}, bf16[128,768]{1,0:T(8,128)(2,1)S(1)}, u32[]{:S(2)}, u32[]{:S(2)}) collective-permute-start(bf16[128,768]{1,0:T(8,128)(2,1)S(1)} %get-tuple-element.46.refs_0_), channel_id=1, source_target_pairs={{0,2},{1,3},{2,4},{3,5},{4,6},{5,7},{6,8},{7,9},{8,10},{9,11},{10,... | collective-permute-start | bytes 589832 | tf_op jit(solution)/shard_map/ppermute | solution.py:307
  11.7 13.1 %collective-permute-start.5 = (bf16[128,768]{1,0:T(8,128)(2,1)S(1)}, bf16[128,768]{1,0:T(8,128)(2,1)S(1)}, u32[]{:S(2)}, u32[]{:S(2)}) collective-permute-start(bf16[128,768]{1,0:T(8,128)(2,1)S(1)} %get-tuple-element.47.refs_1_), channel_id=1, source_target_pairs={{0,2},{1,3},{2,4},{3,5},{4,6},{5,7},{6,8},{7,9},{8,10},{9,11},{10,... | collective-permute-start | bytes 589832 | tf_op jit(solution)/shard_map/ppermute | solution.py:307
  18.5 3.7 %copy-start.1 = (bf16[128,1040]{1,0:T(8,128)(2,1)S(1)}, bf16[128,1040]{1,0:T(8,128)(2,1)}, u32[]{:S(2)}) copy-start(bf16[128,1040]{1,0:T(8,128)(2,1)} %constant.7.clone.table_ref) | copy-start | bytes 798724
  20.2 8.7 %collective-permute-start.6 = (bf16[128,640]{1,0:T(8,128)(2,1)S(1)}, bf16[128,640]{1,0:T(8,128)(2,1)S(1)}, u32[]{:S(2)}, u32[]{:S(2)}) collective-permute-start(bf16[128,640]{1,0:T(8,128)(2,1)S(1)} %shard_map.108), channel_id=1, source_target_pairs={{0,2},{1,3},{2,4},{3,5},{4,6},{5,7},{6,8},{7,9},{8,10},{9,11},{10,... | collective-permute-start | bytes 491528 | tf_op jit(solution)/shard_map/ppermute | solution.py:307

commit v4 on v3

--- a/solution.py
+++ b/solution.py
@@ -11,7 +11,8 @@
 from jax.sharding import PartitionSpec as P
 
 RATE_LOW, RATE_HIGH = 0.000390625, 0.03
-NODES = 8
+NODES = 7
+PADDED = 8
 LAST_TILE = 256
 
 
@@ -46,8 +47,9 @@
     lower = np.where(delta[None] >= 0, wrapped, 0.0)
     upper = np.where(delta[None] < 0, wrapped, 0.0)
     near = np.concatenate(list(lower), axis=1).astype(np.float32)
-    far = np.concatenate(list(upper) + [basis.T, np.zeros((rows, NODES))], axis=1).astype(np.float32)
-    moments = basis[:, ::-1].astype(np.float32)
+    far = np.concatenate(list(upper) + [basis.T, np.zeros((rows, 2 * PADDED - NODES))], axis=1).astype(np.float32)
+    moments = np.zeros((PADDED, rows), np.float32)
+    moments[:NODES] = basis[:, ::-1]
     high = moments.astype(jnp.bfloat16)
     low = (moments - high.astype(np.float32)).astype(jnp.bfloat16)
     last = [float(v) for v in basis[:, rows - 1]]
@@ -167,8 +169,9 @@
             far.append(jnp.sum(far_weights * decay, axis=0, keepdims=True))
             decay_ref[j * modes : (j + 1) * modes, c:d] = decay
             spread_ref[j * modes : (j + 1) * modes, c:d] = later * decay
-        near_ref[:, c:d] = jnp.concatenate(near, axis=0)
-        far_ref[:, c:d] = jnp.concatenate(far, axis=0) * keep
+        blank = [jnp.zeros((PADDED - NODES, d - c), jnp.float32)]
+        near_ref[:, c:d] = jnp.concatenate(near + blank, axis=0)
+        far_ref[:, c:d] = jnp.concatenate(far + blank, axis=0) * keep
         if c < late:
             part = c1[:, c:d] if c < early else c2[:, c - early : d - early]
             state_ref[:, c:d] = modal_state(moment_ref, part, decay_ref, c, d)
@@ -180,7 +183,7 @@
 
 def modal_state(moment_ref, mixed, decay_ref, c, d):
     halves = jnp.dot(moment_ref[...], mixed, preferred_element_type=jnp.float32)
-    moments = halves[:NODES] + halves[NODES:]
+    moments = halves[:PADDED] + halves[PADDED:]
     modes = decay_ref.shape[0] // NODES
     state = decay_ref[0:modes, c:d] * moments[0:1]
     for j in range(1, NODES):
@@ -228,6 +231,7 @@
                 jnp.sum(spread_ref[i * modes : (i + 1) * modes, c:d] * state, axis=0, keepdims=True)
                 for i in range(NODES)
             ]
+            middle.append(jnp.zeros((PADDED - NODES, d - c), jnp.float32))
             middle_ref[:, c:d] = jnp.concatenate(middle, axis=0).astype(middle_ref.dtype)
         offset = offset + chunk.shape[1]
 
@@ -273,7 +277,7 @@
                 stack_ref[j * rows : (j + 1) * rows, : b - a] = (back * far_ref[j : j + 1, c:d]).astype(stack_ref.dtype)
             middle = middle_ref[:, c:d].astype(jnp.float32) * keep
             middle = jnp.concatenate([middle, jnp.zeros_like(middle)], axis=0)
-            stack_ref[NODES * rows : NODES * rows + 2 * NODES, : b - a] = middle.astype(stack_ref.dtype)
+            stack_ref[NODES * rows : NODES * rows + 2 * PADDED, : b - a] = middle.astype(stack_ref.dtype)
             conv = jnp.dot(table_ref[...], stack_ref[:, : b - a], preferred_element_type=jnp.float32)
             total = part_ref[:, c - base : d - base] + conv
             gate = gate_ref[:, c - base : d - base]
@@ -373,7 +377,7 @@
     near, far, *states, key_v, value_v = call(
         functools.partial(prepare_kernel, times, rows),
         [hbm] * 2 + [vmem] * 5,
-        [((NODES, width), f32)] * 2
+        [((PADDED, width), f32)] * 2
         + [((modes, cuts[2]), f32)] * 3
         + [((NODES * modes, width), f32)] * 2
         + [((rows, width), bf16)] * 2,
@@ -384,7 +388,7 @@
     head, middle, *chunks = call(
         edge_kernel,
         [vmem] * 12,
-        [((8, width), bf16), ((NODES, width), bf16)] + [((rows, sizes[i]), bf16) for i in late],
+        [((8, width), bf16), ((PADDED, width), bf16)] + [((rows, sizes[i]), bf16) for i in late],
         (key_v, value_v, rims_in, taps_v, moment_table, c1, c2, *states),
     )
     middle_in = ring(middle, 1)

time: 30.2 us -> 30.1 us (level)
  Pallas kernels: 13.3 us -> 12.9 us
    pallas_call x10, Pallas kernels: 13.3 us -> 12.9 us  [call(): pl.pallas_call(body, in_specs=ins, out_specs=[o[2] if len(o) > 2 else vme...]
  transfers between devices with their start and end apart: 7 -> 7, of which waited for: 3 -> 3; matrix products, arithmetic and copies ran while one was open for 0% -> 0% of each run, Pallas kernels for 36% -> 35%
where the time goes in v4:
time: 30.1 us; the launch traced here: 29.8 us
  Pallas kernels  12.9 us (43%)
  starting transfers between devices  9.56 us (32%)
  waiting for transfers between devices  7.21 us (24%)
    pallas_call x10, Pallas kernels, call(): pl.pallas_call(body, in_specs=ins, out_specs=[o[2] if len(o) > 2 else vme...  12.9 us
    ppermute x7, starting transfers between devices, ring(): lax.ppermute(array, 'seq', [(i, (i + by) % length) for i in range(length)...  9.56 us
    ppermute x7, waiting for transfers between devices, ring(): lax.ppermute(array, 'seq', [(i, (i + by) % length) for i in range(length)...  7.21 us
  transfers between devices with their start and end apart: 7, of which 3 were waited for; matrix products, arithmetic and copies ran while one was open for 0% of the time, Pallas kernels for 35%

profile of v4, /device:TPU:24, one launch (start us, length us, event | category | flops | bytes accessed | tf_op | source)
XLA Modules:
  0.0 29.8 jit_solution(16922677694673141816)
XLA Ops:
  0.0 1.3 %shard_map.100._.c1.refs_0_ = bf16[128,896]{1,0:T(8,128)(2,1)S(1)} custom-call(bf16[128,4096]{1,0:T(8,128)(2,1)} %key_ref.5, bf16[128,4096]{1,0:T(8,128)(2,1)} %value_ref.5, f32[3,3,4096]{2,1,0:T(4,128)} %taps_ref.3), custom_call_target="tpu_custom_call" | custom-call | flops 1 | bytes 1 | tf_op jit(solution)/shard_map/pallas_call | solution.py:332
  1.3 1.6 %collective-permute-start.2 = (bf16[128,896]{1,0:T(8,128)(2,1)S(1)}, bf16[128,896]{1,0:T(8,128)(2,1)S(1)}, u32[]{:S(2)}, u32[]{:S(2)}) collective-permute-start(bf16[128,896]{1,0:T(8,128)(2,1)S(1)} %shard_map.100._.c1.refs_0_), channel_id=1, source_target_pairs={{0,2},{1,3},{2,4},{3,5},{4,6},{5,7},{6,8},{7,9},{8,10},{9,11},{10,... | collective-permute-start | bytes 688136 | tf_op jit(solution)/shard_map/ppermute | solution.py:311
  2.9 0.0 copy-start.4
  2.9 1.6 %shard_map.101 = (bf16[128,1024]{1,0:T(8,128)(2,1)S(1)}, bf16[2,12288]{1,0:T(2,128)(2,1)S(1)}, f32[3,3,4096]{2,1,0:T(4,128)S(1)}, f32[16,4096]{1,0:T(8,128)S(1)}, f32[16,4096]{1,0:T(8,128)S(1)}) custom-call(bf16[128,896]{1,0:T(8,128)(2,1)S(1)} %shard_map.100._.c1.refs_0_, bf16[128,4096]{1,0:T(8,128)(2,1)} %query_ref.5, bf16[128,4096]{1,0:T(8,128)(2,1)} %key_ref.5, ...), custom_call_target="tpu_custom_call" | custom-call | flops 1 | bytes 1 | tf_op jit(solution)/shard_map/pallas_call | solution.py:332
  4.5 0.1 collective-permute-start
  4.6 0.1 collective-permute-start.3
  4.6 0.0 copy-done.4
  4.6 1.3 %shard_map.102 = (f32[8,4096]{1,0:T(8,128)S(1)}, f32[8,4096]{1,0:T(8,128)S(1)}, f32[16,1920]{1,0:T(8,128)S(1)}, f32[16,1920]{1,0:T(8,128)S(1)}, f32[16,1920]{1,0...) custom-call(bf16[128,4096]{1,0:T(8,128)(2,1)} %key_ref.5, ...), custom_call_target="tpu_custom_call" | custom-call | flops 1 | bytes 1 | tf_op jit(solution)/shard_map/pallas_call | solution.py:332
  6.0 3.6 %collective-permute-done.rims_ref = bf16[2,12288]{1,0:T(2,128)(2,1)S(1)} collective-permute-done((bf16[2,12288]{1,0:T(2,128)(2,1)S(1)}, bf16[2,12288]{1,0:T(2,128)(2,1)S(1)}, u32[]{:S(2)}, u32[]{:S(2)}) %collective-permute-start) | collective-permute-done | bytes 49184 | tf_op jit(solution)/shard_map/ppermute | solution.py:311
  9.5 0.0 copy-start
  9.5 0.0 copy-start.2
  9.5 1.4 %shard_map.103 = (bf16[8,4096]{1,0:T(8,128)(2,1)S(1)}, bf16[8,4096]{1,0:T(8,128)(2,1)S(1)}, bf16[128,768]{1,0:T(8,128)(2,1)S(1)}, bf16[128,768]{1,0:T(8,128)(2,1)S(1)}, bf16[128,640]{1,0:T(8,128)(2,1)S(1)}) custom-call(bf16[128,4096]{1,0:T(8,128)(2,1)S(1)} %get-tuple-element.33.key_ref, bf16[128,4096]{1,0:T(8,128)(2,1)S(1)} %get-tuple-element.34.value_ref, ...), custom_call_target="tpu_custom_call" | custom-call | flops 1 | bytes 1 | tf_op jit(solution)/shard_map/pallas_call | solution.py:332
  10.9 0.1 collective-permute-start.1
  11.0 0.7 %collective-permute-start.4 = (bf16[128,768]{1,0:T(8,128)(2,1)S(1)}, bf16[128,768]{1,0:T(8,128)(2,1)S(1)}, u32[]{:S(2)}, u32[]{:S(2)}) collective-permute-start(bf16[128,768]{1,0:T(8,128)(2,1)S(1)} %get-tuple-element.46.refs_0_), channel_id=1, source_target_pairs={{0,2},{1,3},{2,4},{3,5},{4,6},{5,7},{6,8},{7,9},{8,10},{9,11},{10,... | collective-permute-start | bytes 589832 | tf_op jit(solution)/shard_map/ppermute | solution.py:311
  11.7 5.2 %collective-permute-start.5 = (bf16[128,768]{1,0:T(8,128)(2,1)S(1)}, bf16[128,768]{1,0:T(8,128)(2,1)S(1)}, u32[]{:S(2)}, u32[]{:S(2)}) collective-permute-start(bf16[128,768]{1,0:T(8,128)(2,1)S(1)} %get-tuple-element.47.refs_1_), channel_id=1, source_target_pairs={{0,2},{1,3},{2,4},{3,5},{4,6},{5,7},{6,8},{7,9},{8,10},{9,11},{10,... | collective-permute-start | bytes 589832 | tf_op jit(solution)/shard_map/ppermute | solution.py:311
  16.9 0.0 copy-done
  16.9 0.0 copy-done.2
  16.9 0.0 copy-done.3
  16.9 1.5 %shard_map.105 = (f32[128,1920]{1,0:T(8,128)S(1)}, f32[128,1920]{1,0:T(8,128)S(1)}) custom-call(bf16[128,4096]{1,0:T(8,128)(2,1)S(1)} %copy-done, bf16[8,4096]{1,0:T(8,128)(2,1)S(1)} %get-tuple-element.44.head_ref, f32[8,4096]{1,0:T(8,128)S(1)} %get-tuple-element.45.near_ref, f32[3,3,4096]{2,1,0:T(4,128)S(1)} %get-tuple-element.36.taps_ref, ...), custom_call_target="tpu_custom_call" | custom-call | flops 1 | bytes 1 | tf_op jit(solution)/shard_map/pallas_call | solution.py:332
  18.4 0.0 copy-start.1
  18.4 1.7 %shard_map.104 = (f32[128,2176]{1,0:T(8,128)S(1)}, f32[128,2176]{1,0:T(8,128)S(1)}) custom-call(bf16[128,4096]{1,0:T(8,128)(2,1)S(1)} %copy-done, bf16[8,4096]{1,0:T(8,128)(2,1)S(1)} %get-tuple-element.44.head_ref, f32[8,4096]{1,0:T(8,128)S(1)} %get-tuple-element.45.near_ref, f32[3,3,4096]{2,1,0:T(4,128)S(1)} %get-tuple-element.36.taps_ref, ...), custom_call_target="tpu_custom_call" | custom-call | flops 1 | bytes 1 | tf_op jit(solution)/shard_map/pallas_call | solution.py:332
  20.1 0.0 collective-permute-done.1.middle_ref.refs_0_
  20.1 0.0 collective-permute-done.2.refs_1_.refs_2_
  20.1 1.9 %collective-permute-start.6 = (bf16[128,640]{1,0:T(8,128)(2,1)S(1)}, bf16[128,640]{1,0:T(8,128)(2,1)S(1)}, u32[]{:S(2)}, u32[]{:S(2)}) collective-permute-start(bf16[128,640]{1,0:T(8,128)(2,1)S(1)} %shard_map.108), channel_id=1, source_target_pairs={{0,2},{1,3},{2,4},{3,5},{4,6},{5,7},{6,8},{7,9},{8,10},{9,11},{10,... | collective-permute-start | bytes 491528 | tf_op jit(solution)/shard_map/ppermute | solution.py:311
  22.0 0.0 collective-permute-done.3.refs_2_
  22.0 0.0 copy-done.1
  22.0 1.7 %shard_map.106 = (bf16[128,4096]{1,0:T(8,128)(2,1)}, f32[40,1920]{1,0:T(8,128)S(1)}) custom-call(bf16[8,4096]{1,0:T(8,128)(2,1)S(1)} %collective-permute-done.1.middle_ref.refs_0_, f32[8,4096]{1,0:T(8,128)S(1)} %get-tuple-element.43.far_ref, f32[128,1920]{1,0:T(8,128)S(1)} %get-tuple-element.51.part_ref.refs_1_, f32[128,1920]{1,0:T(8,128)S(1)} %get-tuple-element.52.gate_ref, ...), custom_call_target="tpu_custom_call" | custom-call | flops 1 | bytes 1 | tf_op jit(solution)/shard_map/pallas_call | solution.py:332
  23.7 0.0 collective-permute-done.4.refs_2_
  23.7 1.1 %collective-permute-done.5.refs_3_ = bf16[128,768]{1,0:T(8,128)(2,1)S(1)} collective-permute-done((bf16[128,768]{1,0:T(8,128)(2,1)S(1)}, bf16[128,768]{1,0:T(8,128)(2,1)S(1)}, u32[]{:S(2)}, u32[]{:S(2)}) %collective-permute-start.5) | collective-permute-done | bytes 196640 | tf_op jit(solution)/shard_map/ppermute | solution.py:311
  24.8 1.4 %shard_map.107.refs_1_ = bf16[128,4096]{1,0:T(8,128)(2,1)} custom-call(bf16[8,4096]{1,0:T(8,128)(2,1)S(1)} %collective-permute-done.1.middle_ref.refs_0_, f32[8,4096]{1,0:T(8,128)S(1)} %get-tuple-element.43.far_ref, f32[128,2176]{1,0:T(8,128)S(1)} %get-tuple-element.49.refs_0_.part_ref, ...), custom_call_target="tpu_custom_call", output_to_operand_aliasing={{}: (6, {})} | custom-call | flops 1 | bytes 1 | tf_op jit(solution)/shard_map/pallas_call | solution.py:332
  26.2 2.6 %collective-permute-done.6.refs_2_ = bf16[128,640]{1,0:T(8,128)(2,1)S(1)} collective-permute-done((bf16[128,640]{1,0:T(8,128)(2,1)S(1)}, bf16[128,640]{1,0:T(8,128)(2,1)S(1)}, u32[]{:S(2)}, u32[]{:S(2)}) %collective-permute-start.6) | collective-permute-done | bytes 163872 | tf_op jit(solution)/shard_map/ppermute | solution.py:311
  28.8 1.1 %shard_map.109 = bf16[128,4096]{1,0:T(8,128)(2,1)} custom-call(bf16[8,4096]{1,0:T(8,128)(2,1)S(1)} %collective-permute-done.1.middle_ref.refs_0_, f32[8,4096]{1,0:T(8,128)S(1)} %get-tuple-element.43.far_ref, f32[128,2176]{1,0:T(8,128)S(1)} %get-tuple-element.49.refs_0_.part_ref, ...), custom_call_target="tpu_custom_call", output_to_operand_aliasing={{}: (6, {})} | custom-call | flops 1 | bytes 1 | tf_op jit(solution)/shard_map/pallas_call | solution.py:332
  (2 shorter events, 0.0 us)
Async XLA Ops:
  1.3 18.7 %collective-permute-start.2 = (bf16[128,896]{1,0:T(8,128)(2,1)S(1)}, bf16[128,896]{1,0:T(8,128)(2,1)S(1)}, u32[]{:S(2)}, u32[]{:S(2)}) collective-permute-start(bf16[128,896]{1,0:T(8,128)(2,1)S(1)} %shard_map.100._.c1.refs_0_), channel_id=1, source_target_pairs={{0,2},{1,3},{2,4},{3,5},{4,6},{5,7},{6,8},{7,9},{8,10},{9,11},{10,... | collective-permute-start | bytes 688136 | tf_op jit(solution)/shard_map/ppermute | solution.py:311
  2.9 1.7 %copy-start.4 = (bf16[16,128]{1,0:T(8,128)(2,1)S(1)}, bf16[16,128]{1,0:T(8,128)(2,1)}, u32[]{:S(2)}) copy-start(bf16[16,128]{1,0:T(8,128)(2,1)} %constant.8.clone.moment_ref) | copy-start | bytes 12292
  4.5 5.0 %collective-permute-start = (bf16[2,12288]{1,0:T(2,128)(2,1)S(1)}, bf16[2,12288]{1,0:T(2,128)(2,1)S(1)}, u32[]{:S(2)}, u32[]{:S(2)}) collective-permute-start(bf16[2,12288]{1,0:T(2,128)(2,1)S(1)} %get-tuple-element.35), channel_id=1, source_target_pairs={{0,1},{1,2},{2,3},{3,4},{4,5},{5,6},{6,7},{7,8},{8,9},{9,10},{10,1... | collective-permute-start | bytes 147464 | tf_op jit(solution)/shard_map/ppermute | solution.py:311
  4.6 17.5 %collective-permute-start.3 = (bf16[128,1024]{1,0:T(8,128)(2,1)S(1)}, bf16[128,1024]{1,0:T(8,128)(2,1)S(1)}, u32[]{:S(2)}, u32[]{:S(2)}) collective-permute-start(bf16[128,1024]{1,0:T(8,128)(2,1)S(1)} %get-tuple-element.32.c2.refs_1_), channel_id=1, source_target_pairs={{0,2},{1,3},{2,4},{3,5},{4,6},{5,7},{6,8},{7,9},{8,10},{9,11},{10,... | collective-permute-start | bytes 786440 | tf_op jit(solution)/shard_map/ppermute | solution.py:311
  9.5 7.3 %copy-start = (bf16[128,4096]{1,0:T(8,128)(2,1)S(1)}, bf16[128,4096]{1,0:T(8,128)(2,1)}, u32[]{:S(2)}) copy-start(bf16[128,4096]{1,0:T(8,128)(2,1)} %query_ref.5) | copy-start | bytes 3145732
  9.5 7.3 %copy-start.2 = (bf16[128,896]{1,0:T(8,128)(2,1)S(1)}, bf16[128,896]{1,0:T(8,128)(2,1)}, u32[]{:S(2)}) copy-start(bf16[128,896]{1,0:T(8,128)(2,1)} %constant.6.clone.table_ref) | copy-start | bytes 688132
  9.5 7.4 %copy-start.3 = (f32[4096]{0:T(1024)S(1)}, f32[4096]{0:T(1024)}, u32[]{:S(2)}) copy-start(f32[4096]{0:T(1024)} %param.16) | copy-start | bytes 49156
  10.9 9.1 %collective-permute-start.1 = (bf16[8,4096]{1,0:T(8,128)(2,1)S(1)}, bf16[8,4096]{1,0:T(8,128)(2,1)S(1)}, u32[]{:S(2)}, u32[]{:S(2)}) collective-permute-start(bf16[8,4096]{1,0:T(8,128)(2,1)S(1)} %get-tuple-element.42), channel_id=1, source_target_pairs={{0,1},{1,2},{2,3},{3,4},{4,5},{5,6},{6,7},{7,8},{8,9},{9,10},{10,1... | collective-permute-start | bytes 196616 | tf_op jit(solution)/shard_map/ppermute | solution.py:311
  11.0 12.7 %collective-permute-start.4 = (bf16[128,768]{1,0:T(8,128)(2,1)S(1)}, bf16[128,768]{1,0:T(8,128)(2,1)S(1)}, u32[]{:S(2)}, u32[]{:S(2)}) collective-permute-start(bf16[128,768]{1,0:T(8,128)(2,1)S(1)} %get-tuple-element.46.refs_0_), channel_id=1, source_target_pairs={{0,2},{1,3},{2,4},{3,5},{4,6},{5,7},{6,8},{7,9},{8,10},{9,11},{10,... | collective-permute-start | bytes 589832 | tf_op jit(solution)/shard_map/ppermute | solution.py:311
  11.7 13.2 %collective-permute-start.5 = (bf16[128,768]{1,0:T(8,128)(2,1)S(1)}, bf16[128,768]{1,0:T(8,128)(2,1)S(1)}, u32[]{:S(2)}, u32[]{:S(2)}) collective-permute-start(bf16[128,768]{1,0:T(8,128)(2,1)S(1)} %get-tuple-element.47.refs_1_), channel_id=1, source_target_pairs={{0,2},{1,3},{2,4},{3,5},{4,6},{5,7},{6,8},{7,9},{8,10},{9,11},{10,... | collective-permute-start | bytes 589832 | tf_op jit(solution)/shard_map/ppermute | solution.py:311
  18.4 3.6 %copy-start.1 = (bf16[128,912]{1,0:T(8,128)(2,1)S(1)}, bf16[128,912]{1,0:T(8,128)(2,1)}, u32[]{:S(2)}) copy-start(bf16[128,912]{1,0:T(8,128)(2,1)} %constant.7.clone.table_ref) | copy-start | bytes 700420
  20.1 8.7 %collective-permute-start.6 = (bf16[128,640]{1,0:T(8,128)(2,1)S(1)}, bf16[128,640]{1,0:T(8,128)(2,1)S(1)}, u32[]{:S(2)}, u32[]{:S(2)}) collective-permute-start(bf16[128,640]{1,0:T(8,128)(2,1)S(1)} %shard_map.108), channel_id=1, source_target_pairs={{0,2},{1,3},{2,4},{3,5},{4,6},{5,7},{6,8},{7,9},{8,10},{9,11},{10,... | collective-permute-start | bytes 491528 | tf_op jit(solution)/shard_map/ppermute | solution.py:311

commit v5 on v4

--- a/solution.py
+++ b/solution.py
@@ -415,7 +415,7 @@
         input_output_aliases={3: 0},
     )
     back[-1] = ring(final, 2, closed=False)
-    late_own = own(2, count_chunks, chunks)
+    late_own = own(2, count_chunks, [*chunks[:-1], final])
 
     def finish(first, stop, out, pre):
         some = range(first, stop)

time: 30.1 us -> 29.9 us (level)
  waiting for transfers between devices: 7.21 us -> 6.63 us
    ppermute x7, waiting for transfers between devices: 7.21 us -> 6.63 us  [ring(): lax.ppermute(array, 'seq', [(i, (i + by) % length) for i in range(length)...]
  transfers between devices with their start and end apart: 7 -> 7, of which waited for: 3 -> 3; matrix products, arithmetic and copies ran while one was open for 0% -> 0% of each run, Pallas kernels for 35% -> 36%
where the time goes in v5:
time: 29.9 us; the launch traced here: 29.5 us
  Pallas kernels  13 us (43%)
  starting transfers between devices  9.69 us (32%)
  waiting for transfers between devices  6.63 us (22%)
    pallas_call x10, Pallas kernels, call(): pl.pallas_call(body, in_specs=ins, out_specs=[o[2] if len(o) > 2 else vme...  13 us
    ppermute x7, starting transfers between devices, ring(): lax.ppermute(array, 'seq', [(i, (i + by) % length) for i in range(length)...  9.69 us
    ppermute x7, waiting for transfers between devices, ring(): lax.ppermute(array, 'seq', [(i, (i + by) % length) for i in range(length)...  6.63 us
  transfers between devices with their start and end apart: 7, of which 3 were waited for; matrix products, arithmetic and copies ran while one was open for 0% of the time, Pallas kernels for 36%

profile of v5, /device:TPU:24, one launch (start us, length us, event | category | flops | bytes accessed | tf_op | source)
XLA Modules:
  0.0 29.5 jit_solution(16614777378465228477)
XLA Ops:
  0.0 1.3 %shard_map.100._.c1.refs_0_ = bf16[128,896]{1,0:T(8,128)(2,1)S(1)} custom-call(bf16[128,4096]{1,0:T(8,128)(2,1)} %key_ref.5, bf16[128,4096]{1,0:T(8,128)(2,1)} %value_ref.5, f32[3,3,4096]{2,1,0:T(4,128)} %taps_ref.3), custom_call_target="tpu_custom_call" | custom-call | flops 1 | bytes 1 | tf_op jit(solution)/shard_map/pallas_call | solution.py:332
  1.3 1.6 %collective-permute-start.2 = (bf16[128,896]{1,0:T(8,128)(2,1)S(1)}, bf16[128,896]{1,0:T(8,128)(2,1)S(1)}, u32[]{:S(2)}, u32[]{:S(2)}) collective-permute-start(bf16[128,896]{1,0:T(8,128)(2,1)S(1)} %shard_map.100._.c1.refs_0_), channel_id=1, source_target_pairs={{0,2},{1,3},{2,4},{3,5},{4,6},{5,7},{6,8},{7,9},{8,10},{9,11},{10,... | collective-permute-start | bytes 688136 | tf_op jit(solution)/shard_map/ppermute | solution.py:311
  2.9 0.0 copy-start.4
  2.9 1.6 %shard_map.101 = (bf16[128,1024]{1,0:T(8,128)(2,1)S(1)}, bf16[2,12288]{1,0:T(2,128)(2,1)S(1)}, f32[3,3,4096]{2,1,0:T(4,128)S(1)}, f32[16,4096]{1,0:T(8,128)S(1)}, f32[16,4096]{1,0:T(8,128)S(1)}) custom-call(bf16[128,896]{1,0:T(8,128)(2,1)S(1)} %shard_map.100._.c1.refs_0_, bf16[128,4096]{1,0:T(8,128)(2,1)} %query_ref.5, bf16[128,4096]{1,0:T(8,128)(2,1)} %key_ref.5, ...), custom_call_target="tpu_custom_call" | custom-call | flops 1 | bytes 1 | tf_op jit(solution)/shard_map/pallas_call | solution.py:332
  4.5 0.1 collective-permute-start
  4.6 0.1 collective-permute-start.3
  4.6 0.0 copy-done.4
  4.6 1.3 %shard_map.102 = (f32[8,4096]{1,0:T(8,128)S(1)}, f32[8,4096]{1,0:T(8,128)S(1)}, f32[16,1920]{1,0:T(8,128)S(1)}, f32[16,1920]{1,0:T(8,128)S(1)}, f32[16,1920]{1,0...) custom-call(bf16[128,4096]{1,0:T(8,128)(2,1)} %key_ref.5, ...), custom_call_target="tpu_custom_call" | custom-call | flops 1 | bytes 1 | tf_op jit(solution)/shard_map/pallas_call | solution.py:332
  6.0 3.6 %collective-permute-done.rims_ref = bf16[2,12288]{1,0:T(2,128)(2,1)S(1)} collective-permute-done((bf16[2,12288]{1,0:T(2,128)(2,1)S(1)}, bf16[2,12288]{1,0:T(2,128)(2,1)S(1)}, u32[]{:S(2)}, u32[]{:S(2)}) %collective-permute-start) | collective-permute-done | bytes 49184 | tf_op jit(solution)/shard_map/ppermute | solution.py:311
  9.5 0.0 copy-start
  9.5 0.0 copy-start.2
  9.5 1.4 %shard_map.103 = (bf16[8,4096]{1,0:T(8,128)(2,1)S(1)}, bf16[8,4096]{1,0:T(8,128)(2,1)S(1)}, bf16[128,768]{1,0:T(8,128)(2,1)S(1)}, bf16[128,768]{1,0:T(8,128)(2,1)S(1)}, bf16[128,640]{1,0:T(8,128)(2,1)S(1)}) custom-call(bf16[128,4096]{1,0:T(8,128)(2,1)S(1)} %get-tuple-element.33.key_ref, bf16[128,4096]{1,0:T(8,128)(2,1)S(1)} %get-tuple-element.34.value_ref, ...), custom_call_target="tpu_custom_call" | custom-call | flops 1 | bytes 1 | tf_op jit(solution)/shard_map/pallas_call | solution.py:332
  10.9 0.1 collective-permute-start.1
  11.0 0.7 %collective-permute-start.4 = (bf16[128,768]{1,0:T(8,128)(2,1)S(1)}, bf16[128,768]{1,0:T(8,128)(2,1)S(1)}, u32[]{:S(2)}, u32[]{:S(2)}) collective-permute-start(bf16[128,768]{1,0:T(8,128)(2,1)S(1)} %get-tuple-element.46.refs_0_), channel_id=1, source_target_pairs={{0,2},{1,3},{2,4},{3,5},{4,6},{5,7},{6,8},{7,9},{8,10},{9,11},{10,... | collective-permute-start | bytes 589832 | tf_op jit(solution)/shard_map/ppermute | solution.py:311
  11.7 5.2 %collective-permute-start.5 = (bf16[128,768]{1,0:T(8,128)(2,1)S(1)}, bf16[128,768]{1,0:T(8,128)(2,1)S(1)}, u32[]{:S(2)}, u32[]{:S(2)}) collective-permute-start(bf16[128,768]{1,0:T(8,128)(2,1)S(1)} %get-tuple-element.47.refs_1_), channel_id=1, source_target_pairs={{0,2},{1,3},{2,4},{3,5},{4,6},{5,7},{6,8},{7,9},{8,10},{9,11},{10,... | collective-permute-start | bytes 589832 | tf_op jit(solution)/shard_map/ppermute | solution.py:311
  16.9 0.0 copy-done
  16.9 0.0 copy-done.2
  16.9 0.0 copy-done.3
  16.9 1.5 %shard_map.104 = (f32[128,1920]{1,0:T(8,128)S(1)}, f32[128,1920]{1,0:T(8,128)S(1)}) custom-call(bf16[128,4096]{1,0:T(8,128)(2,1)S(1)} %copy-done, bf16[8,4096]{1,0:T(8,128)(2,1)S(1)} %get-tuple-element.44.head_ref, f32[8,4096]{1,0:T(8,128)S(1)} %get-tuple-element.45.near_ref, f32[3,3,4096]{2,1,0:T(4,128)S(1)} %get-tuple-element.36.taps_ref, ...), custom_call_target="tpu_custom_call" | custom-call | flops 1 | bytes 1 | tf_op jit(solution)/shard_map/pallas_call | solution.py:332
  18.4 0.0 collective-permute-done.1.refs_0_.middle_ref
  18.4 0.0 collective-permute-done.2.refs_2_.refs_1_
  18.4 0.0 copy-start.1
  18.4 2.1 %collective-permute-start.6 = (bf16[128,640]{1,0:T(8,128)(2,1)S(1)}, bf16[128,640]{1,0:T(8,128)(2,1)S(1)}, u32[]{:S(2)}, u32[]{:S(2)}) collective-permute-start(bf16[128,640]{1,0:T(8,128)(2,1)S(1)} %shard_map.105.refs_2_), channel_id=1, source_target_pairs={{0,2},{1,3},{2,4},{3,5},{4,6},{5,7},{6,8},{7,9},{8,10},{9,11},{10,... | collective-permute-start | bytes 491528 | tf_op jit(solution)/shard_map/ppermute | solution.py:311
  20.5 1.7 %shard_map.106 = (f32[128,2176]{1,0:T(8,128)S(1)}, f32[128,2176]{1,0:T(8,128)S(1)}) custom-call(bf16[128,4096]{1,0:T(8,128)(2,1)S(1)} %copy-done, bf16[8,4096]{1,0:T(8,128)(2,1)S(1)} %get-tuple-element.44.head_ref, f32[8,4096]{1,0:T(8,128)S(1)} %get-tuple-element.45.near_ref, f32[3,3,4096]{2,1,0:T(4,128)S(1)} %get-tuple-element.36.taps_ref, ...), custom_call_target="tpu_custom_call" | custom-call | flops 1 | bytes 1 | tf_op jit(solution)/shard_map/pallas_call | solution.py:332
  22.2 0.0 collective-permute-done.3.refs_2_
  22.2 0.0 copy-done.1
  22.2 1.7 %shard_map.107 = (bf16[128,4096]{1,0:T(8,128)(2,1)}, f32[40,1920]{1,0:T(8,128)S(1)}) custom-call(bf16[8,4096]{1,0:T(8,128)(2,1)S(1)} %collective-permute-done.1.refs_0_.middle_ref, f32[8,4096]{1,0:T(8,128)S(1)} %get-tuple-element.43.far_ref, f32[128,1920]{1,0:T(8,128)S(1)} %get-tuple-element.48.refs_1_.part_ref, f32[128,1920]{1,0:T(8,128)S(1)} %get-tuple-element.52.gate_ref, ...), custom_call_target="tpu_custom_call" | custom-call | flops 1 | bytes 1 | tf_op jit(solution)/shard_map/pallas_call | solution.py:332
  23.9 0.0 collective-permute-done.4.refs_2_
  23.9 0.9 %collective-permute-done.5.refs_3_ = bf16[128,768]{1,0:T(8,128)(2,1)S(1)} collective-permute-done((bf16[128,768]{1,0:T(8,128)(2,1)S(1)}, bf16[128,768]{1,0:T(8,128)(2,1)S(1)}, u32[]{:S(2)}, u32[]{:S(2)}) %collective-permute-start.5) | collective-permute-done | bytes 196640 | tf_op jit(solution)/shard_map/ppermute | solution.py:311
  24.8 1.4 %shard_map.108.refs_1_ = bf16[128,4096]{1,0:T(8,128)(2,1)} custom-call(bf16[8,4096]{1,0:T(8,128)(2,1)S(1)} %collective-permute-done.1.refs_0_.middle_ref, f32[8,4096]{1,0:T(8,128)S(1)} %get-tuple-element.43.far_ref, f32[128,2176]{1,0:T(8,128)S(1)} %get-tuple-element.50.refs_0_.part_ref, ...), custom_call_target="tpu_custom_call", output_to_operand_aliasing={{}: (6, {})} | custom-call | flops 1 | bytes 1 | tf_op jit(solution)/shard_map/pallas_call | solution.py:332
  26.2 2.2 %collective-permute-done.6.refs_2_ = bf16[128,640]{1,0:T(8,128)(2,1)S(1)} collective-permute-done((bf16[128,640]{1,0:T(8,128)(2,1)S(1)}, bf16[128,640]{1,0:T(8,128)(2,1)S(1)}, u32[]{:S(2)}, u32[]{:S(2)}) %collective-permute-start.6) | collective-permute-done | bytes 163872 | tf_op jit(solution)/shard_map/ppermute | solution.py:311
  28.4 1.1 %shard_map.109 = bf16[128,4096]{1,0:T(8,128)(2,1)} custom-call(bf16[8,4096]{1,0:T(8,128)(2,1)S(1)} %collective-permute-done.1.refs_0_.middle_ref, f32[8,4096]{1,0:T(8,128)S(1)} %get-tuple-element.43.far_ref, f32[128,2176]{1,0:T(8,128)S(1)} %get-tuple-element.50.refs_0_.part_ref, ...), custom_call_target="tpu_custom_call", output_to_operand_aliasing={{}: (6, {})} | custom-call | flops 1 | bytes 1 | tf_op jit(solution)/shard_map/pallas_call | solution.py:332
  (2 shorter events, 0.0 us)
Async XLA Ops:
  1.3 17.1 %collective-permute-start.2 = (bf16[128,896]{1,0:T(8,128)(2,1)S(1)}, bf16[128,896]{1,0:T(8,128)(2,1)S(1)}, u32[]{:S(2)}, u32[]{:S(2)}) collective-permute-start(bf16[128,896]{1,0:T(8,128)(2,1)S(1)} %shard_map.100._.c1.refs_0_), channel_id=1, source_target_pairs={{0,2},{1,3},{2,4},{3,5},{4,6},{5,7},{6,8},{7,9},{8,10},{9,11},{10,... | collective-permute-start | bytes 688136 | tf_op jit(solution)/shard_map/ppermute | solution.py:311
  2.9 1.7 %copy-start.4 = (bf16[16,128]{1,0:T(8,128)(2,1)S(1)}, bf16[16,128]{1,0:T(8,128)(2,1)}, u32[]{:S(2)}) copy-start(bf16[16,128]{1,0:T(8,128)(2,1)} %constant.8.clone.moment_ref) | copy-start | bytes 12292
  4.5 5.0 %collective-permute-start = (bf16[2,12288]{1,0:T(2,128)(2,1)S(1)}, bf16[2,12288]{1,0:T(2,128)(2,1)S(1)}, u32[]{:S(2)}, u32[]{:S(2)}) collective-permute-start(bf16[2,12288]{1,0:T(2,128)(2,1)S(1)} %get-tuple-element.35), channel_id=1, source_target_pairs={{0,1},{1,2},{2,3},{3,4},{4,5},{5,6},{6,7},{7,8},{8,9},{9,10},{10,1... | collective-permute-start | bytes 147464 | tf_op jit(solution)/shard_map/ppermute | solution.py:311
  4.6 17.6 %collective-permute-start.3 = (bf16[128,1024]{1,0:T(8,128)(2,1)S(1)}, bf16[128,1024]{1,0:T(8,128)(2,1)S(1)}, u32[]{:S(2)}, u32[]{:S(2)}) collective-permute-start(bf16[128,1024]{1,0:T(8,128)(2,1)S(1)} %get-tuple-element.32.c2.refs_1_), channel_id=1, source_target_pairs={{0,2},{1,3},{2,4},{3,5},{4,6},{5,7},{6,8},{7,9},{8,10},{9,11},{10,... | collective-permute-start | bytes 786440 | tf_op jit(solution)/shard_map/ppermute | solution.py:311
  9.5 7.3 %copy-start = (bf16[128,4096]{1,0:T(8,128)(2,1)S(1)}, bf16[128,4096]{1,0:T(8,128)(2,1)}, u32[]{:S(2)}) copy-start(bf16[128,4096]{1,0:T(8,128)(2,1)} %query_ref.5) | copy-start | bytes 3145732
  9.5 7.4 %copy-start.2 = (bf16[128,896]{1,0:T(8,128)(2,1)S(1)}, bf16[128,896]{1,0:T(8,128)(2,1)}, u32[]{:S(2)}) copy-start(bf16[128,896]{1,0:T(8,128)(2,1)} %constant.6.clone.table_ref) | copy-start | bytes 688132
  9.5 7.4 %copy-start.3 = (f32[4096]{0:T(1024)S(1)}, f32[4096]{0:T(1024)}, u32[]{:S(2)}) copy-start(f32[4096]{0:T(1024)} %param.16) | copy-start | bytes 49156
  10.9 7.5 %collective-permute-start.1 = (bf16[8,4096]{1,0:T(8,128)(2,1)S(1)}, bf16[8,4096]{1,0:T(8,128)(2,1)S(1)}, u32[]{:S(2)}, u32[]{:S(2)}) collective-permute-start(bf16[8,4096]{1,0:T(8,128)(2,1)S(1)} %get-tuple-element.42), channel_id=1, source_target_pairs={{0,1},{1,2},{2,3},{3,4},{4,5},{5,6},{6,7},{7,8},{8,9},{9,10},{10,1... | collective-permute-start | bytes 196616 | tf_op jit(solution)/shard_map/ppermute | solution.py:311
  11.0 12.9 %collective-permute-start.4 = (bf16[128,768]{1,0:T(8,128)(2,1)S(1)}, bf16[128,768]{1,0:T(8,128)(2,1)S(1)}, u32[]{:S(2)}, u32[]{:S(2)}) collective-permute-start(bf16[128,768]{1,0:T(8,128)(2,1)S(1)} %get-tuple-element.46.refs_0_), channel_id=1, source_target_pairs={{0,2},{1,3},{2,4},{3,5},{4,6},{5,7},{6,8},{7,9},{8,10},{9,11},{10,... | collective-permute-start | bytes 589832 | tf_op jit(solution)/shard_map/ppermute | solution.py:311
  11.7 13.2 %collective-permute-start.5 = (bf16[128,768]{1,0:T(8,128)(2,1)S(1)}, bf16[128,768]{1,0:T(8,128)(2,1)S(1)}, u32[]{:S(2)}, u32[]{:S(2)}) collective-permute-start(bf16[128,768]{1,0:T(8,128)(2,1)S(1)} %get-tuple-element.47.refs_1_), channel_id=1, source_target_pairs={{0,2},{1,3},{2,4},{3,5},{4,6},{5,7},{6,8},{7,9},{8,10},{9,11},{10,... | collective-permute-start | bytes 589832 | tf_op jit(solution)/shard_map/ppermute | solution.py:311
  18.4 3.8 %copy-start.1 = (bf16[128,912]{1,0:T(8,128)(2,1)S(1)}, bf16[128,912]{1,0:T(8,128)(2,1)}, u32[]{:S(2)}) copy-start(bf16[128,912]{1,0:T(8,128)(2,1)} %constant.7.clone.table_ref) | copy-start | bytes 700420
  18.4 10.0 %collective-permute-start.6 = (bf16[128,640]{1,0:T(8,128)(2,1)S(1)}, bf16[128,640]{1,0:T(8,128)(2,1)S(1)}, u32[]{:S(2)}, u32[]{:S(2)}) collective-permute-start(bf16[128,640]{1,0:T(8,128)(2,1)S(1)} %shard_map.105.refs_2_), channel_id=1, source_target_pairs={{0,2},{1,3},{2,4},{3,5},{4,6},{5,7},{6,8},{7,9},{8,10},{9,11},{10,... | collective-permute-start | bytes 491528 | tf_op jit(solution)/shard_map/ppermute | solution.py:311

commit v6 on v5

--- a/solution.py
+++ b/solution.py
@@ -141,16 +141,11 @@
         rims_ref[:, n * whole : (n + 1) * whole] = held[n][8 - edge :]
 
 
-def pass_kernel(*refs):
-    del refs
-
-
 def prepare_kernel(
     times, rows, key_ref, value_ref, residue_ref, rate_ref, moment_ref, c1, c2, near_ref, far_ref, state_ref, first_ref,
     second_ref, decay_ref, spread_ref, key_vmem, value_vmem, sems,
 ):
     modes, width = rate_ref.shape
-    keep = (lax.axis_index("seq") >= 2).astype(jnp.float32)
     early, late = c1.shape[1], state_ref.shape[1]
     copies = []
     for ref, vmem in ((key_ref, key_vmem), (value_ref, value_vmem)):
@@ -171,7 +166,7 @@
             spread_ref[j * modes : (j + 1) * modes, c:d] = later * decay
         blank = [jnp.zeros((PADDED - NODES, d - c), jnp.float32)]
         near_ref[:, c:d] = jnp.concatenate(near + blank, axis=0)
-        far_ref[:, c:d] = jnp.concatenate(far + blank, axis=0) * keep
+        far_ref[:, c:d] = jnp.concatenate(far + blank, axis=0)
         if c < late:
             part = c1[:, c:d] if c < early else c2[:, c - early : d - early]
             state_ref[:, c:d] = modal_state(moment_ref, part, decay_ref, c, d)
@@ -218,7 +213,7 @@
                 head = mixed[:8]
                 state = modal_state(moment_ref, mixed, decay_ref, c, d)
                 slot = c - early
-                if slot < early:
+                if slot < early and chunk is not late[-1]:
                     second = head_ref[:, slot : slot + b - a].astype(jnp.float32)[1:2]
                     whole = (kf * vf)[:16]
                     row = lax.broadcasted_iota(jnp.int32, whole.shape, 0)
@@ -236,8 +231,10 @@
         offset = offset + chunk.shape[1]
 
 
-def own_kernel(edge, start, query_ref, head_ref, near_ref, taps_ref, rims_ref, skip_ref, table_ref, *refs):
+def own_kernel(edge, start, complete, query_ref, head_ref, near_ref, taps_ref, rims_ref, skip_ref, table_ref, *refs):
     *chunks, part_ref, gate_ref, stack_ref = refs
+    if complete:
+        middle_ref, far_table_ref, *chunks = chunks
     rows, _ = query_ref.shape
     keep = (lax.axis_index("seq") >= 1).astype(jnp.float32)
     offset = start
@@ -249,14 +246,76 @@
             for j in range(NODES):
                 stack_ref[j * rows : (j + 1) * rows, : b - a] = (mixed * near_ref[j : j + 1, c:d]).astype(stack_ref.dtype)
             conv = jnp.dot(table_ref[...], stack_ref[:, : b - a], preferred_element_type=jnp.float32)
+            if complete and chunk is chunks[-1]:
+                middle = middle_ref[:, c:d].astype(jnp.float32) * keep
+                middle = jnp.concatenate([middle, jnp.zeros_like(middle)], axis=0).astype(stack_ref.dtype)
+                conv = conv + jnp.dot(far_table_ref[:, NODES * rows :], middle, preferred_element_type=jnp.float32)
             part_ref[:, c - start : d - start] = conv + skip_ref[:, c:d] * mixed
             rim = rims_ref[:, c:d].astype(jnp.float32) * keep
             gate_ref[:, c - start : d - start] = featurize(query_ref[:, c:d], taps_ref[0, :, c:d], rim)
         offset = offset + chunk.shape[1]
 
 
+def repaired(last, far_ref, pre_ref, right, c, d):
+    end = far_ref[0:1, c:d] * last[0]
+    for j in range(1, NODES):
+        end = end + far_ref[j : j + 1, c:d] * last[j]
+    there = (lax.axis_index("seq") >= 2).astype(jnp.float32)
+    total = pre_ref[0:16, c:d]
+    row = lax.broadcasted_iota(jnp.int32, total.shape, 0)
+    total = jnp.where(row == 0, total + end * (right - pre_ref[33:34, c:d] * there), total)
+    return pre_ref[16:32, c:d] * total
+
+
+def send_kernel(start, early, *refs):
+    *_, mixed_ref, head_ref, far_ref, table_ref, out_ref, stack_ref = refs
+    rows, width = mixed_ref.shape
+    for a, b in columns(0, width, stack_ref.shape[1]):
+        c, d = start + a, start + b
+        mixed = mixed_ref[:, a:b].astype(jnp.float32)
+        for j in range(NODES):
+            stack_ref[j * rows : (j + 1) * rows, : b - a] = (mixed * far_ref[j : j + 1, c:d]).astype(stack_ref.dtype)
+        conv = jnp.dot(table_ref[:, : NODES * rows], stack_ref[:, : b - a], preferred_element_type=jnp.float32)
+        out_ref[: rows - 16, a:b] = conv[: rows - 16].astype(out_ref.dtype)
+        bottom = conv[rows - 16 :]
+        slot = c - early
+        if slot < early:
+            row = lax.broadcasted_iota(jnp.int32, bottom.shape, 0)
+            second = head_ref[:, slot : slot + b - a].astype(jnp.float32)[1:2]
+            bottom = jnp.where(row == 15, second, bottom)
+        out_ref[rows - 16 :, a:b] = bottom.astype(out_ref.dtype)
+
+
+def last_kernel(offset, base, slot, last, far_ref, part_ref, gate_ref, pre_ref, _, back_ref, out_ref, stage_ref, repair_ref, sems):
+    rows, width = back_ref.shape
+    copies = []
+
+    def write(source, tall, c, d):
+        copies.append(pltpu.make_async_copy(source, out_ref.at[pl.ds(0, tall), pl.ds(c, d - c)], sems.at[len(copies)]))
+        copies[-1].start()
+
+    first, stop = slot
+    for c, d in columns(first, stop, 512):
+        right = back_ref[rows - 16 :, c - first : d - first].astype(jnp.float32)[15:16]
+        repair_ref[:, c - first : d - first] = repaired(last, far_ref, pre_ref, right, c, d).astype(repair_ref.dtype)
+    if stop > first:
+        write(repair_ref.at[:, pl.ds(0, stop - first)], 16, first, stop)
+    for a, b in columns(0, width, LAST_TILE):
+        c, d = offset + a, offset + b
+        back = back_ref[:, a:b].astype(jnp.float32)
+        bottom = back[rows - 16 :]
+        row = lax.broadcasted_iota(jnp.int32, bottom.shape, 0)
+        back = jnp.concatenate([back[: rows - 16], jnp.where(row == 15, 0.0, bottom)], axis=0)
+        total = part_ref[:, c - base : d - base] + back
+        stage_ref[:, a:b] = (gate_ref[:, c - base : d - base] * total).astype(stage_ref.dtype)
+        write(stage_ref.at[:, pl.ds(a, b - a)], rows, c, d)
+    for copy in copies:
+        copy.wait()
+
+
 def finish_kernel(offset, base, slots, last, middle_ref, far_ref, part_ref, gate_ref, table_ref, *refs):
     keep = (lax.axis_index("seq") >= 1).astype(jnp.float32)
+    there = (lax.axis_index("seq") >= 2).astype(jnp.float32)
     if slots is None:
         _, *backs, out_ref, pre_ref, stack_ref, stage_ref, sems = refs
     else:
@@ -273,8 +332,9 @@
         for a, b in columns(0, width, stack_ref.shape[1]):
             c, d = offset + at + a, offset + at + b
             back = back_ref[:, a:b].astype(jnp.float32)
+            far = far_ref[:, c:d] * there
             for j in range(NODES):
-                stack_ref[j * rows : (j + 1) * rows, : b - a] = (back * far_ref[j : j + 1, c:d]).astype(stack_ref.dtype)
+                stack_ref[j * rows : (j + 1) * rows, : b - a] = (back * far[j : j + 1]).astype(stack_ref.dtype)
             middle = middle_ref[:, c:d].astype(jnp.float32) * keep
             middle = jnp.concatenate([middle, jnp.zeros_like(middle)], axis=0)
             stack_ref[NODES * rows : NODES * rows + 2 * PADDED, : b - a] = middle.astype(stack_ref.dtype)
@@ -291,14 +351,9 @@
     start = 0
     for (first, stop), back_ref in zip(slots or (), backs):
         for c, d in columns(first, stop, 512):
-            end = far_ref[0:1, c:d] * last[0]
-            for j in range(1, NODES):
-                end = end + far_ref[j : j + 1, c:d] * last[j]
             right = back_ref[0:16, c - first : d - first].astype(jnp.float32)[0:1]
-            total = pre_ref[0:16, c:d]
-            row = lax.broadcasted_iota(jnp.int32, total.shape, 0)
-            total = jnp.where(row == 0, total + end * (right - pre_ref[33:34, c:d]), total)
-            repair_ref[:, start + c - first : start + d - first] = (pre_ref[16:32, c:d] * total).astype(repair_ref.dtype)
+            fixed = repaired(last, far_ref, pre_ref, right * there, c, d)
+            repair_ref[:, start + c - first : start + d - first] = fixed.astype(repair_ref.dtype)
         if stop > first:
             write(repair_ref.at[:, pl.ds(start, stop - first)], 16, first, stop)
         start = start + stop - first
@@ -397,32 +452,31 @@
 
     tile = 512
 
-    def own(first, stop, some):
+    def own(first, stop, some, complete):
         return call(
-            functools.partial(own_kernel, edge, cuts[first]),
+            functools.partial(own_kernel, edge, cuts[first], complete),
             [vmem] * (7 + len(some)),
             [((rows, cuts[stop] - cuts[first]), f32)] * 2,
             (query_in, head, near, taps_v, rims_in, skip_row, near_table, *some),
             [pltpu.VMEM((near_table.shape[1], tile), bf16)],
         )
 
-    early_own = own(0, 2, (c1, c2))
+    early_own = own(0, 2, (c1, c2), False)
     (final,) = call(
-        pass_kernel,
-        [anywhere] * 4,
-        [((rows, sizes[-1]), bf16, anywhere)],
-        (middle_in, early_own[0], back[0], chunks[-1]),
-        input_output_aliases={3: 0},
+        functools.partial(send_kernel, cuts[-2], cuts[2]),
+        [anywhere] * 3 + [vmem] * 4,
+        [((rows, sizes[-1]), bf16)],
+        (middle_in, early_own[0], back[0], chunks[-1], head, far, far_table),
+        [pltpu.VMEM((NODES * rows, tile), bf16)],
     )
     back[-1] = ring(final, 2, closed=False)
-    late_own = own(2, count_chunks, [*chunks[:-1], final])
+    late_own = own(2, count_chunks, (middle_in, far_table, *chunks), True)
 
     def finish(first, stop, out, pre):
         some = range(first, stop)
         size = cuts[stop] - cuts[first]
-        step = tile if stop < count_chunks else LAST_TILE
-        pieces = sum(len(columns(0, sizes[i], step)) for i in some)
-        scratch = [pltpu.VMEM((far_table.shape[1], step), bf16), pltpu.VMEM((rows, size), bf16)]
+        pieces = sum(len(columns(0, sizes[i], tile)) for i in some)
+        scratch = [pltpu.VMEM((far_table.shape[1], tile), bf16), pltpu.VMEM((rows, size), bf16)]
         slots = None
         if out is not None:
             slots = [(min(cuts[i] - cuts[2], cuts[2]), min(cuts[i + 1] - cuts[2], cuts[2])) for i in some]
@@ -441,7 +495,19 @@
 
     out, pre = finish(0, 2, None, None)
     (out,) = finish(2, count_chunks - 1, out, pre)
-    (out,) = finish(count_chunks - 1, count_chunks, out, pre)
+    slot = (min(cuts[-2] - cuts[2], cuts[2]), min(width - cuts[2], cuts[2]))
+    (out,) = call(
+        functools.partial(last_kernel, cuts[-2], cuts[2], slot, last),
+        [vmem] * 4 + [anywhere, vmem],
+        [((rows, width), bf16, anywhere)],
+        (far, *late_own, pre, out, back[-1]),
+        [
+            pltpu.VMEM((rows, sizes[-1]), bf16),
+            pltpu.VMEM((16, max(slot[1] - slot[0], unit)), bf16),
+            pltpu.SemaphoreType.DMA((len(columns(0, sizes[-1], LAST_TILE)) + 1,)),
+        ],
+        input_output_aliases={4: 0},
+    )
     return out
 
 

time: 29.9 us -> 29.5 us (0.987)
  transfers between devices with their start and end apart: 7 -> 7, of which waited for: 3 -> 3; matrix products, arithmetic and copies ran while one was open for 0% -> 0% of each run, Pallas kernels for 36% -> 37%
where the time goes in v6:
time: 29.5 us; the launch traced here: 29.1 us
  Pallas kernels  12.9 us (44%)
  starting transfers between devices  9.56 us (32%)
  waiting for transfers between devices  6.49 us (22%)
    pallas_call x10, Pallas kernels, call(): pl.pallas_call(body, in_specs=ins, out_specs=[o[2] if len(o) > 2 else vme...  12.9 us
    ppermute x7, starting transfers between devices, ring(): lax.ppermute(array, 'seq', [(i, (i + by) % length) for i in range(length)...  9.56 us
    ppermute x7, waiting for transfers between devices, ring(): lax.ppermute(array, 'seq', [(i, (i + by) % length) for i in range(length)...  6.49 us
  transfers between devices with their start and end apart: 7, of which 3 were waited for; matrix products, arithmetic and copies ran while one was open for 0% of the time, Pallas kernels for 37%

profile of v6, /device:TPU:24, one launch (start us, length us, event | category | flops | bytes accessed | tf_op | source)
XLA Modules:
  0.0 29.1 jit_solution(9895496312298119908)
XLA Ops:
  0.0 1.3 %shard_map.100._.c1.refs_0_ = bf16[128,896]{1,0:T(8,128)(2,1)S(1)} custom-call(bf16[128,4096]{1,0:T(8,128)(2,1)} %key_ref.5, bf16[128,4096]{1,0:T(8,128)(2,1)} %value_ref.5, f32[3,3,4096]{2,1,0:T(4,128)} %taps_ref.3), custom_call_target="tpu_custom_call" | custom-call | flops 1 | bytes 1 | tf_op jit(solution)/shard_map/pallas_call | solution.py:387
  1.3 1.6 %collective-permute-start.2 = (bf16[128,896]{1,0:T(8,128)(2,1)S(1)}, bf16[128,896]{1,0:T(8,128)(2,1)S(1)}, u32[]{:S(2)}, u32[]{:S(2)}) collective-permute-start(bf16[128,896]{1,0:T(8,128)(2,1)S(1)} %shard_map.100._.c1.refs_0_), channel_id=1, source_target_pairs={{0,2},{1,3},{2,4},{3,5},{4,6},{5,7},{6,8},{7,9},{8,10},{9,11},{10,... | collective-permute-start | bytes 688136 | tf_op jit(solution)/shard_map/ppermute | solution.py:366
  2.9 0.0 copy-start.4
  2.9 1.6 %shard_map.101 = (bf16[128,1024]{1,0:T(8,128)(2,1)S(1)}, bf16[2,12288]{1,0:T(2,128)(2,1)S(1)}, f32[3,3,4096]{2,1,0:T(4,128)S(1)}, f32[16,4096]{1,0:T(8,128)S(1)}, f32[16,4096]{1,0:T(8,128)S(1)}) custom-call(bf16[128,896]{1,0:T(8,128)(2,1)S(1)} %shard_map.100._.c1.refs_0_, bf16[128,4096]{1,0:T(8,128)(2,1)} %query_ref.5, bf16[128,4096]{1,0:T(8,128)(2,1)} %key_ref.5, ...), custom_call_target="tpu_custom_call" | custom-call | flops 1 | bytes 1 | tf_op jit(solution)/shard_map/pallas_call | solution.py:387
  4.5 0.1 collective-permute-start
  4.6 0.1 collective-permute-start.3
  4.6 0.0 copy-done.4
  4.6 1.3 %shard_map.102 = (f32[8,4096]{1,0:T(8,128)S(1)}, f32[8,4096]{1,0:T(8,128)S(1)}, f32[16,1920]{1,0:T(8,128)S(1)}, f32[16,1920]{1,0:T(8,128)S(1)}, f32[16,1920]{1,0...) custom-call(bf16[128,4096]{1,0:T(8,128)(2,1)} %key_ref.5, ...), custom_call_target="tpu_custom_call" | custom-call | flops 1 | bytes 1 | tf_op jit(solution)/shard_map/pallas_call | solution.py:387
  5.9 3.6 %collective-permute-done.rims_ref = bf16[2,12288]{1,0:T(2,128)(2,1)S(1)} collective-permute-done((bf16[2,12288]{1,0:T(2,128)(2,1)S(1)}, bf16[2,12288]{1,0:T(2,128)(2,1)S(1)}, u32[]{:S(2)}, u32[]{:S(2)}) %collective-permute-start) | collective-permute-done | bytes 49184 | tf_op jit(solution)/shard_map/ppermute | solution.py:366
  9.5 0.0 copy-start
  9.5 1.4 %shard_map.103 = (bf16[8,4096]{1,0:T(8,128)(2,1)S(1)}, bf16[8,4096]{1,0:T(8,128)(2,1)S(1)}, bf16[128,768]{1,0:T(8,128)(2,1)S(1)}, bf16[128,768]{1,0:T(8,128)(2,1)S(1)}, bf16[128,640]{1,0:T(8,128)(2,1)S(1)}) custom-call(bf16[128,4096]{1,0:T(8,128)(2,1)S(1)} %get-tuple-element.34.key_ref, bf16[128,4096]{1,0:T(8,128)(2,1)S(1)} %get-tuple-element.35.value_ref, ...), custom_call_target="tpu_custom_call" | custom-call | flops 1 | bytes 1 | tf_op jit(solution)/shard_map/pallas_call | solution.py:387
  10.9 0.0 copy-start.1
  10.9 0.1 collective-permute-start.1
  11.0 0.7 %collective-permute-start.4 = (bf16[128,768]{1,0:T(8,128)(2,1)S(1)}, bf16[128,768]{1,0:T(8,128)(2,1)S(1)}, u32[]{:S(2)}, u32[]{:S(2)}) collective-permute-start(bf16[128,768]{1,0:T(8,128)(2,1)S(1)} %get-tuple-element.46.refs_2_), channel_id=1, source_target_pairs={{0,2},{1,3},{2,4},{3,5},{4,6},{5,7},{6,8},{7,9},{8,10},{9,11},{10,... | collective-permute-start | bytes 589832 | tf_op jit(solution)/shard_map/ppermute | solution.py:366
  11.7 5.2 %collective-permute-start.5 = (bf16[128,768]{1,0:T(8,128)(2,1)S(1)}, bf16[128,768]{1,0:T(8,128)(2,1)S(1)}, u32[]{:S(2)}, u32[]{:S(2)}) collective-permute-start(bf16[128,768]{1,0:T(8,128)(2,1)S(1)} %get-tuple-element.47.refs_3_), channel_id=1, source_target_pairs={{0,2},{1,3},{2,4},{3,5},{4,6},{5,7},{6,8},{7,9},{8,10},{9,11},{10,... | collective-permute-start | bytes 589832 | tf_op jit(solution)/shard_map/ppermute | solution.py:366
  16.9 0.0 copy-done
  16.9 0.0 copy-done.2
  16.9 0.0 copy-done.3
  16.9 1.4 %shard_map.105 = (f32[128,1920]{1,0:T(8,128)S(1)}, f32[128,1920]{1,0:T(8,128)S(1)}) custom-call(bf16[128,4096]{1,0:T(8,128)(2,1)S(1)} %copy-done, bf16[8,4096]{1,0:T(8,128)(2,1)S(1)} %get-tuple-element.43.head_ref.refs_4_, f32[8,4096]{1,0:T(8,128)S(1)} %get-tuple-element.44.near_ref, f32[3,3,4096]{2,1,0:T(4,128)S(1)} %get-tuple-element.37.taps_ref, ...), custom_call_target="tpu_custom_call" | custom-call | flops 1 | bytes 1 | tf_op jit(solution)/shard_map/pallas_call | solution.py:387
  18.4 0.0 collective-permute-done.1.refs_0_.middle_ref
  18.4 0.0 collective-permute-done.2.refs_1_.refs_2_
  18.4 0.0 copy-done.1
  18.4 0.4 %shard_map.108 = bf16[128,640]{1,0:T(8,128)(2,1)S(1)} custom-call(bf16[8,4096]{1,0:T(8,128)(2,1)S(1)} %collective-permute-done.1.refs_0_.middle_ref, f32[128,1920]{1,0:T(8,128)S(1)} %get-tuple-element.51.part_ref.refs_1_, bf16[128,896]{1,0:T(8,128)(2,1)S(1)} %collective-permute-done.2.refs_1_.refs_2_, ...), custom_call_target="tpu_custom_call" | custom-call | flops 1 | bytes 1 | tf_op jit(solution)/shard_map/pallas_call | solution.py:387
  18.8 1.9 %collective-permute-start.6 = (bf16[128,640]{1,0:T(8,128)(2,1)S(1)}, bf16[128,640]{1,0:T(8,128)(2,1)S(1)}, u32[]{:S(2)}, u32[]{:S(2)}) collective-permute-start(bf16[128,640]{1,0:T(8,128)(2,1)S(1)} %shard_map.108), channel_id=1, source_target_pairs={{0,2},{1,3},{2,4},{3,5},{4,6},{5,7},{6,8},{7,9},{8,10},{9,11},{10,... | collective-permute-start | bytes 491528 | tf_op jit(solution)/shard_map/ppermute | solution.py:366
  20.8 1.6 %shard_map.104 = (f32[128,2176]{1,0:T(8,128)S(1)}, f32[128,2176]{1,0:T(8,128)S(1)}) custom-call(bf16[128,4096]{1,0:T(8,128)(2,1)S(1)} %copy-done, bf16[8,4096]{1,0:T(8,128)(2,1)S(1)} %get-tuple-element.43.head_ref.refs_4_, f32[8,4096]{1,0:T(8,128)S(1)} %get-tuple-element.44.near_ref, f32[3,3,4096]{2,1,0:T(4,128)S(1)} %get-tuple-element.37.taps_ref, ...), custom_call_target="tpu_custom_call" | custom-call | flops 1 | bytes 1 | tf_op jit(solution)/shard_map/pallas_call | solution.py:387
  22.4 0.0 collective-permute-done.3.refs_2_
  22.4 1.7 %shard_map.106 = (bf16[128,4096]{1,0:T(8,128)(2,1)}, f32[40,1920]{1,0:T(8,128)S(1)}) custom-call(bf16[8,4096]{1,0:T(8,128)(2,1)S(1)} %collective-permute-done.1.refs_0_.middle_ref, f32[8,4096]{1,0:T(8,128)S(1)} %get-tuple-element.33.far_ref.refs_5_, f32[128,1920]{1,0:T(8,128)S(1)} %get-tuple-element.51.part_ref.refs_1_, ...), custom_call_target="tpu_custom_call" | custom-call | flops 1 | bytes 1 | tf_op jit(solution)/shard_map/pallas_call | solution.py:387
  24.1 0.0 collective-permute-done.4.refs_2_
  24.1 0.7 %collective-permute-done.5.refs_3_ = bf16[128,768]{1,0:T(8,128)(2,1)S(1)} collective-permute-done((bf16[128,768]{1,0:T(8,128)(2,1)S(1)}, bf16[128,768]{1,0:T(8,128)(2,1)S(1)}, u32[]{:S(2)}, u32[]{:S(2)}) %collective-permute-start.5) | collective-permute-done | bytes 196640 | tf_op jit(solution)/shard_map/ppermute | solution.py:366
  24.8 1.4 %shard_map.107._ = bf16[128,4096]{1,0:T(8,128)(2,1)} custom-call(bf16[8,4096]{1,0:T(8,128)(2,1)S(1)} %collective-permute-done.1.refs_0_.middle_ref, f32[8,4096]{1,0:T(8,128)S(1)} %get-tuple-element.33.far_ref.refs_5_, f32[128,2176]{1,0:T(8,128)S(1)} %get-tuple-element.49.refs_0_.part_ref, ...), custom_call_target="tpu_custom_call", output_to_operand_aliasing={{}: (6, {})} | custom-call | flops 1 | bytes 1 | tf_op jit(solution)/shard_map/pallas_call | solution.py:387
  26.2 2.2 %collective-permute-done.6.back_ref = bf16[128,640]{1,0:T(8,128)(2,1)S(1)} collective-permute-done((bf16[128,640]{1,0:T(8,128)(2,1)S(1)}, bf16[128,640]{1,0:T(8,128)(2,1)S(1)}, u32[]{:S(2)}, u32[]{:S(2)}) %collective-permute-start.6) | collective-permute-done | bytes 163872 | tf_op jit(solution)/shard_map/ppermute | solution.py:366
  28.4 0.7 %shard_map.109 = bf16[128,4096]{1,0:T(8,128)(2,1)} custom-call(f32[8,4096]{1,0:T(8,128)S(1)} %get-tuple-element.33.far_ref.refs_5_, f32[128,2176]{1,0:T(8,128)S(1)} %get-tuple-element.49.refs_0_.part_ref, f32[128,2176]{1,0:T(8,128)S(1)} %get-tuple-element.50.gate_ref, ...), custom_call_target="tpu_custom_call", output_to_operand_aliasing={{}: (4, {})} | custom-call | flops 1 | bytes 1 | tf_op jit(solution)/shard_map/pallas_call | solution.py:387
  (2 shorter events, 0.0 us)
Async XLA Ops:
  1.3 17.0 %collective-permute-start.2 = (bf16[128,896]{1,0:T(8,128)(2,1)S(1)}, bf16[128,896]{1,0:T(8,128)(2,1)S(1)}, u32[]{:S(2)}, u32[]{:S(2)}) collective-permute-start(bf16[128,896]{1,0:T(8,128)(2,1)S(1)} %shard_map.100._.c1.refs_0_), channel_id=1, source_target_pairs={{0,2},{1,3},{2,4},{3,5},{4,6},{5,7},{6,8},{7,9},{8,10},{9,11},{10,... | collective-permute-start | bytes 688136 | tf_op jit(solution)/shard_map/ppermute | solution.py:366
  2.9 1.7 %copy-start.4 = (bf16[16,128]{1,0:T(8,128)(2,1)S(1)}, bf16[16,128]{1,0:T(8,128)(2,1)}, u32[]{:S(2)}) copy-start(bf16[16,128]{1,0:T(8,128)(2,1)} %constant.8.clone.moment_ref) | copy-start | bytes 12292
  4.5 5.0 %collective-permute-start = (bf16[2,12288]{1,0:T(2,128)(2,1)S(1)}, bf16[2,12288]{1,0:T(2,128)(2,1)S(1)}, u32[]{:S(2)}, u32[]{:S(2)}) collective-permute-start(bf16[2,12288]{1,0:T(2,128)(2,1)S(1)} %get-tuple-element.36), channel_id=1, source_target_pairs={{0,1},{1,2},{2,3},{3,4},{4,5},{5,6},{6,7},{7,8},{8,9},{9,10},{10,1... | collective-permute-start | bytes 147464 | tf_op jit(solution)/shard_map/ppermute | solution.py:366
  4.6 17.9 %collective-permute-start.3 = (bf16[128,1024]{1,0:T(8,128)(2,1)S(1)}, bf16[128,1024]{1,0:T(8,128)(2,1)S(1)}, u32[]{:S(2)}, u32[]{:S(2)}) collective-permute-start(bf16[128,1024]{1,0:T(8,128)(2,1)S(1)} %get-tuple-element.32.c2.refs_1_), channel_id=1, source_target_pairs={{0,2},{1,3},{2,4},{3,5},{4,6},{5,7},{6,8},{7,9},{8,10},{9,11},{10,... | collective-permute-start | bytes 786440 | tf_op jit(solution)/shard_map/ppermute | solution.py:366
  9.5 7.3 %copy-start = (bf16[128,4096]{1,0:T(8,128)(2,1)S(1)}, bf16[128,4096]{1,0:T(8,128)(2,1)}, u32[]{:S(2)}) copy-start(bf16[128,4096]{1,0:T(8,128)(2,1)} %query_ref.5) | copy-start | bytes 3145732
  9.5 7.4 %copy-start.2 = (bf16[128,896]{1,0:T(8,128)(2,1)S(1)}, bf16[128,896]{1,0:T(8,128)(2,1)}, u32[]{:S(2)}) copy-start(bf16[128,896]{1,0:T(8,128)(2,1)} %constant.6.clone.table_ref) | copy-start | bytes 688132
  9.5 7.4 %copy-start.3 = (f32[4096]{0:T(1024)S(1)}, f32[4096]{0:T(1024)}, u32[]{:S(2)}) copy-start(f32[4096]{0:T(1024)} %param.16) | copy-start | bytes 49156
  10.9 7.5 %copy-start.1 = (bf16[128,912]{1,0:T(8,128)(2,1)S(1)}, bf16[128,912]{1,0:T(8,128)(2,1)}, u32[]{:S(2)}) copy-start(bf16[128,912]{1,0:T(8,128)(2,1)} %constant.7.clone.refs_1_.table_ref.refs_6_) | copy-start | bytes 700420
  10.9 7.4 %collective-permute-start.1 = (bf16[8,4096]{1,0:T(8,128)(2,1)S(1)}, bf16[8,4096]{1,0:T(8,128)(2,1)S(1)}, u32[]{:S(2)}, u32[]{:S(2)}) collective-permute-start(bf16[8,4096]{1,0:T(8,128)(2,1)S(1)} %get-tuple-element.45), channel_id=1, source_target_pairs={{0,1},{1,2},{2,3},{3,4},{4,5},{5,6},{6,7},{7,8},{8,9},{9,10},{10,1... | collective-permute-start | bytes 196616 | tf_op jit(solution)/shard_map/ppermute | solution.py:366
  11.0 13.1 %collective-permute-start.4 = (bf16[128,768]{1,0:T(8,128)(2,1)S(1)}, bf16[128,768]{1,0:T(8,128)(2,1)S(1)}, u32[]{:S(2)}, u32[]{:S(2)}) collective-permute-start(bf16[128,768]{1,0:T(8,128)(2,1)S(1)} %get-tuple-element.46.refs_2_), channel_id=1, source_target_pairs={{0,2},{1,3},{2,4},{3,5},{4,6},{5,7},{6,8},{7,9},{8,10},{9,11},{10,... | collective-permute-start | bytes 589832 | tf_op jit(solution)/shard_map/ppermute | solution.py:366
  11.7 13.2 %collective-permute-start.5 = (bf16[128,768]{1,0:T(8,128)(2,1)S(1)}, bf16[128,768]{1,0:T(8,128)(2,1)S(1)}, u32[]{:S(2)}, u32[]{:S(2)}) collective-permute-start(bf16[128,768]{1,0:T(8,128)(2,1)S(1)} %get-tuple-element.47.refs_3_), channel_id=1, source_target_pairs={{0,2},{1,3},{2,4},{3,5},{4,6},{5,7},{6,8},{7,9},{8,10},{9,11},{10,... | collective-permute-start | bytes 589832 | tf_op jit(solution)/shard_map/ppermute | solution.py:366
  18.8 9.6 %collective-permute-start.6 = (bf16[128,640]{1,0:T(8,128)(2,1)S(1)}, bf16[128,640]{1,0:T(8,128)(2,1)S(1)}, u32[]{:S(2)}, u32[]{:S(2)}) collective-permute-start(bf16[128,640]{1,0:T(8,128)(2,1)S(1)} %shard_map.108), channel_id=1, source_target_pairs={{0,2},{1,3},{2,4},{3,5},{4,6},{5,7},{6,8},{7,9},{8,10},{9,11},{10,... | collective-permute-start | bytes 491528 | tf_op jit(solution)/shard_map/ppermute | solution.py:366

commit v7 on v6

--- a/solution.py
+++ b/solution.py
@@ -190,6 +190,7 @@
     key_ref, value_ref, rims_ref, taps_ref, moment_ref, c1, c2, state_ref, first_ref, second_ref, decay_ref,
     spread_ref, head_ref, middle_ref, *late,
 ):
+    *late, odd_ref = late
     width = key_ref.shape[1]
     early = c1.shape[1] + c2.shape[1]
     modes = state_ref.shape[0]
@@ -226,9 +227,28 @@
                 jnp.sum(spread_ref[i * modes : (i + 1) * modes, c:d] * state, axis=0, keepdims=True)
                 for i in range(NODES)
             ]
-            middle.append(jnp.zeros((PADDED - NODES, d - c), jnp.float32))
-            middle_ref[:, c:d] = jnp.concatenate(middle, axis=0).astype(middle_ref.dtype)
+            for i in range(0, NODES - 1, 2):
+                pair = jnp.concatenate(middle[i : i + 2], axis=0)
+                middle_ref[:, i // 2 * width + c : i // 2 * width + d] = pair.astype(middle_ref.dtype)
+            odd_ref[0:1, c:d] = middle[-1]
         offset = offset + chunk.shape[1]
+    half = width // 2
+    pair = jnp.concatenate([odd_ref[0:1, :half], odd_ref[0:1, half:]], axis=0)
+    middle_ref[:, NODES // 2 * width :] = pair.astype(middle_ref.dtype)
+
+
+def middle_rows(middle_ref, c, d):
+    width = middle_ref.shape[1] * 2 // NODES
+    half, base = width // 2, NODES // 2 * width
+    parts = [middle_ref[:, i * width + c : i * width + d].astype(jnp.float32) for i in range(NODES // 2)]
+    odd = []
+    if c < half:
+        odd.append(middle_ref[:, base + c : base + min(d, half)].astype(jnp.float32)[0:1])
+    if d > half:
+        odd.append(middle_ref[:, base + max(c, half) - half : base + d - half].astype(jnp.float32)[1:2])
+    parts.append(odd[0] if len(odd) == 1 else jnp.concatenate(odd, axis=1))
+    parts.append(jnp.zeros((2 * PADDED - NODES, d - c), jnp.float32))
+    return jnp.concatenate(parts, axis=0)
 
 
 def own_kernel(edge, start, complete, query_ref, head_ref, near_ref, taps_ref, rims_ref, skip_ref, table_ref, *refs):
@@ -247,8 +267,7 @@
                 stack_ref[j * rows : (j + 1) * rows, : b - a] = (mixed * near_ref[j : j + 1, c:d]).astype(stack_ref.dtype)
             conv = jnp.dot(table_ref[...], stack_ref[:, : b - a], preferred_element_type=jnp.float32)
             if complete and chunk is chunks[-1]:
-                middle = middle_ref[:, c:d].astype(jnp.float32) * keep
-                middle = jnp.concatenate([middle, jnp.zeros_like(middle)], axis=0).astype(stack_ref.dtype)
+                middle = (middle_rows(middle_ref, c, d) * keep).astype(stack_ref.dtype)
                 conv = conv + jnp.dot(far_table_ref[:, NODES * rows :], middle, preferred_element_type=jnp.float32)
             part_ref[:, c - start : d - start] = conv + skip_ref[:, c:d] * mixed
             rim = rims_ref[:, c:d].astype(jnp.float32) * keep
@@ -335,8 +354,7 @@
             far = far_ref[:, c:d] * there
             for j in range(NODES):
                 stack_ref[j * rows : (j + 1) * rows, : b - a] = (back * far[j : j + 1]).astype(stack_ref.dtype)
-            middle = middle_ref[:, c:d].astype(jnp.float32) * keep
-            middle = jnp.concatenate([middle, jnp.zeros_like(middle)], axis=0)
+            middle = middle_rows(middle_ref, c, d) * keep
             stack_ref[NODES * rows : NODES * rows + 2 * PADDED, : b - a] = middle.astype(stack_ref.dtype)
             conv = jnp.dot(table_ref[...], stack_ref[:, : b - a], preferred_element_type=jnp.float32)
             total = part_ref[:, c - base : d - base] + conv
@@ -443,8 +461,9 @@
     head, middle, *chunks = call(
         edge_kernel,
         [vmem] * 12,
-        [((8, width), bf16), ((PADDED, width), bf16)] + [((rows, sizes[i]), bf16) for i in late],
+        [((8, width), bf16), ((2, NODES * width // 2), bf16)] + [((rows, sizes[i]), bf16) for i in late],
         (key_v, value_v, rims_in, taps_v, moment_table, c1, c2, *states),
+        [pltpu.VMEM((8, width), f32)],
     )
     middle_in = ring(middle, 1)
     for i in late[:-1]:

time: 29.5 us -> 29.4 us (level)
  waiting for transfers between devices: 6.49 us -> 6.19 us
    ppermute x7, waiting for transfers between devices: 6.49 us -> 6.19 us  [ring(): lax.ppermute(array, 'seq', [(i, (i + by) % length) for i in range(length)...]
  transfers between devices with their start and end apart: 7 -> 7, of which waited for: 3 -> 3; matrix products, arithmetic and copies ran while one was open for 0% -> 0% of each run, Pallas kernels for 37% -> 38%
where the time goes in v7:
time: 29.4 us; the launch traced here: 29.1 us
  Pallas kernels  13.1 us (45%)
  starting transfers between devices  9.56 us (33%)
  waiting for transfers between devices  6.19 us (21%)
    pallas_call x10, Pallas kernels, call(): pl.pallas_call(body, in_specs=ins, out_specs=[o[2] if len(o) > 2 else vme...  13.1 us
    ppermute x7, starting transfers between devices, ring(): lax.ppermute(array, 'seq', [(i, (i + by) % length) for i in range(length)...  9.56 us
    ppermute x7, waiting for transfers between devices, ring(): lax.ppermute(array, 'seq', [(i, (i + by) % length) for i in range(length)...  6.19 us
  transfers between devices with their start and end apart: 7, of which 3 were waited for; matrix products, arithmetic and copies ran while one was open for 0% of the time, Pallas kernels for 38%

profile of v7, /device:TPU:24, one launch (start us, length us, event | category | flops | bytes accessed | tf_op | source)
XLA Modules:
  0.0 29.1 jit_solution(7801020625484009052)
XLA Ops:
  0.0 1.3 %shard_map.100._.c1.refs_0_ = bf16[128,896]{1,0:T(8,128)(2,1)S(1)} custom-call(bf16[128,4096]{1,0:T(8,128)(2,1)} %key_ref.5, bf16[128,4096]{1,0:T(8,128)(2,1)} %value_ref.5, f32[3,3,4096]{2,1,0:T(4,128)} %taps_ref.3), custom_call_target="tpu_custom_call" | custom-call | flops 1 | bytes 1 | tf_op jit(solution)/shard_map/pallas_call | solution.py:405
  1.3 1.6 %collective-permute-start.2 = (bf16[128,896]{1,0:T(8,128)(2,1)S(1)}, bf16[128,896]{1,0:T(8,128)(2,1)S(1)}, u32[]{:S(2)}, u32[]{:S(2)}) collective-permute-start(bf16[128,896]{1,0:T(8,128)(2,1)S(1)} %shard_map.100._.c1.refs_0_), channel_id=1, source_target_pairs={{0,2},{1,3},{2,4},{3,5},{4,6},{5,7},{6,8},{7,9},{8,10},{9,11},{10,... | collective-permute-start | bytes 688136 | tf_op jit(solution)/shard_map/ppermute | solution.py:384
  2.9 0.0 copy-start.4
  2.9 1.6 %shard_map.101 = (bf16[128,1024]{1,0:T(8,128)(2,1)S(1)}, bf16[2,12288]{1,0:T(2,128)(2,1)S(1)}, f32[3,3,4096]{2,1,0:T(4,128)S(1)}, f32[16,4096]{1,0:T(8,128)S(1)}, f32[16,4096]{1,0:T(8,128)S(1)}) custom-call(bf16[128,896]{1,0:T(8,128)(2,1)S(1)} %shard_map.100._.c1.refs_0_, bf16[128,4096]{1,0:T(8,128)(2,1)} %query_ref.5, bf16[128,4096]{1,0:T(8,128)(2,1)} %key_ref.5, ...), custom_call_target="tpu_custom_call" | custom-call | flops 1 | bytes 1 | tf_op jit(solution)/shard_map/pallas_call | solution.py:405
  4.5 0.1 collective-permute-start
  4.6 0.1 collective-permute-start.3
  4.6 0.0 copy-done.4
  4.6 1.3 %shard_map.102 = (f32[8,4096]{1,0:T(8,128)S(1)}, f32[8,4096]{1,0:T(8,128)S(1)}, f32[16,1920]{1,0:T(8,128)S(1)}, f32[16,1920]{1,0:T(8,128)S(1)}, f32[16,1920]{1,0...) custom-call(bf16[128,4096]{1,0:T(8,128)(2,1)} %key_ref.5, ...), custom_call_target="tpu_custom_call" | custom-call | flops 1 | bytes 1 | tf_op jit(solution)/shard_map/pallas_call | solution.py:405
  5.9 3.6 %collective-permute-done.rims_ref = bf16[2,12288]{1,0:T(2,128)(2,1)S(1)} collective-permute-done((bf16[2,12288]{1,0:T(2,128)(2,1)S(1)}, bf16[2,12288]{1,0:T(2,128)(2,1)S(1)}, u32[]{:S(2)}, u32[]{:S(2)}) %collective-permute-start) | collective-permute-done | bytes 49184 | tf_op jit(solution)/shard_map/ppermute | solution.py:384
  9.5 0.0 copy-start
  9.5 1.4 %shard_map.103 = (bf16[8,4096]{1,0:T(8,128)(2,1)S(1)}, bf16[2,14336]{1,0:T(2,128)(2,1)S(1)}, bf16[128,768]{1,0:T(8,128)(2,1)S(1)}, bf16[128,768]{1,0:T(8,128)(2,1)S(1)}, bf16[128,640]{1,0:T(8,128)(2,1)S(1)}) custom-call(bf16[128,4096]{1,0:T(8,128)(2,1)S(1)} %get-tuple-element.34.key_ref, bf16[128,4096]{1,0:T(8,128)(2,1)S(1)} %get-tuple-element.35.value_ref, ...), custom_call_target="tpu_custom_call" | custom-call | flops 1 | bytes 1 | tf_op jit(solution)/shard_map/pallas_call | solution.py:405
  10.9 0.0 copy-start.1
  10.9 0.1 collective-permute-start.1
  11.0 0.7 %collective-permute-start.4 = (bf16[128,768]{1,0:T(8,128)(2,1)S(1)}, bf16[128,768]{1,0:T(8,128)(2,1)S(1)}, u32[]{:S(2)}, u32[]{:S(2)}) collective-permute-start(bf16[128,768]{1,0:T(8,128)(2,1)S(1)} %get-tuple-element.46.refs_2_), channel_id=1, source_target_pairs={{0,2},{1,3},{2,4},{3,5},{4,6},{5,7},{6,8},{7,9},{8,10},{9,11},{10,... | collective-permute-start | bytes 589832 | tf_op jit(solution)/shard_map/ppermute | solution.py:384
  11.7 5.2 %collective-permute-start.5 = (bf16[128,768]{1,0:T(8,128)(2,1)S(1)}, bf16[128,768]{1,0:T(8,128)(2,1)S(1)}, u32[]{:S(2)}, u32[]{:S(2)}) collective-permute-start(bf16[128,768]{1,0:T(8,128)(2,1)S(1)} %get-tuple-element.47.refs_3_), channel_id=1, source_target_pairs={{0,2},{1,3},{2,4},{3,5},{4,6},{5,7},{6,8},{7,9},{8,10},{9,11},{10,... | collective-permute-start | bytes 589832 | tf_op jit(solution)/shard_map/ppermute | solution.py:384
  16.9 0.0 copy-done
  16.9 0.0 copy-done.2
  16.9 0.0 copy-done.3
  16.9 1.5 %shard_map.105 = (f32[128,1920]{1,0:T(8,128)S(1)}, f32[128,1920]{1,0:T(8,128)S(1)}) custom-call(bf16[128,4096]{1,0:T(8,128)(2,1)S(1)} %copy-done, bf16[8,4096]{1,0:T(8,128)(2,1)S(1)} %get-tuple-element.43.head_ref.refs_4_, f32[8,4096]{1,0:T(8,128)S(1)} %get-tuple-element.44.near_ref, f32[3,3,4096]{2,1,0:T(4,128)S(1)} %get-tuple-element.37.taps_ref, ...), custom_call_target="tpu_custom_call" | custom-call | flops 1 | bytes 1 | tf_op jit(solution)/shard_map/pallas_call | solution.py:405
  18.4 0.0 collective-permute-done.1.refs_0_.middle_ref
  18.4 0.0 collective-permute-done.2.refs_1_.refs_2_
  18.4 0.0 copy-done.1
  18.4 0.4 %shard_map.108 = bf16[128,640]{1,0:T(8,128)(2,1)S(1)} custom-call(bf16[2,14336]{1,0:T(2,128)(2,1)S(1)} %collective-permute-done.1.refs_0_.middle_ref, f32[128,1920]{1,0:T(8,128)S(1)} %get-tuple-element.51.part_ref.refs_1_, bf16[128,896]{1,0:T(8,128)(2,1)S(1)} %collective-permute-done.2.refs_1_.refs_2_, ...), custom_call_target="tpu_custom_call" | custom-call | flops 1 | bytes 1 | tf_op jit(solution)/shard_map/pallas_call | solution.py:405
  18.9 1.9 %collective-permute-start.6 = (bf16[128,640]{1,0:T(8,128)(2,1)S(1)}, bf16[128,640]{1,0:T(8,128)(2,1)S(1)}, u32[]{:S(2)}, u32[]{:S(2)}) collective-permute-start(bf16[128,640]{1,0:T(8,128)(2,1)S(1)} %shard_map.108), channel_id=1, source_target_pairs={{0,2},{1,3},{2,4},{3,5},{4,6},{5,7},{6,8},{7,9},{8,10},{9,11},{10,... | collective-permute-start | bytes 491528 | tf_op jit(solution)/shard_map/ppermute | solution.py:384
  20.8 1.7 %shard_map.104 = (f32[128,2176]{1,0:T(8,128)S(1)}, f32[128,2176]{1,0:T(8,128)S(1)}) custom-call(bf16[128,4096]{1,0:T(8,128)(2,1)S(1)} %copy-done, bf16[8,4096]{1,0:T(8,128)(2,1)S(1)} %get-tuple-element.43.head_ref.refs_4_, f32[8,4096]{1,0:T(8,128)S(1)} %get-tuple-element.44.near_ref, f32[3,3,4096]{2,1,0:T(4,128)S(1)} %get-tuple-element.37.taps_ref, ...), custom_call_target="tpu_custom_call" | custom-call | flops 1 | bytes 1 | tf_op jit(solution)/shard_map/pallas_call | solution.py:405
  22.5 0.0 collective-permute-done.3.refs_2_
  22.5 1.8 %shard_map.106 = (bf16[128,4096]{1,0:T(8,128)(2,1)}, f32[40,1920]{1,0:T(8,128)S(1)}) custom-call(bf16[2,14336]{1,0:T(2,128)(2,1)S(1)} %collective-permute-done.1.refs_0_.middle_ref, f32[8,4096]{1,0:T(8,128)S(1)} %get-tuple-element.33.far_ref.refs_5_, f32[128,1920]{1,0:T(8,128)S(1)} %get-tuple-element.51.part_ref.refs_1_, ...), custom_call_target="tpu_custom_call" | custom-call | flops 1 | bytes 1 | tf_op jit(solution)/shard_map/pallas_call | solution.py:405
  24.3 0.0 collective-permute-done.4.refs_2_
  24.3 0.5 %collective-permute-done.5.refs_3_ = bf16[128,768]{1,0:T(8,128)(2,1)S(1)} collective-permute-done((bf16[128,768]{1,0:T(8,128)(2,1)S(1)}, bf16[128,768]{1,0:T(8,128)(2,1)S(1)}, u32[]{:S(2)}, u32[]{:S(2)}) %collective-permute-start.5) | collective-permute-done | bytes 196640 | tf_op jit(solution)/shard_map/ppermute | solution.py:384
  24.8 1.5 %shard_map.107._ = bf16[128,4096]{1,0:T(8,128)(2,1)} custom-call(bf16[2,14336]{1,0:T(2,128)(2,1)S(1)} %collective-permute-done.1.refs_0_.middle_ref, f32[8,4096]{1,0:T(8,128)S(1)} %get-tuple-element.33.far_ref.refs_5_, f32[128,2176]{1,0:T(8,128)S(1)} %get-tuple-element.49.refs_0_.part_ref, ...), custom_call_target="tpu_custom_call", output_to_operand_aliasing={{}: (6, {})} | custom-call | flops 1 | bytes 1 | tf_op jit(solution)/shard_map/pallas_call | solution.py:405
  26.3 2.0 %collective-permute-done.6.back_ref = bf16[128,640]{1,0:T(8,128)(2,1)S(1)} collective-permute-done((bf16[128,640]{1,0:T(8,128)(2,1)S(1)}, bf16[128,640]{1,0:T(8,128)(2,1)S(1)}, u32[]{:S(2)}, u32[]{:S(2)}) %collective-permute-start.6) | collective-permute-done | bytes 163872 | tf_op jit(solution)/shard_map/ppermute | solution.py:384
  28.3 0.7 %shard_map.109 = bf16[128,4096]{1,0:T(8,128)(2,1)} custom-call(f32[8,4096]{1,0:T(8,128)S(1)} %get-tuple-element.33.far_ref.refs_5_, f32[128,2176]{1,0:T(8,128)S(1)} %get-tuple-element.49.refs_0_.part_ref, f32[128,2176]{1,0:T(8,128)S(1)} %get-tuple-element.50.gate_ref, ...), custom_call_target="tpu_custom_call", output_to_operand_aliasing={{}: (4, {})} | custom-call | flops 1 | bytes 1 | tf_op jit(solution)/shard_map/pallas_call | solution.py:405
  (2 shorter events, 0.0 us)
Async XLA Ops:
  1.3 17.1 %collective-permute-start.2 = (bf16[128,896]{1,0:T(8,128)(2,1)S(1)}, bf16[128,896]{1,0:T(8,128)(2,1)S(1)}, u32[]{:S(2)}, u32[]{:S(2)}) collective-permute-start(bf16[128,896]{1,0:T(8,128)(2,1)S(1)} %shard_map.100._.c1.refs_0_), channel_id=1, source_target_pairs={{0,2},{1,3},{2,4},{3,5},{4,6},{5,7},{6,8},{7,9},{8,10},{9,11},{10,... | collective-permute-start | bytes 688136 | tf_op jit(solution)/shard_map/ppermute | solution.py:384
  2.9 1.7 %copy-start.4 = (bf16[16,128]{1,0:T(8,128)(2,1)S(1)}, bf16[16,128]{1,0:T(8,128)(2,1)}, u32[]{:S(2)}) copy-start(bf16[16,128]{1,0:T(8,128)(2,1)} %constant.8.clone.moment_ref) | copy-start | bytes 12292
  4.5 5.0 %collective-permute-start = (bf16[2,12288]{1,0:T(2,128)(2,1)S(1)}, bf16[2,12288]{1,0:T(2,128)(2,1)S(1)}, u32[]{:S(2)}, u32[]{:S(2)}) collective-permute-start(bf16[2,12288]{1,0:T(2,128)(2,1)S(1)} %get-tuple-element.36), channel_id=1, source_target_pairs={{0,1},{1,2},{2,3},{3,4},{4,5},{5,6},{6,7},{7,8},{8,9},{9,10},{10,1... | collective-permute-start | bytes 147464 | tf_op jit(solution)/shard_map/ppermute | solution.py:384
  4.6 17.9 %collective-permute-start.3 = (bf16[128,1024]{1,0:T(8,128)(2,1)S(1)}, bf16[128,1024]{1,0:T(8,128)(2,1)S(1)}, u32[]{:S(2)}, u32[]{:S(2)}) collective-permute-start(bf16[128,1024]{1,0:T(8,128)(2,1)S(1)} %get-tuple-element.32.c2.refs_1_), channel_id=1, source_target_pairs={{0,2},{1,3},{2,4},{3,5},{4,6},{5,7},{6,8},{7,9},{8,10},{9,11},{10,... | collective-permute-start | bytes 786440 | tf_op jit(solution)/shard_map/ppermute | solution.py:384
  9.5 7.4 %copy-start = (bf16[128,4096]{1,0:T(8,128)(2,1)S(1)}, bf16[128,4096]{1,0:T(8,128)(2,1)}, u32[]{:S(2)}) copy-start(bf16[128,4096]{1,0:T(8,128)(2,1)} %query_ref.5) | copy-start | bytes 3145732
  9.5 7.4 %copy-start.2 = (bf16[128,896]{1,0:T(8,128)(2,1)S(1)}, bf16[128,896]{1,0:T(8,128)(2,1)}, u32[]{:S(2)}) copy-start(bf16[128,896]{1,0:T(8,128)(2,1)} %constant.6.clone.table_ref) | copy-start | bytes 688132
  9.5 7.4 %copy-start.3 = (f32[4096]{0:T(1024)S(1)}, f32[4096]{0:T(1024)}, u32[]{:S(2)}) copy-start(f32[4096]{0:T(1024)} %param.16) | copy-start | bytes 49156
  10.9 7.5 %copy-start.1 = (bf16[128,912]{1,0:T(8,128)(2,1)S(1)}, bf16[128,912]{1,0:T(8,128)(2,1)}, u32[]{:S(2)}) copy-start(bf16[128,912]{1,0:T(8,128)(2,1)} %constant.7.clone.refs_1_.table_ref.refs_6_) | copy-start | bytes 700420
  10.9 7.4 %collective-permute-start.1 = (bf16[2,14336]{1,0:T(2,128)(2,1)S(1)}, bf16[2,14336]{1,0:T(2,128)(2,1)S(1)}, u32[]{:S(2)}, u32[]{:S(2)}) collective-permute-start(bf16[2,14336]{1,0:T(2,128)(2,1)S(1)} %get-tuple-element.45), channel_id=1, source_target_pairs={{0,1},{1,2},{2,3},{3,4},{4,5},{5,6},{6,7},{7,8},{8,9},{9,10},{10,1... | collective-permute-start | bytes 172040 | tf_op jit(solution)/shard_map/ppermute | solution.py:384
  11.0 13.2 %collective-permute-start.4 = (bf16[128,768]{1,0:T(8,128)(2,1)S(1)}, bf16[128,768]{1,0:T(8,128)(2,1)S(1)}, u32[]{:S(2)}, u32[]{:S(2)}) collective-permute-start(bf16[128,768]{1,0:T(8,128)(2,1)S(1)} %get-tuple-element.46.refs_2_), channel_id=1, source_target_pairs={{0,2},{1,3},{2,4},{3,5},{4,6},{5,7},{6,8},{7,9},{8,10},{9,11},{10,... | collective-permute-start | bytes 589832 | tf_op jit(solution)/shard_map/ppermute | solution.py:384
  11.7 13.1 %collective-permute-start.5 = (bf16[128,768]{1,0:T(8,128)(2,1)S(1)}, bf16[128,768]{1,0:T(8,128)(2,1)S(1)}, u32[]{:S(2)}, u32[]{:S(2)}) collective-permute-start(bf16[128,768]{1,0:T(8,128)(2,1)S(1)} %get-tuple-element.47.refs_3_), channel_id=1, source_target_pairs={{0,2},{1,3},{2,4},{3,5},{4,6},{5,7},{6,8},{7,9},{8,10},{9,11},{10,... | collective-permute-start | bytes 589832 | tf_op jit(solution)/shard_map/ppermute | solution.py:384
  18.9 9.5 %collective-permute-start.6 = (bf16[128,640]{1,0:T(8,128)(2,1)S(1)}, bf16[128,640]{1,0:T(8,128)(2,1)S(1)}, u32[]{:S(2)}, u32[]{:S(2)}) collective-permute-start(bf16[128,640]{1,0:T(8,128)(2,1)S(1)} %shard_map.108), channel_id=1, source_target_pairs={{0,2},{1,3},{2,4},{3,5},{4,6},{5,7},{6,8},{7,9},{8,10},{9,11},{10,... | collective-permute-start | bytes 491528 | tf_op jit(solution)/shard_map/ppermute | solution.py:384
